TPU v7x, 32 devices: a whole 2x2x4 slice. The times are simulated.
32 devices in a mesh: space: 8 (over z, x), chan: 4 (over y, core).
Axes of the slice: x: 2, y: 2, z: 4, core: 2. Of those that a mesh axis runs over, the one named last changes fastest.
Arguments:
- features: bfloat16 [64, 64, 512], P('space', 'chan'), may hold values from -6 to 6
- weight: bfloat16 [27, 64, 64], P(None, 'chan'), may hold values from -0.15625 to 0.15625
- cotangent: bfloat16 [64, 64, 512], P('space', 'chan'), may hold values from -6 to 6
- neighbours: int32 [64, 27], P('space'), may hold values from -1 to 63, as said below
Outputs:
- output: bfloat16 [64, 64, 512], P('space', 'chan')
- grad_input: bfloat16 [64, 64, 512], P('space', 'chan')
- grad_weight: float32 [27, 64, 64], P(None, 'chan')
Inputs may be any that keep to these rules, and one draw needn't show every extreme that they name: `neighbours`: row r lists, for the displacement (i, j, k) in the finite set (-1, 0, 1)^3 at entry 9 (i + 1) + 3 (j + 1) + (k + 1), the slot of the brick at that displacement in bricks, or -1 where the scene has none. Slot s belongs to device s // 8 of space, and a neighbour at first displacement i belongs to the device of index one's own + i. The relation is symmetric: if row r names s at entry m, row s names r at entry 26 - m. A device's occupied bricks fill its first slots, and the last device of space has all 8 slots occupied; an empty slot's row is all -1, no row names an empty slot, and an occupied brick's entry 13 is its own slot.
All inputs are finite; a program needn't handle non-finite values.
Results may differ from a plain program's by a relative error of at most 0.001.
Values may be sent and summed in bfloat16 or wider, within the bound.
No kernel may reach another device: no remote copies, remote signals or barrier semaphores. Data moves between devices by JAX's collectives and lax.ppermute only.
A program may use at most 128 MiB of HBM per device.

v0:
```python
import functools

import jax
import jax.numpy as jnp
from jax import lax
from jax.experimental import pallas as pl
from jax.experimental.pallas import tpu as pltpu
from jax.sharding import PartitionSpec as P

f32, bf16, i32 = jnp.float32, jnp.bfloat16, jnp.int32
VMEM = pl.BlockSpec(memory_space=pltpu.VMEM)
SMEM = pl.BlockSpec(memory_space=pltpu.SMEM)
PARAMS = pltpu.CompilerParams(vmem_limit_bytes=48 * 1024 * 1024)


def iota(shape, axis):
    return lax.broadcasted_iota(i32, shape, axis)


def call(kernel, out_shape, scratch, *args, specs, flops=0, moved=0):
    return pl.pallas_call(
        kernel,
        out_shape=out_shape,
        in_specs=specs,
        out_specs=jax.tree.map(lambda _: VMEM, out_shape),
        scratch_shapes=scratch,
        compiler_params=PARAMS,
        cost_estimate=pl.CostEstimate(flops=flops, bytes_accessed=moved, transcendentals=0),
    )(*args)


def prepare_kernel(place_ref, feat_ref, cot_ref, weight_ref, sent_ref, first_ref, second_ref):
    rows = feat_ref.shape[0] * feat_ref.shape[1]
    feat = feat_ref[...].reshape(rows, 512)
    cot = cot_ref[...].reshape(rows, 512)
    sent_ref[:, 0:512] = feat
    for group in range(4):
        taps = [weight_ref[8 * group + t] if 8 * group + t < 27 else jnp.zeros((16, 64), bf16) for t in range(8)]
        sent_ref[:, 512 + 64 * group : 576 + 64 * group] = jnp.concatenate(taps, axis=0)
    low = jnp.concatenate([feat[:, 0:64], cot[:, 0:64]], axis=1)
    high = jnp.concatenate([feat[:, 448:512], cot[:, 448:512]], axis=1)
    even = place_ref[0] % 2 == 0

    @pl.when(even)
    def _():
        first_ref[...] = high
        second_ref[...] = low

    @pl.when(jnp.logical_not(even))
    def _():
        first_ref[...] = low
        second_ref[...] = high


def kernel_grad_kernel(scale, place_ref, near_ref, got_ref, cot_ref, first_ref, second_ref, part_ref, sent_ref, padded, products):
    bricks = cot_ref.shape[0]
    rows = bricks * 16
    cot = cot_ref[...].reshape(rows, 512)
    even = jnp.full((rows, 128), place_ref[0] % 2, i32) == 0
    first, second = first_ref[...].astype(f32), second_ref[...].astype(f32)
    before = jnp.where(even, second, first)
    after = jnp.where(even, first, second)
    left = iota((rows, 128), 1) < 64
    sent_ref[:, 0:512] = cot
    sent_ref[:, 512:640] = jnp.where(left, before, pltpu.roll(after, 64, 1)).astype(bf16)
    sent_ref[:, 640:768] = jnp.where(left, pltpu.roll(before, 64, 1), after).astype(bf16)

    flat = jnp.transpose(cot.astype(f32)).astype(bf16)
    planes = [jnp.transpose(view)[64:128].astype(bf16) for view in (before, after)]
    near = near_ref[...]
    near = jnp.where(near < 0, bricks, near % bricks).astype(f32)
    widen = (iota((bricks, rows), 1) // 16 == iota((bricks, rows), 0)).astype(f32)
    source = lax.dot_general(near, widen, (((0,), (0,)), ((), ())), preferred_element_type=f32)
    source = source.astype(i32) * 16 + iota((27, rows), 1) % 16
    row_ids = iota((rows, rows), 0)
    edge = iota((1, 8, 128), 1)
    for i in range(3):
        for j in range(3):
            if i == 1:
                columns = flat.reshape(8, 8, 8, 128)
                if j != 1:
                    columns = columns[:, 7:8] if j == 0 else columns[:, 0:1]
            else:
                columns = planes[i // 2].reshape(1, 8, 8, 128)
                if j != 1:
                    columns = columns[:, 7:8] if j == 0 else columns[:, 0:1]
            wide, deep = columns.shape[0], columns.shape[1]
            count = wide * deep
            picks = [
                (row_ids == source[9 * i + 3 * j + k : 9 * i + 3 * j + k + 1, :]).astype(f32).astype(bf16)
                for k in range(3)
            ]
            moved = jnp.dot(columns.reshape(count * 8, 128), jnp.concatenate(picks, axis=1), preferred_element_type=f32)
            lower, own, upper = (moved[:, 128 * k : 128 * k + 128].reshape(count, 8, 128) for k in range(3))
            down = jnp.where(edge == 0, pltpu.roll(lower, 1, 1), pltpu.roll(own, 1, 1))
            up = jnp.where(edge == 7, pltpu.roll(upper, 7, 1), pltpu.roll(own, 7, 1))
            xs = (0, 1) if i == 0 else ((1, 9) if i == 1 else (9, 10))
            ys = (0, 1) if j == 0 else ((1, 9) if j == 1 else (9, 10))
            for c, value in enumerate((down, own, up)):
                padded[c, xs[0] : xs[1], ys[0] : ys[1]] = value.reshape(wide, deep, 8, 128)

    feat = got_ref[:, :, 0:512].reshape(4 * rows, 512)
    lane_group = iota((16, 128), 1) // 16
    sums = []
    for begin, end in ((0, 8), (8, 14), (14, 22), (22, 27)):
        for tap in range(begin, end, 2):
            windows = []
            for one in (tap, min(tap + 1, end - 1)):
                mirror = 26 - one
                a, b, c = mirror // 9, mirror // 3 % 3, mirror % 3
                windows.append(padded[c, a : a + 8, b : b + 8].reshape(512, 128).astype(bf16))
            both = jnp.dot(feat, jnp.concatenate(windows, axis=1), preferred_element_type=f32)
            products[tap - begin] = both[:, 0:128]
            products[tap - begin + 1] = both[:, 128:256]
        last = end - begin - 1
        blocks = []
        for quarter in range(4):
            total = None
            for shift in range(8):
                chosen = None
                for brick in range(bricks):
                    slot = min((brick + shift) % 8, last)
                    start = quarter * rows + brick * 16
                    block = products[slot, start : start + 16, :]
                    chosen = block if chosen is None else jnp.where(lane_group == brick, block, chosen)
                if shift:
                    chosen = pltpu.roll(chosen, 16 * shift, 1)
                total = chosen if total is None else total + chosen
            blocks.append(total)
        sums.append(jnp.concatenate(blocks, axis=0))
    part_ref[0:128] = jnp.transpose(jnp.concatenate([sums[0], sums[2]], axis=0)) * scale
    part_ref[128:224] = jnp.transpose(jnp.concatenate([sums[1], sums[3]], axis=0))[0:96] * scale


def pad_kernel(place_ref, near_ref, feat_ref, cot_ref, weight_ref, grid_ref, mat_ref, flat, planes, padded):
    bricks = near_ref.shape[0]
    for s in range(bricks):
        rows = slice(16 * s, 16 * s + 16)
        both = jnp.concatenate([feat_ref[q, rows, 0:512] for q in range(4)] + [cot_ref[q, rows, 0:512] for q in range(4)], axis=0)
        flat[512 * s : 512 * s + 512] = jnp.transpose(both.astype(f32))
        both = jnp.concatenate(
            [cot_ref[q, rows, 512:640] for q in range(4)] + [cot_ref[q, rows, 640:768] for q in range(4)], axis=0
        )
        planes[128 * s : 128 * s + 128] = jnp.transpose(both.astype(f32))
    flat[512 * bricks : 512 * bricks + 512] = jnp.zeros((512, 128), f32)
    planes[128 * bricks : 128 * bricks + 128] = jnp.zeros((128, 128), f32)

    for r in range(bricks):
        for i in range(3):
            for j in range(3):
                for k in range(3):
                    listed = near_ref[r, 9 * i + 3 * j + k]
                    s = jnp.where(listed < 0, bricks, listed % bricks)
                    source, base = (flat, s * 512) if i == 1 else (planes, s * 128 + (64 if i == 2 else 0))
                    x_pairs = [(x + 1, x) for x in range(8)] if i == 1 else [(0 if i == 0 else 9, 0)]
                    y_pairs = [(y + 1, y) for y in range(8)] if j == 1 else [(0, 7) if j == 0 else (9, 0)]
                    z_to, z_from = (1, 0) if k == 1 else ((0, 7) if k == 0 else (9, 0))
                    if k == 1:
                        for x_to, x_from in x_pairs:
                            for y_to, y_from in y_pairs:
                                piece = source[pl.ds(base + 64 * x_from + 8 * y_from, 8), :]
                                padded[pl.ds(80 * (10 * x_to + y_to) + 8 + r, 8, 8), :] = piece
                    elif j == 1:
                        for x_to, x_from in x_pairs:
                            piece = source[pl.ds(base + 64 * x_from + z_from, 8, 8), :]
                            padded[pl.ds(80 * (10 * x_to + 1) + 8 * z_to + r, 8, 80), :] = piece
                    elif i == 1:
                        piece = source[pl.ds(base + 8 * y_pairs[0][1] + z_from, 8, 64), :]
                        padded[pl.ds(80 * (10 + y_pairs[0][0]) + 8 * z_to + r, 8, 800), :] = piece
                    else:
                        piece = source[pl.ds(base + 8 * y_pairs[0][1] + z_from, 1), :]
                        padded[pl.ds(80 * (10 * x_pairs[0][0] + y_pairs[0][0]) + 8 * z_to + r, 1), :] = piece
    for x in range(10):
        grid_ref[800 * x : 800 * x + 800] = padded[800 * x : 800 * x + 800].astype(bf16)

    chan = place_ref[1]
    lanes = iota((48, 128), 1)
    spots = iota((48, 128), 0)
    forward = (lanes == 32 * (spots // 16) + spots % 16).astype(f32).astype(bf16)
    lanes = iota((256, 128), 1)
    spots = iota((256, 128), 0)
    picks = {}
    for group in range(4):
        for c in range(3):
            hit = (lanes - 32 * c - 16 == spots - 64 * group - 16 * chan) & (lanes >= 32 * c + 16) & (lanes < 32 * c + 32)
            picks[group, c] = hit.astype(f32).astype(bf16)
    for spot in range(9):
        own = weight_ref[3 * spot : 3 * spot + 3].reshape(48, 64)
        mat_ref[128 * spot : 128 * spot + 64] = lax.dot_general(
            own, forward, (((0,), (0,)), ((), ())), preferred_element_type=f32
        ).astype(bf16)
        total = None
        for c in range(3):
            tap = 26 - 3 * spot - c
            begin = 16 * (tap % 8)
            block = jnp.concatenate([feat_ref[q, begin : begin + 16, 512:768] for q in range(4)], axis=0)
            term = jnp.dot(block, picks[tap // 8, c], preferred_element_type=f32)
            total = term if total is None else total + term
        mat_ref[128 * spot + 64 : 128 * spot + 128] = total.astype(bf16)


def conv_kernel(grid_ref, mat_ref, out_ref, grad_ref, done):
    bricks = out_ref.shape[0]

    def layer(x, carry):
        pieces = []
        for a in range(3):
            for b in range(3):
                start = pl.multiple_of((x + a) * 800 + 80 * b, 16)
                pieces.append(grid_ref[pl.ds(start, 640), :])
        sums = jnp.dot(jnp.concatenate(pieces, axis=1), mat_ref[...], preferred_element_type=f32).reshape(8, 80, 128)
        total = sums[:, 0:64] + pltpu.roll(sums[:, 8:72], 96, 2) + pltpu.roll(sums[:, 16:80], 64, 2)
        done[pl.ds(pl.multiple_of(x * 512, 512), 512), :] = total.reshape(512, 128)
        return carry

    lax.fori_loop(0, 8, layer, 0)
    for r in range(bricks):
        turned = jnp.transpose(done[pl.ds(r, 512, 8), :])
        out_ref[r] = turned[0:16].astype(bf16)
        grad_ref[r] = turned[16:32].astype(bf16)


def finish_kernel(one_ref, other_ref, grad_ref):
    total = one_ref[...] + other_ref[...]
    for tap in range(27):
        slot = tap % 14
        block = total[16 * slot : 16 * slot + 16]
        grad_ref[tap] = block[:, 0:64] if tap < 14 else block[:, 64:128]


def body(features, weight, cotangent, neighbours):
    bricks, narrow = features.shape[0], features.shape[1]
    rows = bricks * narrow
    length = lax.axis_size("space")
    place = jnp.stack([lax.axis_index("space"), lax.axis_index("chan")]).astype(i32)
    shape = jax.ShapeDtypeStruct

    packed, first, second = call(
        prepare_kernel,
        (shape((rows, 768), bf16), shape((rows, 128), bf16), shape((rows, 128), bf16)),
        [],
        place, features, cotangent, weight,
        specs=[SMEM, VMEM, VMEM, VMEM],
    )
    ahead = [pair for i in range(0, length - 1, 2) for pair in ((i, i + 1), (i + 1, i))]
    behind = [pair for i in range(1, length - 1, 2) for pair in ((i, i + 1), (i + 1, i))]
    first = lax.ppermute(first, "space", ahead)
    second = lax.ppermute(second, "space", behind)
    got = lax.all_gather(packed, "chan", axis=0, tiled=False)

    scale = float(bricks * length * 512) ** -0.5
    part, packed = call(
        functools.partial(kernel_grad_kernel, scale),
        (shape((224, 128), f32), shape((rows, 768), bf16)),
        [pltpu.VMEM((3, 10, 10, 8, 128), f32), pltpu.VMEM((8, 4 * rows, 128), f32)],
        place, neighbours, got, cotangent, first, second,
        specs=[SMEM, VMEM, VMEM, VMEM, VMEM, VMEM],
    )
    steps = []
    step = 1
    while step < length:
        steps.append(step)
        step *= 2

    def partner(step):
        return lax.ppermute(part, "space", [(i, i ^ step) for i in range(length)])

    got_cot = lax.all_gather(packed, "chan", axis=0, tiled=False)
    for step in steps[:-1]:
        part = part + partner(step)
    grid, matrix = call(
        pad_kernel,
        (shape((8000, 128), bf16), shape((1152, 128), bf16)),
        [
            pltpu.VMEM(((bricks + 1) * 512, 128), f32),
            pltpu.VMEM(((bricks + 1) * 128, 128), f32),
            pltpu.VMEM((8000, 128), f32),
        ],
        place, neighbours, got, got_cot, weight,
        specs=[SMEM, SMEM, VMEM, VMEM, VMEM],
    )
    output, grad_input = call(
        conv_kernel,
        (shape(features.shape, bf16), shape(features.shape, bf16)),
        [pltpu.VMEM((4096, 128), f32)],
        grid, matrix,
        specs=[VMEM, VMEM],
    )
    grad_weight = call(
        finish_kernel, shape(weight.shape, f32), [], part, partner(steps[-1]), specs=[VMEM, VMEM]
    )
    return (output, grad_input, grad_weight)


def solution(mesh):
    in_specs = (
        P("space", "chan", None),
        P(None, "chan", None),
        P("space", "chan", None),
        P("space", None),
    )
    out_specs = (P("space", "chan", None), P("space", "chan", None), P(None, "chan", None))
    return jax.shard_map(body, mesh=mesh, in_specs=in_specs, out_specs=out_specs, check_vma=False)
```

profile of v0, /device:TPU:0, one launch (start us, length us, event | category | flops | bytes accessed | tf_op | source)
XLA Modules:
  0.0 55.1 jit_solution(7956485591501511430)
XLA Ops:
  0.6 0.0 copy-start.6
  0.6 0.1 pad_add_fusion.place_ref
  0.7 0.0 copy-start
  0.7 0.9 %copy-done = bf16[8,16,512]{2,1,0:T(8,128)(2,1)S(1)} copy-done((bf16[8,16,512]{2,1,0:T(8,128)(2,1)S(1)}, bf16[8,16,512]{2,1,0:T(8,128)(2,1)}, u32[]{:S(2)}) %copy-start) | copy-done | bytes 131096
  1.6 0.0 copy-start.2
  1.6 0.9 %copy-done.2 = bf16[27,16,64]{2,1,0:T(8,128)(2,1)S(1)} copy-done((bf16[27,16,64]{2,1,0:T(8,128)(2,1)S(1)}, bf16[27,16,64]{2,1,0:T(8,128)(2,1)}, u32[]{:S(2)}) %copy-start.2) | copy-done | bytes 55320
  2.5 0.0 copy-start.4
  2.5 0.9 %copy-done.4 = bf16[8,16,512]{2,1,0:T(8,128)(2,1)S(1)} copy-done((bf16[8,16,512]{2,1,0:T(8,128)(2,1)S(1)}, bf16[8,16,512]{2,1,0:T(8,128)(2,1)}, u32[]{:S(2)}) %copy-start.4) | copy-done | bytes 131096
  3.4 0.0 copy-start.3
  3.4 0.6 %shard_map.67 = (bf16[128,768]{1,0:T(8,128)(2,1)S(1)}, bf16[128,128]{1,0:T(8,128)(2,1)S(1)}, bf16[128,128]{1,0:T(8,128)(2,1)S(1)}) custom-call(s32[2]{0:T(128)S(1)} %pad_add_fusion.place_ref, bf16[8,16,512]{2,1,0:T(8,128)(2,1)S(1)} %copy-done.4, bf16[8,16,512]{2,1,0:T(8,128)(2,1)S(1)} %copy-done, bf16[27,16,64]{2,1,0:T(8,128)(2,1)S(1)} %copy-done.2), custom_call_target="tpu_custom_call" | custom-call | tf_op jit(solution)/shard_map/pallas_call | solution.py:21
  4.1 3.0 %collective-permute-start = (bf16[128,128]{1,0:T(8,128)(2,1)S(1)}, bf16[128,128]{1,0:T(8,128)(2,1)S(1)}, u32[]{:S(2)}, u32[]{:S(2)}) collective-permute-start(bf16[128,128]{1,0:T(8,128)(2,1)S(1)} %get-tuple-element.13), channel_id=1, source_target_pairs={{0,4},{4,0},{8,12},{12,8},{16,20},{20,16},{24,28},{28,24},{1,5},{5... | collective-permute-start | bytes 98312 | tf_op jit(solution)/shard_map/ppermute | solution.py:247
  7.1 0.7 %collective-permute-start.1 = (bf16[128,128]{1,0:T(8,128)(2,1)S(1)}, bf16[128,128]{1,0:T(8,128)(2,1)S(1)}, u32[]{:S(2)}, u32[]{:S(2)}) collective-permute-start(bf16[128,128]{1,0:T(8,128)(2,1)S(1)} %get-tuple-element.14), channel_id=1, source_target_pairs={{4,8},{8,4},{12,16},{16,12},{20,24},{24,20},{5,9},{9,5},{13,17},{1... | collective-permute-start | bytes 98312 | tf_op jit(solution)/shard_map/ppermute | solution.py:248
  7.8 8.6 %all-gather = bf16[512,768]{1,0:T(8,128)(2,1)S(1)} all-gather(bf16[128,768]{1,0:T(8,128)(2,1)S(1)} %get-tuple-element.12), channel_id=2, replica_groups=mesh['space'=8,'chan'=4] {'chan'}, dimensions={0}, use_global_device_ids=true | all-gather | bytes 983040 | tf_op jit(solution)/shard_map/all_gather | solution.py:249
  16.4 0.0 collective-permute-done.first_ref
  16.4 0.0 collective-permute-done.1.second_ref
  16.4 0.0 copy-start.1
  16.4 0.9 %copy-done.1 = bf16[8,16,512]{2,1,0:T(8,128)(2,1)S(1)} copy-done((bf16[8,16,512]{2,1,0:T(8,128)(2,1)S(1)}, bf16[8,16,512]{2,1,0:T(8,128)(2,1)}, u32[]{:S(2)}) %copy-start.1) | copy-done | bytes 131096
  17.3 0.0 copy-start.5
  17.3 0.7 %copy-done.5 = s32[8,27]{1,0:T(8,128)S(1)} copy-done((s32[8,27]{1,0:T(8,128)S(1)}, s32[8,27]{1,0:T(8,128)}, u32[]{:S(2)}) %copy-start.5) | copy-done | bytes 888
  18.0 3.3 %shard_map.68 = (f32[224,128]{1,0:T(8,128)S(1)}, bf16[128,768]{1,0:T(8,128)(2,1)S(1)}) custom-call(s32[2]{0:T(128)S(1)} %pad_add_fusion.place_ref, s32[8,27]{1,0:T(8,128)S(1)} %copy-done.5, bf16[4,128,768]{2,1,0:T(8,128)(2,1)S(1)} %bitcast.4, bf16[8,16,512]{2,1,0:T(8,128)(2,1)S(1)} %copy-done.1, bf16[128,128]{1,0:T(8,128)(2,1)S(1)} %collective-permute-done.first_ref, ...), custom_call_target="tpu_custom_call" | custom-call | tf_op jit(solution)/shard_map/pallas_call | solution.py:21
  21.3 4.4 %collective-permute-start.2 = (f32[224,128]{1,0:T(8,128)S(1)}, f32[224,128]{1,0:T(8,128)S(1)}, u32[]{:S(2)}, u32[]{:S(2)}) collective-permute-start(f32[224,128]{1,0:T(8,128)S(1)} %get-tuple-element.20), channel_id=1, source_target_pairs={{0,4},{4,0},{8,12},{12,8},{16,20},{20,16},{24,28},{28,24},{1,5},{5... | collective-permute-start | bytes 344072 | tf_op jit(solution)/shard_map/ppermute | solution.py:266
  25.6 3.7 %collective-permute-done.2 = f32[224,128]{1,0:T(8,128)S(1)} collective-permute-done((f32[224,128]{1,0:T(8,128)S(1)}, f32[224,128]{1,0:T(8,128)S(1)}, u32[]{:S(2)}, u32[]{:S(2)}) %collective-permute-start.2) | collective-permute-done | bytes 114720 | tf_op jit(solution)/shard_map/ppermute | solution.py:266
  29.3 1.6 %collective-permute-start.3 = (f32[224,128]{1,0:T(8,128)S(1)}, f32[224,128]{1,0:T(8,128)S(1)}, u32[]{:S(2)}, u32[]{:S(2)}) collective-permute-start(f32[224,128]{1,0:T(8,128)S(1)} %add.6), channel_id=1, source_target_pairs={{0,8},{4,12},{8,0},{12,4},{16,24},{20,28},{24,16},{28,20},{1,9},{5... | collective-permute-start | bytes 344072 | tf_op jit(solution)/shard_map/ppermute | solution.py:266
  30.9 3.2 %collective-permute-done.3 = f32[224,128]{1,0:T(8,128)S(1)} collective-permute-done((f32[224,128]{1,0:T(8,128)S(1)}, f32[224,128]{1,0:T(8,128)S(1)}, u32[]{:S(2)}, u32[]{:S(2)}) %collective-permute-start.3) | collective-permute-done | bytes 114720 | tf_op jit(solution)/shard_map/ppermute | solution.py:266
  34.2 2.7 %collective-permute-start.4 = (f32[224,128]{1,0:T(8,128)S(1)}, f32[224,128]{1,0:T(8,128)S(1)}, u32[]{:S(2)}, u32[]{:S(2)}) collective-permute-start(f32[224,128]{1,0:T(8,128)S(1)} %add.7.one_ref), channel_id=1, source_target_pairs={{0,16},{4,20},{8,24},{12,28},{16,0},{20,4},{24,8},{28,12},{1,17},{... | collective-permute-start | bytes 344072 | tf_op jit(solution)/shard_map/ppermute | solution.py:266
  36.9 7.6 %all-gather.1 = bf16[512,768]{1,0:T(8,128)(2,1)S(1)} all-gather(bf16[128,768]{1,0:T(8,128)(2,1)S(1)} %get-tuple-element.15), channel_id=3, replica_groups=mesh['space'=8,'chan'=4] {'chan'}, dimensions={0}, use_global_device_ids=true | all-gather | bytes 983040 | tf_op jit(solution)/shard_map/all_gather | solution.py:268
  44.5 0.0 copy-done.6
  44.5 0.0 copy-done.3
  44.5 3.2 %shard_map.69 = (bf16[8000,128]{1,0:T(8,128)(2,1)S(1)}, bf16[1152,128]{1,0:T(8,128)(2,1)S(1)}) custom-call(s32[2]{0:T(128)S(1)} %pad_add_fusion.place_ref, s32[8,27]{1,0:T(8,128)S(1)} %copy-done.6, bf16[4,128,768]{2,1,0:T(8,128)(2,1)S(1)} %bitcast.5, bf16[4,128,768]{2,1,0:T(8,128)(2,1)S(1)} %bitcast.6, bf16[27,16,64]{2,1,0:T(8,128)(2,1)S(1)} %copy-done.3), custom_call_target="tpu_custom_call" | custom-call | tf_op jit(solution)/shard_map/pallas_call | solution.py:21
  47.7 6.6 %shard_map.70 = (bf16[8,16,512]{2,1,0:T(8,128)(2,1)}, bf16[8,16,512]{2,1,0:T(8,128)(2,1)}) custom-call(bf16[8000,128]{1,0:T(8,128)(2,1)S(1)} %get-tuple-element.16.grid_ref, bf16[1152,128]{1,0:T(8,128)(2,1)S(1)} %get-tuple-element.17.mat_ref), custom_call_target="tpu_custom_call" | custom-call | tf_op jit(solution)/shard_map/pallas_call | solution.py:21
  54.3 0.0 collective-permute-done.4.other_ref
  54.3 0.8 %shard_map.71 = f32[27,16,64]{2,1,0:T(8,128)} custom-call(f32[224,128]{1,0:T(8,128)S(1)} %add.7.one_ref, f32[224,128]{1,0:T(8,128)S(1)} %collective-permute-done.4.other_ref), custom_call_target="tpu_custom_call" | custom-call | tf_op jit(solution)/shard_map/pallas_call | solution.py:21
  (2 shorter events, 0.0 us)
Async XLA Ops:
  0.6 43.9 %copy-start.6 = (s32[8,27]{1,0:T(8,128)S(1)}, s32[8,27]{1,0:T(8,128)}, u32[]{:S(2)}) copy-start(s32[8,27]{1,0:T(8,128)} %near_ref.3) | copy-start | bytes 2596
  0.7 0.9 %copy-start = (bf16[8,16,512]{2,1,0:T(8,128)(2,1)S(1)}, bf16[8,16,512]{2,1,0:T(8,128)(2,1)}, u32[]{:S(2)}) copy-start(bf16[8,16,512]{2,1,0:T(8,128)(2,1)} %cot_ref.3) | copy-start | bytes 393220
  1.6 0.9 %copy-start.2 = (bf16[27,16,64]{2,1,0:T(8,128)(2,1)S(1)}, bf16[27,16,64]{2,1,0:T(8,128)(2,1)}, u32[]{:S(2)}) copy-start(bf16[27,16,64]{2,1,0:T(8,128)(2,1)} %weight_ref.3) | copy-start | bytes 165892
  2.5 0.9 %copy-start.4 = (bf16[8,16,512]{2,1,0:T(8,128)(2,1)S(1)}, bf16[8,16,512]{2,1,0:T(8,128)(2,1)}, u32[]{:S(2)}) copy-start(bf16[8,16,512]{2,1,0:T(8,128)(2,1)} %feat_ref.1) | copy-start | bytes 393220
  3.4 41.1 %copy-start.3 = (bf16[27,16,64]{2,1,0:T(8,128)(2,1)S(1)}, bf16[27,16,64]{2,1,0:T(8,128)(2,1)}, u32[]{:S(2)}) copy-start(bf16[27,16,64]{2,1,0:T(8,128)(2,1)} %weight_ref.3) | copy-start | bytes 165892
  4.1 12.3 %collective-permute-start = (bf16[128,128]{1,0:T(8,128)(2,1)S(1)}, bf16[128,128]{1,0:T(8,128)(2,1)S(1)}, u32[]{:S(2)}, u32[]{:S(2)}) collective-permute-start(bf16[128,128]{1,0:T(8,128)(2,1)S(1)} %get-tuple-element.13), channel_id=1, source_target_pairs={{0,4},{4,0},{8,12},{12,8},{16,20},{20,16},{24,28},{28,24},{1,5},{5... | collective-permute-start | bytes 98312 | tf_op jit(solution)/shard_map/ppermute | solution.py:247
  7.1 9.3 %collective-permute-start.1 = (bf16[128,128]{1,0:T(8,128)(2,1)S(1)}, bf16[128,128]{1,0:T(8,128)(2,1)S(1)}, u32[]{:S(2)}, u32[]{:S(2)}) collective-permute-start(bf16[128,128]{1,0:T(8,128)(2,1)S(1)} %get-tuple-element.14), channel_id=1, source_target_pairs={{4,8},{8,4},{12,16},{16,12},{20,24},{24,20},{5,9},{9,5},{13,17},{1... | collective-permute-start | bytes 98312 | tf_op jit(solution)/shard_map/ppermute | solution.py:248
  16.4 0.9 %copy-start.1 = (bf16[8,16,512]{2,1,0:T(8,128)(2,1)S(1)}, bf16[8,16,512]{2,1,0:T(8,128)(2,1)}, u32[]{:S(2)}) copy-start(bf16[8,16,512]{2,1,0:T(8,128)(2,1)} %cot_ref.3) | copy-start | bytes 393220
  17.3 0.7 %copy-start.5 = (s32[8,27]{1,0:T(8,128)S(1)}, s32[8,27]{1,0:T(8,128)}, u32[]{:S(2)}) copy-start(s32[8,27]{1,0:T(8,128)} %near_ref.3) | copy-start | bytes 2596
  21.3 8.0 %collective-permute-start.2 = (f32[224,128]{1,0:T(8,128)S(1)}, f32[224,128]{1,0:T(8,128)S(1)}, u32[]{:S(2)}, u32[]{:S(2)}) collective-permute-start(f32[224,128]{1,0:T(8,128)S(1)} %get-tuple-element.20), channel_id=1, source_target_pairs={{0,4},{4,0},{8,12},{12,8},{16,20},{20,16},{24,28},{28,24},{1,5},{5... | collective-permute-start | bytes 344072 | tf_op jit(solution)/shard_map/ppermute | solution.py:266
  29.3 4.9 %collective-permute-start.3 = (f32[224,128]{1,0:T(8,128)S(1)}, f32[224,128]{1,0:T(8,128)S(1)}, u32[]{:S(2)}, u32[]{:S(2)}) collective-permute-start(f32[224,128]{1,0:T(8,128)S(1)} %add.6), channel_id=1, source_target_pairs={{0,8},{4,12},{8,0},{12,4},{16,24},{20,28},{24,16},{28,20},{1,9},{5... | collective-permute-start | bytes 344072 | tf_op jit(solution)/shard_map/ppermute | solution.py:266
  34.2 20.1 %collective-permute-start.4 = (f32[224,128]{1,0:T(8,128)S(1)}, f32[224,128]{1,0:T(8,128)S(1)}, u32[]{:S(2)}, u32[]{:S(2)}) collective-permute-start(f32[224,128]{1,0:T(8,128)S(1)} %add.7.one_ref), channel_id=1, source_target_pairs={{0,16},{4,20},{8,24},{12,28},{16,0},{20,4},{24,8},{28,12},{1,17},{... | collective-permute-start | bytes 344072 | tf_op jit(solution)/shard_map/ppermute | solution.py:266
where the time goes:
time: 55.3 us; the launch traced here: 55.1 us
  blocking collectives  16.3 us (29%)
  Pallas kernels  14.5 us (26%)
  starting transfers between devices  12.3 us (22%)
  waiting for transfers between devices  6.92 us (13%)
  local copies, waits for them, and re-layouts  4.31 us (8%)
  between operations  0.69 us (1%)
    pallas_call x5, Pallas kernels, call(): pl.pallas_call(kernel, out_shape=out_shape, in_specs=specs, out_specs=jax...  14.5 us
    ppermute x3, starting transfers between devices, partner(): return lax.ppermute(part, 'space', [(i, i ^ step) for i in range(length)])  8.64 us
    all_gather x1, blocking collectives, body(): got = lax.all_gather(packed, 'chan', axis=0, tiled=False)  8.63 us
    all_gather x1, blocking collectives, body(): got_cot = lax.all_gather(packed, 'chan', axis=0, tiled=False)  7.63 us
    ppermute x3, waiting for transfers between devices, partner(): return lax.ppermute(part, 'space', [(i, i ^ step) for i in range(length)])  6.91 us
    unnamed x14, local copies, waits for them, and re-layouts  4.31 us
    ppermute x1, starting transfers between devices, body(): first = lax.ppermute(first, 'space', ahead)  3.01 us
  transfers between devices with their start and end apart: 5, of which 2 were waited for; matrix products, arithmetic and copies ran while one was open for 0% of the time, Pallas kernels for 18%

commit v1 on v0

v1 whole, which is shorter than its diff:
```python
import functools

import jax
import jax.numpy as jnp
from jax import lax
from jax.experimental import pallas as pl
from jax.experimental.pallas import tpu as pltpu
from jax.sharding import PartitionSpec as P

f32, bf16, i32 = jnp.float32, jnp.bfloat16, jnp.int32
VMEM = pl.BlockSpec(memory_space=pltpu.VMEM)
HBM = pl.BlockSpec(memory_space=pltpu.HBM)
SMEM = pl.BlockSpec(memory_space=pltpu.SMEM)

GROUPS = ((0, 8), (8, 14), (14, 22), (22, 27))


def iota(shape, axis):
    return lax.broadcasted_iota(i32, shape, axis)


def call(kernel, out_shape, scratch, *args, specs, limit=48 << 20):
    return pl.pallas_call(
        kernel,
        out_shape=out_shape,
        in_specs=specs,
        out_specs=jax.tree.map(lambda _: VMEM, out_shape),
        scratch_shapes=scratch,
        compiler_params=pltpu.CompilerParams(vmem_limit_bytes=limit),
    )(*args)


def prepare_kernel(feat_any, cot_any, weight_any, near_any, feat_ref, cot_ref, weight_ref, near_ref, first_ref, second_ref, sems):
    rows = first_ref.shape[0]
    pairs = ((feat_any, feat_ref), (cot_any, cot_ref), (weight_any, weight_ref), (near_any, near_ref))
    copies = [pltpu.make_async_copy(source, target, sems.at[i]) for i, (source, target) in enumerate(pairs)]
    for copy in copies:
        copy.start()
    for copy in copies[:2]:
        copy.wait()
    low = jnp.concatenate([view[:, :, 0:64].reshape(rows, 64) for view in (feat_ref, cot_ref)], axis=1)
    high = jnp.concatenate([view[:, :, 448:512].reshape(rows, 64) for view in (feat_ref, cot_ref)], axis=1)
    even = lax.axis_index("space") % 2 == 0

    @pl.when(even)
    def _():
        first_ref[...] = high
        second_ref[...] = low

    @pl.when(jnp.logical_not(even))
    def _():
        first_ref[...] = low
        second_ref[...] = high

    for copy in copies[2:]:
        copy.wait()


def pack_kernel(cot_ref, weight_ref, first_ref, second_ref, sent_ref):
    rows = first_ref.shape[0]
    even = jnp.full((rows, 128), lax.axis_index("space") % 2, i32) == 0
    first, second = first_ref[...].astype(f32), second_ref[...].astype(f32)
    before = jnp.where(even, second, first)
    after = jnp.where(even, first, second)
    left = iota((rows, 128), 1) < 64
    sent_ref[:, 0:512] = cot_ref[...].reshape(rows, 512)
    sent_ref[:, 512:640] = jnp.where(left, before, pltpu.roll(after, 64, 1)).astype(bf16)
    sent_ref[:, 640:768] = jnp.where(left, pltpu.roll(before, 64, 1), after).astype(bf16)
    for group in range(4):
        taps = [weight_ref[8 * group + t] if 8 * group + t < 27 else jnp.zeros((16, 64), bf16) for t in range(8)]
        sent_ref[:, 768 + 64 * group : 832 + 64 * group] = jnp.concatenate(taps, axis=0)


def tap_sums(views, windows, bricks, products):
    rows = bricks * 16
    feat = jnp.concatenate([view[...].reshape(rows, 512) for view in views], axis=0)
    lane_group = iota((16, 128), 1) // 16
    sums = []
    pair = 0
    for begin, end in GROUPS:
        for tap in range(begin, end, 2):
            both = jnp.dot(feat, windows(pair, tap, min(tap + 1, end - 1)), preferred_element_type=f32)
            products[tap - begin] = both[:, 0:128]
            products[tap - begin + 1] = both[:, 128:256]
            pair += 1
        last = end - begin - 1
        blocks = []
        for index in range(len(views)):
            total = None
            for shift in range(8):
                chosen = None
                for brick in range(bricks):
                    start = index * rows + brick * 16
                    block = products[min((brick + shift) % 8, last), start : start + 16, :]
                    chosen = block if chosen is None else jnp.where(lane_group == brick, block, chosen)
                if shift:
                    chosen = pltpu.roll(chosen, 16 * shift, 1)
                total = chosen if total is None else total + chosen
            blocks.append(total)
        sums.append(blocks)
    return sums


def near_grad_kernel(near_ref, packed_ref, feat_ref, feat1_ref, windows_ref, sums_ref, padded, products):
    rows = packed_ref.shape[0]
    flat = jnp.transpose(packed_ref[:, 0:512].astype(f32)).astype(bf16)
    planes = jnp.transpose(packed_ref[:, 640:768].astype(f32)).astype(bf16)
    bricks = near_ref.shape[0]
    listed = near_ref[...]
    listed = jnp.where(listed < 0, bricks, listed % bricks).astype(f32)
    widen = (iota((bricks, rows), 1) // 16 == iota((bricks, rows), 0)).astype(f32)
    source = lax.dot_general(listed, widen, (((0,), (0,)), ((), ())), preferred_element_type=f32)
    source = source.astype(i32) * 16 + iota((27, rows), 1) % 16
    row_ids = iota((rows, rows), 0)
    edge = iota((1, 8, 128), 1)
    for i in range(3):
        for j in range(3):
            columns = flat.reshape(8, 8, 8, 128) if i == 1 else planes[32 * i : 32 * i + 64].reshape(1, 8, 8, 128)
            if j != 1:
                columns = columns[:, 7:8] if j == 0 else columns[:, 0:1]
            wide, deep = columns.shape[0], columns.shape[1]
            count = wide * deep
            picks = [
                (row_ids == source[9 * i + 3 * j + k : 9 * i + 3 * j + k + 1, :]).astype(f32).astype(bf16)
                for k in range(3)
            ]
            moved = jnp.dot(columns.reshape(count * 8, 128), jnp.concatenate(picks, axis=1), preferred_element_type=f32)
            lower, own, upper = (moved[:, 128 * k : 128 * k + 128].reshape(count, 8, 128) for k in range(3))
            down = jnp.where(edge == 0, pltpu.roll(lower, 1, 1), pltpu.roll(own, 1, 1))
            up = jnp.where(edge == 7, pltpu.roll(upper, 7, 1), pltpu.roll(own, 7, 1))
            xs = (0, 1) if i == 0 else ((1, 9) if i == 1 else (9, 10))
            ys = (0, 1) if j == 0 else ((1, 9) if j == 1 else (9, 10))
            for c, value in enumerate((down, own, up)):
                padded[c, xs[0] : xs[1], ys[0] : ys[1]] = value.reshape(wide, deep, 8, 128)

    def windows(pair, *taps):
        views = []
        for tap in taps:
            a, b, c = (26 - tap) // 9, (26 - tap) // 3 % 3, (26 - tap) % 3
            views.append(padded[c, a : a + 8, b : b + 8].reshape(512, 128).astype(bf16))
        both = jnp.concatenate(views, axis=1)
        windows_ref[pair] = both
        return both

    sums = tap_sums((feat_ref, feat1_ref), windows, feat_ref.shape[0], products)
    for group in range(4):
        sums_ref[group] = jnp.concatenate(sums[group], axis=0)


def far_grad_kernel(scale, windows_ref, feat2_ref, feat3_ref, sums_ref, part_ref, products, ordered):
    chan = lax.axis_index("chan")
    sums = tap_sums((feat2_ref, feat3_ref), lambda pair, *taps: windows_ref[pair], feat2_ref.shape[0], products)
    for group in range(4):
        both = sums_ref[group]
        for apart, block in enumerate((both[0:16], both[16:32], *sums[group])):
            ordered[group, pl.ds(pl.multiple_of(16 * (chan ^ apart), 16), 16), :] = block
    part_ref[0:128] = jnp.transpose(jnp.concatenate([ordered[0], ordered[2]], axis=0)) * scale
    part_ref[128:224] = jnp.transpose(jnp.concatenate([ordered[1], ordered[3]], axis=0))[0:96] * scale


def pad_kernel(near_ref, weight_ref, *refs):
    feats, cots, (grid_ref, mat_ref, flat, planes, padded) = refs[:4], refs[4:8], refs[8:]
    bricks = near_ref.shape[0]
    for s in range(bricks):
        rows = slice(16 * s, 16 * s + 16)
        both = jnp.concatenate([feat[s] for feat in feats] + [cot[rows, 0:512] for cot in cots], axis=0)
        flat[512 * s : 512 * s + 512] = jnp.transpose(both.astype(f32))
        both = jnp.concatenate([cot[rows, 512:640] for cot in cots] + [cot[rows, 640:768] for cot in cots], axis=0)
        planes[128 * s : 128 * s + 128] = jnp.transpose(both.astype(f32))
    flat[512 * bricks : 512 * bricks + 512] = jnp.zeros((512, 128), f32)
    planes[128 * bricks : 128 * bricks + 128] = jnp.zeros((128, 128), f32)

    for r in range(bricks):
        for i in range(3):
            for j in range(3):
                for k in range(3):
                    listed = near_ref[r, 9 * i + 3 * j + k]
                    s = jnp.where(listed < 0, bricks, listed % bricks)
                    source, base = (flat, s * 512) if i == 1 else (planes, s * 128 + (64 if i == 2 else 0))
                    x_pairs = [(x + 1, x) for x in range(8)] if i == 1 else [(0 if i == 0 else 9, 0)]
                    y_pairs = [(y + 1, y) for y in range(8)] if j == 1 else [(0, 7) if j == 0 else (9, 0)]
                    z_to, z_from = (1, 0) if k == 1 else ((0, 7) if k == 0 else (9, 0))
                    if k == 1:
                        for x_to, x_from in x_pairs:
                            for y_to, y_from in y_pairs:
                                piece = source[pl.ds(base + 64 * x_from + 8 * y_from, 8), :]
                                padded[pl.ds(80 * (10 * x_to + y_to) + 8 + r, 8, 8), :] = piece
                    elif j == 1:
                        for x_to, x_from in x_pairs:
                            piece = source[pl.ds(base + 64 * x_from + z_from, 8, 8), :]
                            padded[pl.ds(80 * (10 * x_to + 1) + 8 * z_to + r, 8, 80), :] = piece
                    elif i == 1:
                        piece = source[pl.ds(base + 8 * y_pairs[0][1] + z_from, 8, 64), :]
                        padded[pl.ds(80 * (10 + y_pairs[0][0]) + 8 * z_to + r, 8, 800), :] = piece
                    else:
                        piece = source[pl.ds(base + 8 * y_pairs[0][1] + z_from, 1), :]
                        padded[pl.ds(80 * (10 * x_pairs[0][0] + y_pairs[0][0]) + 8 * z_to + r, 1), :] = piece
    for x in range(10):
        grid_ref[800 * x : 800 * x + 800] = padded[800 * x : 800 * x + 800].astype(bf16)

    chan = lax.axis_index("chan")
    lanes = iota((48, 128), 1)
    spots = iota((48, 128), 0)
    forward = (lanes == 32 * (spots // 16) + spots % 16).astype(f32).astype(bf16)
    lanes = iota((256, 128), 1)
    spots = iota((256, 128), 0)
    picks = {}
    for group in range(4):
        for c in range(3):
            hit = (lanes - 32 * c - 16 == spots - 64 * group - 16 * chan) & (lanes >= 32 * c + 16) & (lanes < 32 * c + 32)
            picks[group, c] = hit.astype(f32).astype(bf16)
    for spot in range(9):
        own = weight_ref[3 * spot : 3 * spot + 3].reshape(48, 64)
        turned = lax.dot_general(own, forward, (((0,), (0,)), ((), ())), preferred_element_type=f32).astype(bf16)
        for q in range(4):
            mat_ref[pl.ds(pl.multiple_of(128 * spot + 16 * (chan ^ q), 16), 16), :] = turned[16 * q : 16 * q + 16]
        total = None
        for c in range(3):
            tap = 26 - 3 * spot - c
            begin = 16 * (tap % 8)
            block = jnp.concatenate([cot[begin : begin + 16, 768:1024] for cot in cots], axis=0)
            term = jnp.dot(block, picks[tap // 8, c], preferred_element_type=f32)
            total = term if total is None else total + term
        mat_ref[128 * spot + 64 : 128 * spot + 128] = total.astype(bf16)


def conv_layers(grid_ref, mat_ref, done, first, last):
    def layer(x, carry):
        pieces = []
        for a in range(3):
            for b in range(3):
                start = pl.multiple_of((x + a) * 800 + 80 * b, 16)
                pieces.append(grid_ref[pl.ds(start, 640), :])
        sums = jnp.dot(jnp.concatenate(pieces, axis=1), mat_ref[...], preferred_element_type=f32).reshape(8, 80, 128)
        total = sums[:, 0:64] + pltpu.roll(sums[:, 8:72], 96, 2) + pltpu.roll(sums[:, 16:80], 64, 2)
        done[pl.ds(pl.multiple_of((x - first) * 512, 512), 512), :] = total.reshape(512, 128)
        return carry

    lax.fori_loop(first, last, layer, 0)


def low_kernel(grid_ref, mat_ref, done_ref):
    conv_layers(grid_ref, mat_ref, done_ref, 0, 4)


def high_kernel(grid_ref, mat_ref, low_ref, out_ref, grad_ref, done):
    conv_layers(grid_ref, mat_ref, done, 4, 8)
    for r in range(out_ref.shape[0]):
        turned = jnp.transpose(jnp.concatenate([view[pl.ds(r, 256, 8), :] for view in (low_ref, done)], axis=0))
        out_ref[r] = turned[0:16].astype(bf16)
        grad_ref[r] = turned[16:32].astype(bf16)


def finish_kernel(one_ref, other_ref, grad_ref):
    total = one_ref[...] + other_ref[...]
    for tap in range(27):
        slot = tap % 14
        block = total[16 * slot : 16 * slot + 16]
        grad_ref[tap] = block[:, 0:64] if tap < 14 else block[:, 64:128]


def body(features, weight, cotangent, neighbours):
    bricks, narrow = features.shape[0], features.shape[1]
    rows = bricks * narrow
    length = lax.axis_size("space")
    shape = jax.ShapeDtypeStruct

    def across(value, apart, axis="chan"):
        return lax.ppermute(value, axis, [(i, i ^ apart) for i in range(lax.axis_size(axis))])

    feat2 = across(features, 2)
    feat1 = across(features, 1)
    inputs = (features, cotangent, weight, neighbours)
    feat, cot, kernel_rows, near, first, second = call(
        prepare_kernel,
        tuple(shape(view.shape, view.dtype) for view in inputs) + (shape((rows, 128), bf16), shape((rows, 128), bf16)),
        [pltpu.SemaphoreType.DMA((4,))],
        *(pltpu.with_memory_space_constraint(view, pltpu.HBM) for view in inputs),
        specs=[HBM] * 4,
    )
    ahead = [pair for i in range(0, length - 1, 2) for pair in ((i, i + 1), (i + 1, i))]
    behind = [pair for i in range(1, length - 1, 2) for pair in ((i, i + 1), (i + 1, i))]
    first = lax.ppermute(first, "space", ahead)
    second = lax.ppermute(second, "space", behind)
    first, second, feat2 = lax.optimization_barrier((first, second, feat2))
    packed = call(
        pack_kernel, shape((rows, 1024), bf16), [], cot, kernel_rows, first, second, specs=[VMEM] * 4
    )
    packed2 = across(packed, 2)
    packed1 = across(packed, 1)
    feat3 = across(feat2, 1)
    windows, sums = call(
        near_grad_kernel,
        (shape((14, 512, 256), bf16), shape((4, 32, 128), f32)),
        [pltpu.VMEM((3, 10, 10, 8, 128), f32), pltpu.VMEM((8, 2 * rows, 128), f32)],
        near, packed, feat, feat1,
        specs=[VMEM] * 4,
    )
    part = call(
        functools.partial(far_grad_kernel, float(bricks * length * 512) ** -0.5),
        shape((224, 128), f32),
        [pltpu.VMEM((8, 2 * rows, 128), f32), pltpu.VMEM((4, 64, 128), f32)],
        windows, feat2, feat3, sums,
        specs=[VMEM] * 4,
    )
    packed2, part = lax.optimization_barrier((packed2, part))
    packed3 = across(packed2, 1)
    steps = []
    step = 1
    while step < length:
        steps.append(step)
        step *= 2
    grid, matrix = call(
        pad_kernel,
        (shape((8000, 128), bf16), shape((1152, 128), bf16)),
        [
            pltpu.VMEM(((bricks + 1) * 512, 128), f32),
            pltpu.VMEM(((bricks + 1) * 128, 128), f32),
            pltpu.VMEM((8000, 128), f32),
        ],
        near, kernel_rows, feat, feat1, feat2, feat3, packed, packed1, packed2, packed3,
        specs=[SMEM] + [VMEM] * 9,
    )
    other = across(part, steps[0], "space")
    for step in steps[1:-1]:
        other, grid, matrix = lax.optimization_barrier((other, grid, matrix))
        part = part + other
        other = across(part, step, "space")
    low = call(low_kernel, shape((2048, 128), f32), [], grid, matrix, specs=[VMEM, VMEM])
    other, low = lax.optimization_barrier((other, low))
    part = part + other
    other = across(part, steps[-1], "space")
    output, grad_input = call(
        high_kernel,
        (shape(features.shape, bf16), shape(features.shape, bf16)),
        [pltpu.VMEM((2048, 128), f32)],
        grid, matrix, low,
        specs=[VMEM, VMEM, VMEM],
    )
    other, output, grad_input = lax.optimization_barrier((other, output, grad_input))
    grad_weight = call(finish_kernel, shape(weight.shape, f32), [], part, other, specs=[VMEM, VMEM])
    return (output, grad_input, grad_weight)


def solution(mesh):
    in_specs = (
        P("space", "chan", None),
        P(None, "chan", None),
        P("space", "chan", None),
        P("space", None),
    )
    out_specs = (P("space", "chan", None), P("space", "chan", None), P(None, "chan", None))
    return jax.shard_map(body, mesh=mesh, in_specs=in_specs, out_specs=out_specs, check_vma=False)
```

time: 55.3 us -> 38.4 us (0.69)
  blocking collectives: 16.3 us -> 0 us
  local copies, waits for them, and re-layouts: 4.31 us -> 0 us
  starting transfers between devices: 12.3 us -> 16.1 us
    all_gather x2 -> x0, blocking collectives: 16.3 us -> none  [the longest x1 8.63 us: body(): got = lax.all_gather(packed, 'chan', axis=0, tiled=False)]
    ppermute x3 -> x9, starting transfers between devices: 8.64 us -> 13.9 us  [across(): lax.ppermute(value, axis, [(i, i ^ apart) for i in range(lax.axis_size(ax...]
    unnamed x14 -> x0, local copies, waits for them, and re-layouts: 4.31 us -> none
    ppermute x3 -> x9, waiting for transfers between devices: 6.91 us -> 4.76 us  [across(): lax.ppermute(value, axis, [(i, i ^ apart) for i in range(lax.axis_size(ax...]
    ppermute x1, waiting for transfers between devices: 0.01 us -> 1.76 us  [body(): first = lax.ppermute(first, 'space', ahead)]
    ppermute x1, starting transfers between devices: 3.01 us -> 1.56 us  [body(): first = lax.ppermute(first, 'space', ahead)]
    pallas_call x5 -> x8, Pallas kernels: 14.5 us -> 14.9 us  [call(): pl.pallas_call(kernel, out_shape=out_shape, in_specs=specs, out_specs=jax...]
  transfers between devices with their start and end apart: 5 -> 11, of which waited for: 2 -> 6; matrix products, arithmetic and copies ran while one was open for 0% -> 0% of each run, Pallas kernels for 18% -> 37%
where the time goes in v1:
time: 38.4 us; the launch traced here: 38.3 us
  starting transfers between devices  16.1 us (42%)
  Pallas kernels  14.9 us (39%)
  waiting for transfers between devices  6.52 us (17%)
  between operations  0.7 us (2%)
    pallas_call x8, Pallas kernels, call(): pl.pallas_call(kernel, out_shape=out_shape, in_specs=specs, out_specs=jax...  14.9 us
    ppermute x9, starting transfers between devices, across(): lax.ppermute(value, axis, [(i, i ^ apart) for i in range(lax.axis_size(ax...  13.9 us
    ppermute x9, waiting for transfers between devices, across(): lax.ppermute(value, axis, [(i, i ^ apart) for i in range(lax.axis_size(ax...  4.76 us
    ppermute x1, waiting for transfers between devices, body(): first = lax.ppermute(first, 'space', ahead)  1.76 us
    ppermute x1, starting transfers between devices, body(): first = lax.ppermute(first, 'space', ahead)  1.56 us
  transfers between devices with their start and end apart: 11, of which 6 were waited for; matrix products, arithmetic and copies ran while one was open for 0% of the time, Pallas kernels for 37%

profile of v1, /device:TPU:0, one launch (start us, length us, event | category | flops | bytes accessed | tf_op | source)
XLA Modules:
  0.0 38.3 jit_solution(16052174706580678358)
XLA Ops:
  0.6 3.0 %collective-permute-start.2 = (bf16[8,16,512]{2,1,0:T(8,128)(2,1)}, bf16[8,16,512]{2,1,0:T(8,128)(2,1)S(1)}, u32[]{:S(2)}, u32[]{:S(2)}) collective-permute-start(bf16[8,16,512]{2,1,0:T(8,128)(2,1)} %feat_any.1), channel_id=1, source_target_pairs={{0,2},{1,3},{2,0},{3,1},{4,6},{5,7},{6,4},{7,5},{8,10},{9,11},{10,... | collective-permute-start | bytes 393224 | tf_op jit(solution)/shard_map/ppermute | solution.py:269
  3.7 1.1 %shard_map.67 = (bf16[8,16,512]{2,1,0:T(8,128)(2,1)S(1)}, bf16[8,16,512]{2,1,0:T(8,128)(2,1)S(1)}, bf16[27,16,64]{2,1,0:T(8,128)(2,1)S(1)}, s32[8,27]{1,0:T(8,12...) custom-call(bf16[8,16,512]{2,1,0:T(8,128)(2,1)} %feat_any.1, bf16[8,16,512]{2,1,0:T(8,128)(2,1)} %cot_any.1, ...), custom_call_target="tpu_custom_call" | custom-call | tf_op jit(solution)/shard_map/pallas_call | solution.py:23
  4.8 1.6 %collective-permute-start = (bf16[128,128]{1,0:T(8,128)(2,1)S(1)}, bf16[128,128]{1,0:T(8,128)(2,1)S(1)}, u32[]{:S(2)}, u32[]{:S(2)}) collective-permute-start(bf16[128,128]{1,0:T(8,128)(2,1)S(1)} %get-tuple-element.30), channel_id=1, source_target_pairs={{0,4},{4,0},{8,12},{12,8},{16,20},{20,16},{24,28},{28,24},{1,5},{5... | collective-permute-start | bytes 98312 | tf_op jit(solution)/shard_map/ppermute | solution.py:283
  6.3 0.7 %collective-permute-start.1 = (bf16[128,128]{1,0:T(8,128)(2,1)S(1)}, bf16[128,128]{1,0:T(8,128)(2,1)S(1)}, u32[]{:S(2)}, u32[]{:S(2)}) collective-permute-start(bf16[128,128]{1,0:T(8,128)(2,1)S(1)} %get-tuple-element.31), channel_id=1, source_target_pairs={{4,8},{8,4},{12,16},{16,12},{20,24},{24,20},{5,9},{9,5},{13,17},{1... | collective-permute-start | bytes 98312 | tf_op jit(solution)/shard_map/ppermute | solution.py:284
  7.0 1.8 %collective-permute-done.first_ref = bf16[128,128]{1,0:T(8,128)(2,1)S(1)} collective-permute-done((bf16[128,128]{1,0:T(8,128)(2,1)S(1)}, bf16[128,128]{1,0:T(8,128)(2,1)S(1)}, u32[]{:S(2)}, u32[]{:S(2)}) %collective-permute-start) | collective-permute-done | bytes 32800 | tf_op jit(solution)/shard_map/ppermute | solution.py:283
  8.7 0.0 collective-permute-done.1.second_ref
  8.7 0.0 collective-permute-done.2.feat2_ref.refs_2_
  8.7 0.1 shard_map.68.packed_ref.refs_4_
  8.9 0.4 %collective-permute-start.3 = (bf16[128,1024]{1,0:T(8,128)(2,1)S(1)}, bf16[128,1024]{1,0:T(8,128)(2,1)S(1)}, u32[]{:S(2)}, u32[]{:S(2)}) collective-permute-start(bf16[128,1024]{1,0:T(8,128)(2,1)S(1)} %shard_map.68.packed_ref.refs_4_), channel_id=1, source_target_pairs={{0,2},{1,3},{2,0},{3,1},{4,6},{5,7},{6,4},{7,5},{8,10},{9,11},{10,... | collective-permute-start | bytes 786440 | tf_op jit(solution)/shard_map/ppermute | solution.py:269
  9.3 0.0 collective-permute-start.4
  9.3 0.5 %collective-permute-start.5 = (bf16[8,16,512]{2,1,0:T(8,128)(2,1)S(1)}, bf16[8,16,512]{2,1,0:T(8,128)(2,1)S(1)}, u32[]{:S(2)}, u32[]{:S(2)}) collective-permute-start(bf16[8,16,512]{2,1,0:T(8,128)(2,1)S(1)} %collective-permute-done.2.feat2_ref.refs_2_), channel_id=1, source_target_pairs={{0,1},{1,0},{2,3},{3,2},{4,5},{5,4},{6,7},{7,6},{8,9},{9,8},{10,11... | collective-permute-start | bytes 393224 | tf_op jit(solution)/shard_map/ppermute | solution.py:269
  9.8 0.0 collective-permute-start.7
  9.8 1.2 %collective-permute-done.4.feat1_ref.refs_1_ = bf16[8,16,512]{2,1,0:T(8,128)(2,1)S(1)} collective-permute-done((bf16[8,16,512]{2,1,0:T(8,128)(2,1)}, bf16[8,16,512]{2,1,0:T(8,128)(2,1)S(1)}, u32[]{:S(2)}, u32[]{:S(2)}) %collective-permute-start.4) | collective-permute-done | bytes 131104 | tf_op jit(solution)/shard_map/ppermute | solution.py:269
  11.0 1.9 %shard_map.69 = (bf16[14,512,256]{2,1,0:T(8,128)(2,1)S(1)}, f32[4,32,128]{2,1,0:T(8,128)S(1)}) custom-call(s32[8,27]{1,0:T(8,128)S(1)} %get-tuple-element.34.near_ref, bf16[128,1024]{1,0:T(8,128)(2,1)S(1)} %shard_map.68.packed_ref.refs_4_, bf16[8,16,512]{2,1,0:T(8,128)(2,1)S(1)} %get-tuple-element.35.feat_ref.refs_0_, ...), custom_call_target="tpu_custom_call" | custom-call | tf_op jit(solution)/shard_map/pallas_call | solution.py:23
  12.9 0.0 collective-permute-done.5.feat3_ref.refs_3_
  12.9 1.3 %shard_map.70 = f32[224,128]{1,0:T(8,128)S(1)} custom-call(bf16[14,512,256]{2,1,0:T(8,128)(2,1)S(1)} %get-tuple-element.36.windows_ref, bf16[8,16,512]{2,1,0:T(8,128)(2,1)S(1)} %collective-permute-done.2.feat2_ref.refs_2_, bf16[8,16,512]{2,1,0:T(8,128)(2,1)S(1)} %collective-permute-done.5.feat3_ref.refs_3_, f32[4,32,128]{2,1,0:T(8,128)S(1)} %get-tuple-element.38.sums_ref), custom_call_target="tpu_custom_call" | custom-call | tf_op jit(solution)/shard_map/pallas_call | solution.py:23
  14.2 1.6 %collective-permute-done.3.refs_6_ = bf16[128,1024]{1,0:T(8,128)(2,1)S(1)} collective-permute-done((bf16[128,1024]{1,0:T(8,128)(2,1)S(1)}, bf16[128,1024]{1,0:T(8,128)(2,1)S(1)}, u32[]{:S(2)}, u32[]{:S(2)}) %collective-permute-start.3) | collective-permute-done | bytes 262176 | tf_op jit(solution)/shard_map/ppermute | solution.py:269
  15.9 0.0 collective-permute-start.8
  15.9 4.3 %collective-permute-start.6 = (f32[224,128]{1,0:T(8,128)S(1)}, f32[224,128]{1,0:T(8,128)S(1)}, u32[]{:S(2)}, u32[]{:S(2)}) collective-permute-start(f32[224,128]{1,0:T(8,128)S(1)} %shard_map.70), channel_id=1, source_target_pairs={{0,4},{4,0},{8,12},{12,8},{16,20},{20,16},{24,28},{28,24},{1,5},{5... | collective-permute-start | bytes 344072 | tf_op jit(solution)/shard_map/ppermute | solution.py:269
  20.1 0.0 collective-permute-done.7.refs_5_
  20.1 0.0 collective-permute-done.8.refs_7_
  20.1 3.1 %shard_map.71 = (bf16[8000,128]{1,0:T(8,128)(2,1)S(1)}, bf16[1152,128]{1,0:T(8,128)(2,1)S(1)}) custom-call(s32[8,27]{1,0:T(8,128)S(1)} %get-tuple-element.34.near_ref, bf16[27,16,64]{2,1,0:T(8,128)(2,1)S(1)} %get-tuple-element.29.weight_ref, bf16[8,16,512]{2,1,0:T(8,128)(2,1)S(1)} %get-tuple-element.35.feat_ref.refs_0_, ...), custom_call_target="tpu_custom_call" | custom-call | tf_op jit(solution)/shard_map/pallas_call | solution.py:23
  23.3 0.7 %collective-permute-done.6 = f32[224,128]{1,0:T(8,128)S(1)} collective-permute-done((f32[224,128]{1,0:T(8,128)S(1)}, f32[224,128]{1,0:T(8,128)S(1)}, u32[]{:S(2)}, u32[]{:S(2)}) %collective-permute-start.6) | collective-permute-done | bytes 114720 | tf_op jit(solution)/shard_map/ppermute | solution.py:269
  24.0 2.9 %collective-permute-start.9 = (f32[224,128]{1,0:T(8,128)S(1)}, f32[224,128]{1,0:T(8,128)S(1)}, u32[]{:S(2)}, u32[]{:S(2)}) collective-permute-start(f32[224,128]{1,0:T(8,128)S(1)} %add.6), channel_id=1, source_target_pairs={{0,8},{4,12},{8,0},{12,4},{16,24},{20,28},{24,16},{28,20},{1,9},{5... | collective-permute-start | bytes 344072 | tf_op jit(solution)/shard_map/ppermute | solution.py:269
  26.8 2.7 %shard_map.72.low_ref = f32[2048,128]{1,0:T(8,128)S(1)} custom-call(bf16[8000,128]{1,0:T(8,128)(2,1)S(1)} %get-tuple-element.44.grid_ref, bf16[1152,128]{1,0:T(8,128)(2,1)S(1)} %get-tuple-element.45.mat_ref), custom_call_target="tpu_custom_call" | custom-call | tf_op jit(solution)/shard_map/pallas_call | solution.py:23
  29.5 0.3 collective-permute-done.9
  29.9 2.8 %collective-permute-start.10 = (f32[224,128]{1,0:T(8,128)S(1)}, f32[224,128]{1,0:T(8,128)S(1)}, u32[]{:S(2)}, u32[]{:S(2)}) collective-permute-start(f32[224,128]{1,0:T(8,128)S(1)} %add.7.one_ref), channel_id=1, source_target_pairs={{0,16},{4,20},{8,24},{12,28},{16,0},{20,4},{24,8},{28,12},{1,17},{... | collective-permute-start | bytes 344072 | tf_op jit(solution)/shard_map/ppermute | solution.py:269
  32.7 3.9 %shard_map.73 = (bf16[8,16,512]{2,1,0:T(8,128)(2,1)}, bf16[8,16,512]{2,1,0:T(8,128)(2,1)}) custom-call(bf16[8000,128]{1,0:T(8,128)(2,1)S(1)} %get-tuple-element.44.grid_ref, bf16[1152,128]{1,0:T(8,128)(2,1)S(1)} %get-tuple-element.45.mat_ref, f32[2048,128]{1,0:T(8,128)S(1)} %shard_map.72.low_ref), custom_call_target="tpu_custom_call" | custom-call | tf_op jit(solution)/shard_map/pallas_call | solution.py:23
  36.6 0.9 %collective-permute-done.10.other_ref = f32[224,128]{1,0:T(8,128)S(1)} collective-permute-done((f32[224,128]{1,0:T(8,128)S(1)}, f32[224,128]{1,0:T(8,128)S(1)}, u32[]{:S(2)}, u32[]{:S(2)}) %collective-permute-start.10) | collective-permute-done | bytes 114720 | tf_op jit(solution)/shard_map/ppermute | solution.py:269
  37.5 0.8 %shard_map.74 = f32[27,16,64]{2,1,0:T(8,128)} custom-call(f32[224,128]{1,0:T(8,128)S(1)} %add.7.one_ref, f32[224,128]{1,0:T(8,128)S(1)} %collective-permute-done.10.other_ref), custom_call_target="tpu_custom_call" | custom-call | tf_op jit(solution)/shard_map/pallas_call | solution.py:23
  (2 shorter events, 0.0 us)
Async XLA Ops:
  0.6 8.1 %collective-permute-start.2 = (bf16[8,16,512]{2,1,0:T(8,128)(2,1)}, bf16[8,16,512]{2,1,0:T(8,128)(2,1)S(1)}, u32[]{:S(2)}, u32[]{:S(2)}) collective-permute-start(bf16[8,16,512]{2,1,0:T(8,128)(2,1)} %feat_any.1), channel_id=1, source_target_pairs={{0,2},{1,3},{2,0},{3,1},{4,6},{5,7},{6,4},{7,5},{8,10},{9,11},{10,... | collective-permute-start | bytes 393224 | tf_op jit(solution)/shard_map/ppermute | solution.py:269
  4.8 4.0 %collective-permute-start = (bf16[128,128]{1,0:T(8,128)(2,1)S(1)}, bf16[128,128]{1,0:T(8,128)(2,1)S(1)}, u32[]{:S(2)}, u32[]{:S(2)}) collective-permute-start(bf16[128,128]{1,0:T(8,128)(2,1)S(1)} %get-tuple-element.30), channel_id=1, source_target_pairs={{0,4},{4,0},{8,12},{12,8},{16,20},{20,16},{24,28},{28,24},{1,5},{5... | collective-permute-start | bytes 98312 | tf_op jit(solution)/shard_map/ppermute | solution.py:283
  6.3 2.4 %collective-permute-start.1 = (bf16[128,128]{1,0:T(8,128)(2,1)S(1)}, bf16[128,128]{1,0:T(8,128)(2,1)S(1)}, u32[]{:S(2)}, u32[]{:S(2)}) collective-permute-start(bf16[128,128]{1,0:T(8,128)(2,1)S(1)} %get-tuple-element.31), channel_id=1, source_target_pairs={{4,8},{8,4},{12,16},{16,12},{20,24},{24,20},{5,9},{9,5},{13,17},{1... | collective-permute-start | bytes 98312 | tf_op jit(solution)/shard_map/ppermute | solution.py:284
  8.9 7.0 %collective-permute-start.3 = (bf16[128,1024]{1,0:T(8,128)(2,1)S(1)}, bf16[128,1024]{1,0:T(8,128)(2,1)S(1)}, u32[]{:S(2)}, u32[]{:S(2)}) collective-permute-start(bf16[128,1024]{1,0:T(8,128)(2,1)S(1)} %shard_map.68.packed_ref.refs_4_), channel_id=1, source_target_pairs={{0,2},{1,3},{2,0},{3,1},{4,6},{5,7},{6,4},{7,5},{8,10},{9,11},{10,... | collective-permute-start | bytes 786440 | tf_op jit(solution)/shard_map/ppermute | solution.py:269
  9.3 1.7 %collective-permute-start.4 = (bf16[8,16,512]{2,1,0:T(8,128)(2,1)}, bf16[8,16,512]{2,1,0:T(8,128)(2,1)S(1)}, u32[]{:S(2)}, u32[]{:S(2)}) collective-permute-start(bf16[8,16,512]{2,1,0:T(8,128)(2,1)} %feat_any.1), channel_id=1, source_target_pairs={{0,1},{1,0},{2,3},{3,2},{4,5},{5,4},{6,7},{7,6},{8,9},{9,8},{10,11... | collective-permute-start | bytes 393224 | tf_op jit(solution)/shard_map/ppermute | solution.py:269
  9.3 3.6 %collective-permute-start.5 = (bf16[8,16,512]{2,1,0:T(8,128)(2,1)S(1)}, bf16[8,16,512]{2,1,0:T(8,128)(2,1)S(1)}, u32[]{:S(2)}, u32[]{:S(2)}) collective-permute-start(bf16[8,16,512]{2,1,0:T(8,128)(2,1)S(1)} %collective-permute-done.2.feat2_ref.refs_2_), channel_id=1, source_target_pairs={{0,1},{1,0},{2,3},{3,2},{4,5},{5,4},{6,7},{7,6},{8,9},{9,8},{10,11... | collective-permute-start | bytes 393224 | tf_op jit(solution)/shard_map/ppermute | solution.py:269
  9.8 10.3 %collective-permute-start.7 = (bf16[128,1024]{1,0:T(8,128)(2,1)S(1)}, bf16[128,1024]{1,0:T(8,128)(2,1)S(1)}, u32[]{:S(2)}, u32[]{:S(2)}) collective-permute-start(bf16[128,1024]{1,0:T(8,128)(2,1)S(1)} %shard_map.68.packed_ref.refs_4_), channel_id=1, source_target_pairs={{0,1},{1,0},{2,3},{3,2},{4,5},{5,4},{6,7},{7,6},{8,9},{9,8},{10,11... | collective-permute-start | bytes 786440 | tf_op jit(solution)/shard_map/ppermute | solution.py:269
  15.9 4.3 %collective-permute-start.8 = (bf16[128,1024]{1,0:T(8,128)(2,1)S(1)}, bf16[128,1024]{1,0:T(8,128)(2,1)S(1)}, u32[]{:S(2)}, u32[]{:S(2)}) collective-permute-start(bf16[128,1024]{1,0:T(8,128)(2,1)S(1)} %collective-permute-done.3.refs_6_), channel_id=1, source_target_pairs={{0,1},{1,0},{2,3},{3,2},{4,5},{5,4},{6,7},{7,6},{8,9},{9,8},{10,11... | collective-permute-start | bytes 786440 | tf_op jit(solution)/shard_map/ppermute | solution.py:269
  15.9 8.1 %collective-permute-start.6 = (f32[224,128]{1,0:T(8,128)S(1)}, f32[224,128]{1,0:T(8,128)S(1)}, u32[]{:S(2)}, u32[]{:S(2)}) collective-permute-start(f32[224,128]{1,0:T(8,128)S(1)} %shard_map.70), channel_id=1, source_target_pairs={{0,4},{4,0},{8,12},{12,8},{16,20},{20,16},{24,28},{28,24},{1,5},{5... | collective-permute-start | bytes 344072 | tf_op jit(solution)/shard_map/ppermute | solution.py:269
  24.0 5.9 %collective-permute-start.9 = (f32[224,128]{1,0:T(8,128)S(1)}, f32[224,128]{1,0:T(8,128)S(1)}, u32[]{:S(2)}, u32[]{:S(2)}) collective-permute-start(f32[224,128]{1,0:T(8,128)S(1)} %add.6), channel_id=1, source_target_pairs={{0,8},{4,12},{8,0},{12,4},{16,24},{20,28},{24,16},{28,20},{1,9},{5... | collective-permute-start | bytes 344072 | tf_op jit(solution)/shard_map/ppermute | solution.py:269
  29.9 7.6 %collective-permute-start.10 = (f32[224,128]{1,0:T(8,128)S(1)}, f32[224,128]{1,0:T(8,128)S(1)}, u32[]{:S(2)}, u32[]{:S(2)}) collective-permute-start(f32[224,128]{1,0:T(8,128)S(1)} %add.7.one_ref), channel_id=1, source_target_pairs={{0,16},{4,20},{8,24},{12,28},{16,0},{20,4},{24,8},{28,12},{1,17},{... | collective-permute-start | bytes 344072 | tf_op jit(solution)/shard_map/ppermute | solution.py:269

commit v2 on v1

v2 whole, which is shorter than its diff:
```python
import functools

import jax
import jax.numpy as jnp
from jax import lax
from jax.experimental import pallas as pl
from jax.experimental.pallas import tpu as pltpu
from jax.sharding import PartitionSpec as P

f32, bf16, i32 = jnp.float32, jnp.bfloat16, jnp.int32
VMEM = pl.BlockSpec(memory_space=pltpu.VMEM)
HBM = pl.BlockSpec(memory_space=pltpu.HBM)

COSTS = {}
GROUPS = ((0, 8), (8, 14), (14, 22), (22, 27))


def iota(shape, axis):
    return lax.broadcasted_iota(i32, shape, axis)


def call(kernel, out_shape, scratch, *args, specs):
    name = getattr(kernel, "func", kernel).__name__
    return pl.pallas_call(
        kernel,
        name=name,
        out_shape=out_shape,
        in_specs=specs,
        out_specs=jax.tree.map(lambda _: VMEM, out_shape),
        scratch_shapes=scratch,
        compiler_params=pltpu.CompilerParams(vmem_limit_bytes=48 << 20),
        cost_estimate=pl.CostEstimate(flops=COSTS.get(name, 0), bytes_accessed=0, transcendentals=0),
    )(*args)


def prepare_kernel(feat_any, cot_any, weight_any, near_any, both_ref, weight_ref, near_ref, first_ref, second_ref, sems):
    rows = first_ref.shape[0]
    pairs = (
        (feat_any, both_ref.at[:, :, 0:512]),
        (cot_any, both_ref.at[:, :, 512:1024]),
        (weight_any, weight_ref),
        (near_any, near_ref),
    )
    copies = [pltpu.make_async_copy(source, target, sems.at[i]) for i, (source, target) in enumerate(pairs)]
    for copy in copies:
        copy.start()
    for copy in copies[:2]:
        copy.wait()
    low = jnp.concatenate([both_ref[:, :, i : i + 64].reshape(rows, 64) for i in (0, 512)], axis=1)
    high = jnp.concatenate([both_ref[:, :, i : i + 64].reshape(rows, 64) for i in (448, 960)], axis=1)
    even = lax.axis_index("space") % 2 == 0

    @pl.when(even)
    def _():
        first_ref[...] = high
        second_ref[...] = low

    @pl.when(jnp.logical_not(even))
    def _():
        first_ref[...] = low
        second_ref[...] = high

    for copy in copies[2:]:
        copy.wait()


def pack_kernel(both_ref, weight_ref, first_ref, second_ref, near_pack_ref, far_pack_ref):
    rows = first_ref.shape[0]
    even = jnp.full((rows, 128), lax.axis_index("space") % 2, i32) == 0
    first, second = first_ref[...].astype(f32), second_ref[...].astype(f32)
    before = jnp.where(even, second, first)
    after = jnp.where(even, first, second)
    left = iota((rows, 128), 1) < 64
    feat = jnp.where(left, before, pltpu.roll(after, 64, 1)).astype(bf16)
    cot = jnp.where(left, pltpu.roll(before, 64, 1), after).astype(bf16)
    groups = []
    for group in range(4):
        taps = [weight_ref[8 * group + t] if 8 * group + t < 27 else jnp.zeros((16, 64), bf16) for t in range(8)]
        groups.append(jnp.concatenate(taps, axis=0))
    kernel = jnp.concatenate(groups, axis=1)
    spots, lanes = iota((256, 128), 0), iota((256, 128), 1)
    place = lax.axis_index("chan") // 2
    for target, pair in ((near_pack_ref, place), (far_pack_ref, place ^ 1)):
        target[:, 0:128] = feat
        target[:, 128:256] = cot
        owned = spots == 64 * (lanes // 32) + 32 * pair + lanes % 32
        part = jnp.dot(kernel, owned.astype(f32).astype(bf16), preferred_element_type=f32)
        target[:, 256:384] = part.astype(bf16)
    far_pack_ref[:, 384:896] = both_ref[:, :, 512:1024].reshape(rows, 512)


def tap_sums(products, count, bricks):
    lane_group = iota((16, 128), 1) // 16
    sums = []
    for begin, end in GROUPS:
        blocks = []
        for view in range(count):
            total = None
            for shift in range(8):
                chosen = None
                for brick in range(bricks):
                    start = (view * bricks + brick) * 16
                    block = products[min(begin + (brick + shift) % 8, end - 1), start : start + 16, :]
                    chosen = block if chosen is None else jnp.where(lane_group == brick, block, chosen)
                if shift:
                    chosen = pltpu.roll(chosen, 16 * shift, 1)
                total = chosen if total is None else total + chosen
            blocks.append(total)
        sums.append(blocks)
    return sums


def brick_picker(near_ref, rows):
    bricks = near_ref.shape[0]
    listed = near_ref[...]
    listed = jnp.where(listed < 0, bricks, listed % bricks).astype(f32)
    widen = (iota((bricks, rows), 1) // 16 == iota((bricks, rows), 0)).astype(f32)
    source = lax.dot_general(listed, widen, (((0,), (0,)), ((), ())), preferred_element_type=f32)
    source = source.astype(i32) * 16 + iota((27, rows), 1) % 16
    row_ids = iota((rows, rows), 0)

    def pick(i, j):
        first = 9 * i + 3 * j
        picks = [(row_ids == source[first + k : first + k + 1, :]).astype(f32).astype(bf16) for k in range(3)]
        return jnp.concatenate(picks, axis=1)

    return pick


def shifted_columns(columns, pick, j):
    if j != 1:
        columns = columns[:, 7:8] if j == 0 else columns[:, 0:1]
    wide, deep = columns.shape[0], columns.shape[1]
    count = wide * deep
    edge = iota((1, 8, 128), 1)
    moved = jnp.dot(columns.reshape(count * 8, 128), pick, preferred_element_type=f32)
    lower, own, upper = (moved[:, 128 * k : 128 * k + 128].reshape(count, 8, 128) for k in range(3))
    down = jnp.where(edge == 0, pltpu.roll(lower, 1, 1), pltpu.roll(own, 1, 1))
    up = jnp.where(edge == 7, pltpu.roll(upper, 7, 1), pltpu.roll(own, 7, 1))
    return [value.reshape(wide, deep, 8, 128) for value in (down, own, up)]


ROWS_TO = ((0, 1), (1, 9), (9, 10))


def near_grad_kernel(near_ref, both_ref, both1_ref, windows_ref, sums_ref, padded, products):
    bricks = near_ref.shape[0]
    rows = bricks * 16
    flat = jnp.transpose(both_ref[:, :, 512:1024].reshape(rows, 512).astype(f32)).astype(bf16).reshape(8, 8, 8, 128)
    pick = brick_picker(near_ref, rows)
    for x in (0, 9):
        padded[:, x] = jnp.zeros((3, 10, 8, 128), f32)
    for j in range(3):
        for c, value in enumerate(shifted_columns(flat, pick(1, j), j)):
            padded[c, 1:9, ROWS_TO[j][0] : ROWS_TO[j][1]] = value
    feat = jnp.concatenate([view[:, :, 0:512].reshape(rows, 512) for view in (both_ref, both1_ref)], axis=0)
    for pair in range(14):
        views = []
        for tap in (2 * pair, min(2 * pair + 1, 26)):
            a, b, c = (26 - tap) // 9, (26 - tap) // 3 % 3, (26 - tap) % 3
            views.append(padded[c, a : a + 8, b : b + 8].reshape(512, 128).astype(bf16))
        window = jnp.concatenate(views, axis=1)
        windows_ref[pair] = window
        both = jnp.dot(feat, window, preferred_element_type=f32)
        products[2 * pair] = both[:, 0:128]
        products[2 * pair + 1] = both[:, 128:256]
    sums = tap_sums(products, 2, bricks)
    for group in range(4):
        sums_ref[group] = jnp.concatenate(sums[group], axis=0)


def plane_ends(views, side):
    rows = views[0].shape[0] * 16
    start = 0 if side == 0 else 448
    return jnp.concatenate([view[:, :, start : start + 64].reshape(rows, 64) for view in views], axis=0)


def halo_grad_kernel(near_ref, packed_ref, both_ref, both1_ref, sums_ref, windows_ref, total_ref, edges, products):
    bricks = near_ref.shape[0]
    rows = bricks * 16
    planes = jnp.transpose(packed_ref[:, 128:256].astype(f32)).astype(bf16)
    pick = brick_picker(near_ref, rows)
    for side in range(2):
        columns = planes[64 * side : 64 * side + 64].reshape(1, 8, 8, 128)
        for j in range(3):
            for c, value in enumerate(shifted_columns(columns, pick(2 * side, j), j)):
                edges[side, c, ROWS_TO[j][0] : ROWS_TO[j][1]] = value.reshape(value.shape[1:])
    for side in range(2):
        views = []
        for place in range(9):
            b, c = (8 - place) // 3, (8 - place) % 3
            views.append(edges[side, c, b : b + 8].reshape(64, 128).astype(bf16))
        window = jnp.concatenate(views, axis=1)
        windows_ref[side] = window
        both = jnp.dot(plane_ends([both_ref, both1_ref], side), window, preferred_element_type=f32)
        for place in range(9):
            products[18 * (1 - side) + place] = both[:, 128 * place : 128 * place + 128]
    for place in range(9, 18):
        products[place] = jnp.zeros((2 * rows, 128), f32)
    sums = tap_sums(products, 2, bricks)
    for group in range(4):
        total_ref[group] = sums_ref[group] + jnp.concatenate(sums[group], axis=0)


def far_grad_kernel(scale, windows_ref, edge_windows_ref, feat2_ref, feat3_ref, sums_ref, part_ref, products, ordered):
    chan = lax.axis_index("chan")
    bricks = feat2_ref.shape[0]
    rows = bricks * 16
    views = [feat2_ref, feat3_ref]
    for side in range(2):
        both = jnp.dot(plane_ends(views, side), edge_windows_ref[side], preferred_element_type=f32)
        for place in range(9):
            products[18 * (1 - side) + place] = both[:, 128 * place : 128 * place + 128]
    far = jnp.concatenate([view[...].reshape(rows, 512) for view in views], axis=0)
    for pair in range(14):
        both = jnp.dot(far, windows_ref[pair], preferred_element_type=f32)
        for tap in range(2 * pair, min(2 * pair + 2, 27)):
            one = both[:, 128 * (tap % 2) : 128 * (tap % 2) + 128]
            products[tap] = one if 9 <= tap < 18 else one + products[tap]
    sums = tap_sums(products, 2, bricks)
    for group in range(4):
        both = sums_ref[group]
        for apart, block in enumerate((both[0:16], both[16:32], *sums[group])):
            ordered[group, pl.ds(pl.multiple_of(16 * (chan ^ apart), 16), 16), :] = block
    part_ref[0:128] = jnp.transpose(jnp.concatenate([ordered[0], ordered[2]], axis=0)) * scale
    part_ref[128:224] = jnp.transpose(jnp.concatenate([ordered[1], ordered[3]], axis=0))[0:96] * scale


def pad_bricks(near, padded, source, size, xs):
    bricks = near.shape[0]
    for r in range(bricks):
        for i, base, x_pairs in xs:
            for j in range(3):
                for k in range(3):
                    listed = near[r, 9 * i + 3 * j + k]
                    start = jnp.where(listed < 0, bricks, listed % bricks) * size + base
                    y_pairs = [(y + 1, y) for y in range(8)] if j == 1 else [(0, 7) if j == 0 else (9, 0)]
                    z_to, z_from = (1, 0) if k == 1 else ((0, 7) if k == 0 else (9, 0))
                    if k == 1:
                        for x_to, x_from in x_pairs:
                            for y_to, y_from in y_pairs:
                                piece = source[pl.ds(start + 64 * x_from + 8 * y_from, 8), :]
                                padded[pl.ds(80 * (10 * x_to + y_to) + 8 + r, 8, 8), :] = piece
                    elif j == 1:
                        for x_to, x_from in x_pairs:
                            piece = source[pl.ds(start + 64 * x_from + z_from, 8, 8), :]
                            padded[pl.ds(80 * (10 * x_to + 1) + 8 * z_to + r, 8, 80), :] = piece
                    elif i == 1:
                        piece = source[pl.ds(start + 8 * y_pairs[0][1] + z_from, 8, 64), :]
                        padded[pl.ds(80 * y_pairs[0][0] + 8 * z_to + r, 8, 800), :] = piece
                    else:
                        piece = source[pl.ds(start + 8 * y_pairs[0][1] + z_from, 1), :]
                        padded[pl.ds(80 * (10 * x_pairs[0][0] + y_pairs[0][0]) + 8 * z_to + r, 1), :] = piece


def inner_kernel(near_ref, weight_ref, *refs):
    both, both1, feat2, feat3 = refs[:4]
    packs, (grid_ref, mat_ref, flat, padded, near, sem) = refs[4:8], refs[8:]
    copy = pltpu.make_async_copy(near_ref, near, sem)
    copy.start()
    bricks = feat2.shape[0]
    feats = [both.at[:, :, 0:512], both1.at[:, :, 0:512], feat2, feat3]
    cots = [both.at[:, :, 512:1024], both1.at[:, :, 512:1024]]
    for s in range(bricks):
        rows = slice(16 * s, 16 * s + 16)
        views = [view[s] for view in feats + cots] + [pack[rows, 384:896] for pack in packs[2:]]
        flat[512 * s : 512 * s + 512] = jnp.transpose(jnp.concatenate(views, axis=0).astype(f32))
    flat[512 * bricks : 512 * bricks + 512] = jnp.zeros((512, 128), f32)

    chan = lax.axis_index("chan")
    lanes = iota((48, 128), 1)
    spots = iota((48, 128), 0)
    forward = (lanes == 32 * (spots // 16) + spots % 16).astype(f32).astype(bf16)
    lanes = iota((128, 128), 1)
    spots = iota((128, 128), 0)
    picks = {}
    for group in range(4):
        for c in range(3):
            hit = lanes - 32 * c - 16 == spots - 32 * group - 16 * (chan % 2)
            hit = hit & (lanes >= 32 * c + 16) & (lanes < 32 * c + 32)
            picks[group, c] = hit.astype(f32).astype(bf16)
    for spot in range(9):
        own = weight_ref[3 * spot : 3 * spot + 3].reshape(48, 64)
        turned = lax.dot_general(own, forward, (((0,), (0,)), ((), ())), preferred_element_type=f32).astype(bf16)
        for q in range(4):
            mat_ref[pl.ds(pl.multiple_of(128 * spot + 16 * (chan ^ q), 16), 16), :] = turned[16 * q : 16 * q + 16]
        total = None
        for c in range(3):
            tap = 26 - 3 * spot - c
            block = jnp.concatenate([pack[16 * (tap % 8) : 16 * (tap % 8) + 16, 256:384] for pack in packs], axis=0)
            term = jnp.dot(block, picks[tap // 8, c], preferred_element_type=f32)
            total = term if total is None else total + term
        mat_ref[128 * spot + 64 : 128 * spot + 128] = total.astype(bf16)

    copy.wait()
    pad_bricks(near, padded, flat, 512, [(1, 0, [(x, x) for x in range(8)])])
    for x in range(8):
        grid_ref[800 * x : 800 * x + 800] = padded[800 * x : 800 * x + 800].astype(bf16)


def conv_layer(views, mat_ref):
    pieces = [view[80 * b : 80 * b + 640, :] for view in views for b in range(3)]
    sums = jnp.dot(jnp.concatenate(pieces, axis=1), mat_ref[...], preferred_element_type=f32).reshape(8, 80, 128)
    total = sums[:, 0:64] + pltpu.roll(sums[:, 8:72], 96, 2) + pltpu.roll(sums[:, 16:80], 64, 2)
    return total.reshape(512, 128)


def middle_kernel(grid_ref, mat_ref, done_ref):
    def layer(x, carry):
        views = [grid_ref.at[pl.ds(pl.multiple_of(800 * (x + a), 16), 800)] for a in range(3)]
        done_ref[pl.ds(pl.multiple_of(512 * x, 512), 512), :] = conv_layer(views, mat_ref)
        return carry

    lax.fori_loop(0, 6, layer, 0)


def outer_kernel(near_ref, grid_ref, mat_ref, middle_ref, *refs):
    packs, (out_ref, grad_ref, planes, padded, edges, low, high, near, sem) = refs[:4], refs[4:]
    copy = pltpu.make_async_copy(near_ref, near, sem)
    copy.start()
    bricks = near_ref.shape[0]
    for s in range(bricks):
        rows = slice(16 * s, 16 * s + 16)
        pair = jnp.concatenate([pack[rows, 0:128] for pack in packs] + [pack[rows, 128:256] for pack in packs], axis=0)
        planes[128 * s : 128 * s + 128] = jnp.transpose(pair.astype(f32))
    planes[128 * bricks : 128 * bricks + 128] = jnp.zeros((128, 128), f32)
    copy.wait()
    pad_bricks(near, padded, planes, 128, [(0, 0, [(0, 0)]), (2, 64, [(1, 0)])])
    edges[...] = padded[...].astype(bf16)
    layers = [edges.at[0:800]] + [grid_ref.at[800 * x : 800 * x + 800] for x in (0, 1, 6, 7)] + [edges.at[800:1600]]
    low[...] = conv_layer(layers[0:3], mat_ref)
    high[...] = conv_layer(layers[3:6], mat_ref)
    for r in range(bricks):
        views = [low[pl.ds(r, 64, 8), :], middle_ref[pl.ds(r, 384, 8), :], high[pl.ds(r, 64, 8), :]]
        turned = jnp.transpose(jnp.concatenate(views, axis=0))
        out_ref[r] = turned[0:16].astype(bf16)
        grad_ref[r] = turned[16:32].astype(bf16)


def finish_kernel(one_ref, other_ref, grad_ref):
    total = one_ref[...] + other_ref[...]
    for tap in range(27):
        slot = tap % 14
        block = total[16 * slot : 16 * slot + 16]
        grad_ref[tap] = block[:, 0:64] if tap < 14 else block[:, 64:128]


def body(features, weight, cotangent, neighbours):
    bricks, narrow = features.shape[0], features.shape[1]
    rows = bricks * narrow
    length = lax.axis_size("space")
    shape = jax.ShapeDtypeStruct

    def across(name, value, apart, axis="chan"):
        with jax.named_scope(name):
            return lax.ppermute(value, axis, [(i, i ^ apart) for i in range(lax.axis_size(axis))])

    inputs = (features, cotangent, weight, neighbours)
    inputs = (features, cotangent, weight, neighbours)
    both, own, near, first, second = call(
        prepare_kernel,
        (
            shape((bricks, narrow, 1024), bf16),
            shape(weight.shape, bf16),
            shape(neighbours.shape, i32),
            shape((rows, 128), bf16),
            shape((rows, 128), bf16),
        ),
        [pltpu.SemaphoreType.DMA((4,))],
        *(pltpu.with_memory_space_constraint(view, pltpu.HBM) for view in inputs),
        specs=[HBM] * 4,
    )
    def meet(value, begin):
        mates = {i: i + 1 for i in range(begin, length - 1, 2)}
        mates.update({after: before for before, after in mates.items()})
        wide = lax.axis_size("chan")
        place = lambda i, c: mates[i] * wide + c if i in mates else i * wide + (c ^ 1)
        pairs = [(i * wide + c, place(i, c)) for i in range(length) for c in range(wide)]
        return lax.ppermute(value, ("space", "chan"), pairs)

    with jax.named_scope("plane_first"):
        first = meet(first, 0)
    with jax.named_scope("plane_second"):
        second = meet(second, 1)
    both1 = across("both_core", both, 1)
    feat2 = across("feat_y", features, 2)
    windows, sums = call(
        near_grad_kernel,
        (shape((14, 512, 256), bf16), shape((4, 32, 128), f32)),
        [pltpu.VMEM((3, 10, 10, 8, 128), f32), pltpu.VMEM((28, 2 * rows, 128), f32)],
        near, both, both1,
        specs=[VMEM] * 3,
    )
    first, second, sums = lax.optimization_barrier((first, second, sums))
    near_pack, far_pack = call(
        pack_kernel,
        (shape((rows, 384), bf16), shape((rows, 896), bf16)),
        [],
        both, own, first, second,
        specs=[VMEM] * 4,
    )
    far_pack2 = across("pack_y", far_pack, 2)
    edge_windows, sums = call(
        halo_grad_kernel,
        (shape((2, 64, 1152), bf16), shape((4, 32, 128), f32)),
        [pltpu.VMEM((2, 3, 10, 8, 128), f32), pltpu.VMEM((27, 2 * rows, 128), f32)],
        near, near_pack, both, both1, sums,
        specs=[VMEM] * 5,
    )
    feat3 = across("feat_far", feat2, 1)
    part = call(
        functools.partial(far_grad_kernel, float(bricks * length * 512) ** -0.5),
        shape((224, 128), f32),
        [pltpu.VMEM((27, 2 * rows, 128), f32), pltpu.VMEM((4, 64, 128), f32)],
        windows, edge_windows, feat2, feat3, sums,
        specs=[VMEM] * 5,
    )
    steps = []
    step = 1
    while step < length:
        steps.append(step)
        step *= 2
    other = across("sum_first", part, steps[0], "space")
    near_pack1 = across("pack_core", near_pack, 1)
    far_pack3 = across("pack_far", far_pack2, 1)
    grid, matrix = call(
        inner_kernel,
        (shape((6400, 128), bf16), shape((1152, 128), bf16)),
        [
            pltpu.VMEM(((bricks + 1) * 512, 128), f32),
            pltpu.VMEM((6400, 128), f32),
            pltpu.SMEM(neighbours.shape, i32),
            pltpu.SemaphoreType.DMA,
        ],
        near, own, both, both1, feat2, feat3, near_pack, near_pack1, far_pack2, far_pack3,
        specs=[VMEM] * 10,
    )
    for step in steps[1:]:
        part = part + other
        if step < steps[-1]:
            other = across("sum_next", part, step, "space")
            other, grid = lax.optimization_barrier((other, grid))
        else:
            other = across("sum_last", part, step, "space")
    middle = call(middle_kernel, shape((3072, 128), f32), [], grid, matrix, specs=[VMEM, VMEM])
    output, grad_input = call(
        outer_kernel,
        (shape(features.shape, bf16), shape(features.shape, bf16)),
        [
            pltpu.VMEM(((bricks + 1) * 128, 128), f32),
            pltpu.VMEM((1600, 128), f32),
            pltpu.VMEM((1600, 128), bf16),
            pltpu.VMEM((512, 128), f32),
            pltpu.VMEM((512, 128), f32),
            pltpu.SMEM(neighbours.shape, i32),
            pltpu.SemaphoreType.DMA,
        ],
        near, grid, matrix, middle, near_pack, near_pack1, far_pack2, far_pack3,
        specs=[VMEM] * 8,
    )
    other, output, grad_input = lax.optimization_barrier((other, output, grad_input))
    grad_weight = call(finish_kernel, shape(weight.shape, f32), [], part, other, specs=[VMEM, VMEM])
    return (output, grad_input, grad_weight)


def solution(mesh):
    in_specs = (
        P("space", "chan", None),
        P(None, "chan", None),
        P("space", "chan", None),
        P("space", None),
    )
    out_specs = (P("space", "chan", None), P("space", "chan", None), P(None, "chan", None))
    return jax.shard_map(body, mesh=mesh, in_specs=in_specs, out_specs=out_specs, check_vma=False)
```

time: 38.4 us -> 35.7 us (0.930)
  starting transfers between devices: 16.1 us -> 12 us
  Pallas kernels: 14.9 us -> 15.8 us
  waiting for transfers between devices: 6.52 us -> 7 us
    ppermute x9, starting transfers between devices: 13.9 us -> 9.22 us  [across(): lax.ppermute(value, axis, [(i, i ^ apart) for i in range(lax.axis_size(ax...]
    ppermute x9, waiting for transfers between devices: 4.76 us -> 6.99 us  [across(): lax.ppermute(value, axis, [(i, i ^ apart) for i in range(lax.axis_size(ax...]
    ppermute x2, waiting for transfers between devices: 1.76 us -> 0.01 us  [meet(): return lax.ppermute(value, ('space', 'chan'), pairs)]
    pallas_call x8 -> x9, Pallas kernels: 14.9 us -> 15.8 us  [call(): pl.pallas_call(kernel, name=name, out_shape=out_shape, in_specs=specs, ou...]
    ppermute x2, starting transfers between devices: 2.21 us -> 2.74 us  [meet(): return lax.ppermute(value, ('space', 'chan'), pairs)]
  transfers between devices with their start and end apart: 11 -> 11, of which waited for: 6 -> 4; matrix products, arithmetic and copies ran while one was open for 0% -> 0% of each run, Pallas kernels for 37% -> 39%
where the time goes in v2:
time: 35.7 us; the launch traced here: 35.6 us
  Pallas kernels  15.8 us (44%)
  starting transfers between devices  12 us (34%)
  waiting for transfers between devices  7 us (20%)
  between operations  0.74 us (2%)
    pallas_call x9, Pallas kernels, call(): pl.pallas_call(kernel, name=name, out_shape=out_shape, in_specs=specs, ou...  15.8 us
    ppermute x9, starting transfers between devices, across(): lax.ppermute(value, axis, [(i, i ^ apart) for i in range(lax.axis_size(ax...  9.22 us
    ppermute x9, waiting for transfers between devices, across(): lax.ppermute(value, axis, [(i, i ^ apart) for i in range(lax.axis_size(ax...  6.99 us
    ppermute x2, starting transfers between devices, meet(): return lax.ppermute(value, ('space', 'chan'), pairs)  2.74 us
  transfers between devices with their start and end apart: 11, of which 4 were waited for; matrix products, arithmetic and copies ran while one was open for 0% of the time, Pallas kernels for 39%

profile of v2, /device:TPU:0, one launch (start us, length us, event | category | flops | bytes accessed | tf_op | source)
XLA Modules:
  0.0 35.6 jit_solution(4710739735113277157)
XLA Ops:
  0.6 1.1 %prepare_kernel.1 = (bf16[8,16,1024]{2,1,0:T(8,128)(2,1)S(1)}, bf16[27,16,64]{2,1,0:T(8,128)(2,1)S(1)}, s32[8,27]{1,0:T(8,128)S(1)}, bf16[128,128]{1,0:T(8,128)(2,1)S(1)}, bf16[128,128]{1,0:T(8,128)(2,1)S(1)}) custom-call(bf16[8,16,512]{2,1,0:T(8,128)(2,1)} %feat_any.1, bf16[8,16,512]{2,1,0:T(8,128)(2,1)} %cot_any.1, bf16[27,16,64]{2,1,0:T(8,128)(2,1)} %weight_any.1, ...), custom_call_target="tpu_custom_call" | custom-call | tf_op jit(solution)/shard_map/prepare_kernel/pallas_call | solution.py:24
  1.7 0.5 %collective-permute-start = (bf16[8,16,1024]{2,1,0:T(8,128)(2,1)S(1)}, bf16[8,16,1024]{2,1,0:T(8,128)(2,1)S(1)}, u32[]{:S(2)}, u32[]{:S(2)}) collective-permute-start(bf16[8,16,1024]{2,1,0:T(8,128)(2,1)S(1)} %get-tuple-element.27.both_ref.refs_0_), channel_id=1, source_target_pairs={{0,1},{1,0},{2,3},{3,2},{4,5},{5,4},{6,7},{7,6},{8,9},{9,8},{10,11... | collective-permute-start | bytes 786440 | tf_op jit(solution)/shard_map/both_core/ppermute | solution.py:356
  2.3 2.6 %collective-permute-start.1 = (bf16[128,128]{1,0:T(8,128)(2,1)S(1)}, bf16[128,128]{1,0:T(8,128)(2,1)S(1)}, u32[]{:S(2)}, u32[]{:S(2)}) collective-permute-start(bf16[128,128]{1,0:T(8,128)(2,1)S(1)} %get-tuple-element.30), channel_id=1, source_target_pairs={{0,4},{1,5},{2,6},{3,7},{4,0},{5,1},{6,2},{7,3},{8,12},{9,13},{10,... | collective-permute-start | bytes 98312 | tf_op jit(solution)/shard_map/plane_first/ppermute | solution.py:379
  4.8 0.2 collective-permute-start.2
  5.0 1.5 %collective-permute-start.3 = (bf16[8,16,512]{2,1,0:T(8,128)(2,1)}, bf16[8,16,512]{2,1,0:T(8,128)(2,1)S(1)}, u32[]{:S(2)}, u32[]{:S(2)}) collective-permute-start(bf16[8,16,512]{2,1,0:T(8,128)(2,1)} %feat_any.1), channel_id=1, source_target_pairs={{0,2},{1,3},{2,0},{3,1},{4,6},{5,7},{6,4},{7,5},{8,10},{9,11},{10,... | collective-permute-start | bytes 393224 | tf_op jit(solution)/shard_map/feat_y/ppermute | solution.py:356
  6.5 0.0 collective-permute-done.both1_ref.refs_1_
  6.5 1.8 %near_grad_kernel.1 = (bf16[14,512,256]{2,1,0:T(8,128)(2,1)S(1)}, f32[4,32,128]{2,1,0:T(8,128)S(1)}) custom-call(s32[8,27]{1,0:T(8,128)S(1)} %get-tuple-element.26.near_ref, bf16[8,16,1024]{2,1,0:T(8,128)(2,1)S(1)} %get-tuple-element.27.both_ref.refs_0_, bf16[8,16,1024]{2,1,0:T(8,128)(2,1)S(1)} %collective-permute-done.both1_ref.refs_1_), custom_call_target="tpu_custom_call" | custom-call | tf_op jit(solution)/shard_map/near_grad_kernel/pallas_call | solution.py:24
  8.3 0.0 collective-permute-done.1.first_ref
  8.3 0.0 collective-permute-done.2.second_ref
  8.4 0.2 pack_kernel.1
  8.6 0.6 %collective-permute-start.8 = (bf16[128,896]{1,0:T(8,128)(2,1)S(1)}, bf16[128,896]{1,0:T(8,128)(2,1)S(1)}, u32[]{:S(2)}, u32[]{:S(2)}) collective-permute-start(bf16[128,896]{1,0:T(8,128)(2,1)S(1)} %get-tuple-element.39), channel_id=1, source_target_pairs={{0,2},{1,3},{2,0},{3,1},{4,6},{5,7},{6,4},{7,5},{8,10},{9,11},{10,... | collective-permute-start | bytes 688136 | tf_op jit(solution)/shard_map/pack_y/ppermute | solution.py:356
  9.2 1.8 %collective-permute-done.3.feat2_ref.refs_2_ = bf16[8,16,512]{2,1,0:T(8,128)(2,1)S(1)} collective-permute-done((bf16[8,16,512]{2,1,0:T(8,128)(2,1)}, bf16[8,16,512]{2,1,0:T(8,128)(2,1)S(1)}, u32[]{:S(2)}, u32[]{:S(2)}) %collective-permute-start.3) | collective-permute-done | bytes 131104 | tf_op jit(solution)/shard_map/feat_y/ppermute | solution.py:356
  10.9 0.0 collective-permute-start.4
  11.0 0.9 %halo_grad_kernel.1 = (bf16[2,64,1152]{2,1,0:T(8,128)(2,1)S(1)}, f32[4,32,128]{2,1,0:T(8,128)S(1)}) custom-call(s32[8,27]{1,0:T(8,128)S(1)} %get-tuple-element.26.near_ref, bf16[128,384]{1,0:T(8,128)(2,1)S(1)} %get-tuple-element.35.packed_ref.refs_4_.refs_0_, bf16[8,16,1024]{2,1,0:T(8,128)(2,1)S(1)} %get-tuple-element.27.both_ref.refs_0_, ...), custom_call_target="tpu_custom_call" | custom-call | tf_op jit(solution)/shard_map/halo_grad_kernel/pallas_call | solution.py:24
  11.9 0.4 %collective-permute-done.4.feat3_ref.refs_3_ = bf16[8,16,512]{2,1,0:T(8,128)(2,1)S(1)} collective-permute-done((bf16[8,16,512]{2,1,0:T(8,128)(2,1)S(1)}, bf16[8,16,512]{2,1,0:T(8,128)(2,1)S(1)}, u32[]{:S(2)}, u32[]{:S(2)}) %collective-permute-start.4) | collective-permute-done | bytes 131104 | tf_op jit(solution)/shard_map/feat_far/ppermute | solution.py:356
  12.3 1.6 %far_grad_kernel.1 = f32[224,128]{1,0:T(8,128)S(1)} custom-call(bf16[14,512,256]{2,1,0:T(8,128)(2,1)S(1)} %get-tuple-element.28.windows_ref, bf16[2,64,1152]{2,1,0:T(8,128)(2,1)S(1)} %get-tuple-element.37.edge_windows_ref, bf16[8,16,512]{2,1,0:T(8,128)(2,1)S(1)} %collective-permute-done.3.feat2_ref.refs_2_, ...), custom_call_target="tpu_custom_call" | custom-call | tf_op jit(solution)/shard_map/far_grad_kernel/pallas_call | solution.py:24
  13.9 2.5 %collective-permute-start.5 = (f32[224,128]{1,0:T(8,128)S(1)}, f32[224,128]{1,0:T(8,128)S(1)}, u32[]{:S(2)}, u32[]{:S(2)}) collective-permute-start(f32[224,128]{1,0:T(8,128)S(1)} %far_grad_kernel.1), channel_id=1, source_target_pairs={{0,4},{4,0},{8,12},{12,8},{16,20},{20,16},{24,28},{28,24},{1,5},{5... | collective-permute-start | bytes 344072 | tf_op jit(solution)/shard_map/sum_first/ppermute | solution.py:356
  16.4 0.0 collective-permute-done.8.refs_6_.refs_2_
  16.4 0.0 collective-permute-start.9
  16.4 3.5 %collective-permute-done.5 = f32[224,128]{1,0:T(8,128)S(1)} collective-permute-done((f32[224,128]{1,0:T(8,128)S(1)}, f32[224,128]{1,0:T(8,128)S(1)}, u32[]{:S(2)}, u32[]{:S(2)}) %collective-permute-start.5) | collective-permute-done | bytes 114720 | tf_op jit(solution)/shard_map/sum_first/ppermute | solution.py:356
  19.8 1.6 %collective-permute-start.6 = (f32[224,128]{1,0:T(8,128)S(1)}, f32[224,128]{1,0:T(8,128)S(1)}, u32[]{:S(2)}, u32[]{:S(2)}) collective-permute-start(f32[224,128]{1,0:T(8,128)S(1)} %add.6), channel_id=1, source_target_pairs={{0,8},{4,12},{8,0},{12,4},{16,24},{20,28},{24,16},{28,20},{1,9},{5... | collective-permute-start | bytes 344072 | tf_op jit(solution)/shard_map/sum_next/ppermute | solution.py:356
  21.5 0.0 collective-permute-start.7
  21.5 1.3 %collective-permute-done.7.refs_5_.refs_1_ = bf16[128,384]{1,0:T(8,128)(2,1)S(1)} collective-permute-done((bf16[128,384]{1,0:T(8,128)(2,1)S(1)}, bf16[128,384]{1,0:T(8,128)(2,1)S(1)}, u32[]{:S(2)}, u32[]{:S(2)}) %collective-permute-start.7) | collective-permute-done | bytes 98336 | tf_op jit(solution)/shard_map/pack_core/ppermute | solution.py:356
  22.8 0.0 collective-permute-done.9.refs_7_.refs_3_
  22.8 2.4 %inner_kernel.1 = (bf16[6400,128]{1,0:T(8,128)(2,1)S(1)}, bf16[1152,128]{1,0:T(8,128)(2,1)S(1)}) custom-call(s32[8,27]{1,0:T(8,128)S(1)} %get-tuple-element.26.near_ref, bf16[27,16,64]{2,1,0:T(8,128)(2,1)S(1)} %get-tuple-element.29.weight_ref, bf16[8,16,1024]{2,1,0:T(8,128)(2,1)S(1)} %get-tuple-element.27.both_ref.refs_0_, ...), custom_call_target="tpu_custom_call" | custom-call | tf_op jit(solution)/shard_map/inner_kernel/pallas_call | solution.py:24
  25.2 0.0 collective-permute-done.6
  25.2 2.5 %collective-permute-start.10 = (f32[224,128]{1,0:T(8,128)S(1)}, f32[224,128]{1,0:T(8,128)S(1)}, u32[]{:S(2)}, u32[]{:S(2)}) collective-permute-start(f32[224,128]{1,0:T(8,128)S(1)} %add.7.one_ref), channel_id=1, source_target_pairs={{0,16},{4,20},{8,24},{12,28},{16,0},{20,4},{24,8},{28,12},{1,17},{... | collective-permute-start | bytes 344072 | tf_op jit(solution)/shard_map/sum_last/ppermute | solution.py:356
  27.7 4.1 %middle_kernel.1.middle_ref = f32[3072,128]{1,0:T(8,128)S(1)} custom-call(bf16[6400,128]{1,0:T(8,128)(2,1)S(1)} %get-tuple-element.42.grid_ref, bf16[1152,128]{1,0:T(8,128)(2,1)S(1)} %get-tuple-element.43.mat_ref), custom_call_target="tpu_custom_call" | custom-call | tf_op jit(solution)/shard_map/middle_kernel/pallas_call | solution.py:24
  31.8 3.0 %outer_kernel.1 = (bf16[8,16,512]{2,1,0:T(8,128)(2,1)}, bf16[8,16,512]{2,1,0:T(8,128)(2,1)}) custom-call(s32[8,27]{1,0:T(8,128)S(1)} %get-tuple-element.26.near_ref, bf16[6400,128]{1,0:T(8,128)(2,1)S(1)} %get-tuple-element.42.grid_ref, bf16[1152,128]{1,0:T(8,128)(2,1)S(1)} %get-tuple-element.43.mat_ref, f32[3072,128]{1,0:T(8,128)S(1)} %middle_kernel.1.middle_ref, ...), custom_call_target="tpu_custom_call" | custom-call | tf_op jit(solution)/shard_map/outer_kernel/pallas_call | solution.py:24
  34.8 0.0 collective-permute-done.10.other_ref
  34.8 0.8 %finish_kernel.1 = f32[27,16,64]{2,1,0:T(8,128)} custom-call(f32[224,128]{1,0:T(8,128)S(1)} %add.7.one_ref, f32[224,128]{1,0:T(8,128)S(1)} %collective-permute-done.10.other_ref), custom_call_target="tpu_custom_call" | custom-call | tf_op jit(solution)/shard_map/finish_kernel/pallas_call | solution.py:24
  (2 shorter events, 0.0 us)
Async XLA Ops:
  1.7 4.8 %collective-permute-start = (bf16[8,16,1024]{2,1,0:T(8,128)(2,1)S(1)}, bf16[8,16,1024]{2,1,0:T(8,128)(2,1)S(1)}, u32[]{:S(2)}, u32[]{:S(2)}) collective-permute-start(bf16[8,16,1024]{2,1,0:T(8,128)(2,1)S(1)} %get-tuple-element.27.both_ref.refs_0_), channel_id=1, source_target_pairs={{0,1},{1,0},{2,3},{3,2},{4,5},{5,4},{6,7},{7,6},{8,9},{9,8},{10,11... | collective-permute-start | bytes 786440 | tf_op jit(solution)/shard_map/both_core/ppermute | solution.py:356
  2.3 6.1 %collective-permute-start.1 = (bf16[128,128]{1,0:T(8,128)(2,1)S(1)}, bf16[128,128]{1,0:T(8,128)(2,1)S(1)}, u32[]{:S(2)}, u32[]{:S(2)}) collective-permute-start(bf16[128,128]{1,0:T(8,128)(2,1)S(1)} %get-tuple-element.30), channel_id=1, source_target_pairs={{0,4},{1,5},{2,6},{3,7},{4,0},{5,1},{6,2},{7,3},{8,12},{9,13},{10,... | collective-permute-start | bytes 98312 | tf_op jit(solution)/shard_map/plane_first/ppermute | solution.py:379
  4.8 3.5 %collective-permute-start.2 = (bf16[128,128]{1,0:T(8,128)(2,1)S(1)}, bf16[128,128]{1,0:T(8,128)(2,1)S(1)}, u32[]{:S(2)}, u32[]{:S(2)}) collective-permute-start(bf16[128,128]{1,0:T(8,128)(2,1)S(1)} %get-tuple-element.31), channel_id=1, source_target_pairs={{0,1},{1,0},{2,3},{3,2},{4,8},{5,9},{6,10},{7,11},{8,4},{9,5},{10,... | collective-permute-start | bytes 98312 | tf_op jit(solution)/shard_map/plane_second/ppermute | solution.py:379
  5.0 6.0 %collective-permute-start.3 = (bf16[8,16,512]{2,1,0:T(8,128)(2,1)}, bf16[8,16,512]{2,1,0:T(8,128)(2,1)S(1)}, u32[]{:S(2)}, u32[]{:S(2)}) collective-permute-start(bf16[8,16,512]{2,1,0:T(8,128)(2,1)} %feat_any.1), channel_id=1, source_target_pairs={{0,2},{1,3},{2,0},{3,1},{4,6},{5,7},{6,4},{7,5},{8,10},{9,11},{10,... | collective-permute-start | bytes 393224 | tf_op jit(solution)/shard_map/feat_y/ppermute | solution.py:356
  8.6 7.8 %collective-permute-start.8 = (bf16[128,896]{1,0:T(8,128)(2,1)S(1)}, bf16[128,896]{1,0:T(8,128)(2,1)S(1)}, u32[]{:S(2)}, u32[]{:S(2)}) collective-permute-start(bf16[128,896]{1,0:T(8,128)(2,1)S(1)} %get-tuple-element.39), channel_id=1, source_target_pairs={{0,2},{1,3},{2,0},{3,1},{4,6},{5,7},{6,4},{7,5},{8,10},{9,11},{10,... | collective-permute-start | bytes 688136 | tf_op jit(solution)/shard_map/pack_y/ppermute | solution.py:356
  10.9 1.3 %collective-permute-start.4 = (bf16[8,16,512]{2,1,0:T(8,128)(2,1)S(1)}, bf16[8,16,512]{2,1,0:T(8,128)(2,1)S(1)}, u32[]{:S(2)}, u32[]{:S(2)}) collective-permute-start(bf16[8,16,512]{2,1,0:T(8,128)(2,1)S(1)} %collective-permute-done.3.feat2_ref.refs_2_), channel_id=1, source_target_pairs={{0,1},{1,0},{2,3},{3,2},{4,5},{5,4},{6,7},{7,6},{8,9},{9,8},{10,11... | collective-permute-start | bytes 393224 | tf_op jit(solution)/shard_map/feat_far/ppermute | solution.py:356
  13.9 5.9 %collective-permute-start.5 = (f32[224,128]{1,0:T(8,128)S(1)}, f32[224,128]{1,0:T(8,128)S(1)}, u32[]{:S(2)}, u32[]{:S(2)}) collective-permute-start(f32[224,128]{1,0:T(8,128)S(1)} %far_grad_kernel.1), channel_id=1, source_target_pairs={{0,4},{4,0},{8,12},{12,8},{16,20},{20,16},{24,28},{28,24},{1,5},{5... | collective-permute-start | bytes 344072 | tf_op jit(solution)/shard_map/sum_first/ppermute | solution.py:356
  16.4 6.4 %collective-permute-start.9 = (bf16[128,896]{1,0:T(8,128)(2,1)S(1)}, bf16[128,896]{1,0:T(8,128)(2,1)S(1)}, u32[]{:S(2)}, u32[]{:S(2)}) collective-permute-start(bf16[128,896]{1,0:T(8,128)(2,1)S(1)} %collective-permute-done.8.refs_6_.refs_2_), channel_id=1, source_target_pairs={{0,1},{1,0},{2,3},{3,2},{4,5},{5,4},{6,7},{7,6},{8,9},{9,8},{10,11... | collective-permute-start | bytes 688136 | tf_op jit(solution)/shard_map/pack_far/ppermute | solution.py:356
  19.8 5.3 %collective-permute-start.6 = (f32[224,128]{1,0:T(8,128)S(1)}, f32[224,128]{1,0:T(8,128)S(1)}, u32[]{:S(2)}, u32[]{:S(2)}) collective-permute-start(f32[224,128]{1,0:T(8,128)S(1)} %add.6), channel_id=1, source_target_pairs={{0,8},{4,12},{8,0},{12,4},{16,24},{20,28},{24,16},{28,20},{1,9},{5... | collective-permute-start | bytes 344072 | tf_op jit(solution)/shard_map/sum_next/ppermute | solution.py:356
  21.5 1.3 %collective-permute-start.7 = (bf16[128,384]{1,0:T(8,128)(2,1)S(1)}, bf16[128,384]{1,0:T(8,128)(2,1)S(1)}, u32[]{:S(2)}, u32[]{:S(2)}) collective-permute-start(bf16[128,384]{1,0:T(8,128)(2,1)S(1)} %get-tuple-element.35.packed_ref.refs_4_.refs_0_), channel_id=1, source_target_pairs={{0,1},{1,0},{2,3},{3,2},{4,5},{5,4},{6,7},{7,6},{8,9},{9,8},{10,11... | collective-permute-start | bytes 294920 | tf_op jit(solution)/shard_map/pack_core/ppermute | solution.py:356
  25.2 9.6 %collective-permute-start.10 = (f32[224,128]{1,0:T(8,128)S(1)}, f32[224,128]{1,0:T(8,128)S(1)}, u32[]{:S(2)}, u32[]{:S(2)}) collective-permute-start(f32[224,128]{1,0:T(8,128)S(1)} %add.7.one_ref), channel_id=1, source_target_pairs={{0,16},{4,20},{8,24},{12,28},{16,0},{20,4},{24,8},{28,12},{1,17},{... | collective-permute-start | bytes 344072 | tf_op jit(solution)/shard_map/sum_last/ppermute | solution.py:356

commit v3 on v2

--- a/solution.py
+++ b/solution.py
@@ -11,7 +11,7 @@
 VMEM = pl.BlockSpec(memory_space=pltpu.VMEM)
 HBM = pl.BlockSpec(memory_space=pltpu.HBM)
 
-COSTS = {}
+COSTS = {"pack_kernel": 2_000_000_000}
 GROUPS = ((0, 8), (8, 14), (14, 22), (22, 27))
 
 
@@ -19,14 +19,14 @@
     return lax.broadcasted_iota(i32, shape, axis)
 
 
-def call(kernel, out_shape, scratch, *args, specs):
+def call(kernel, out_shape, scratch, *args, specs, out_spec=VMEM):
     name = getattr(kernel, "func", kernel).__name__
     return pl.pallas_call(
         kernel,
         name=name,
         out_shape=out_shape,
         in_specs=specs,
-        out_specs=jax.tree.map(lambda _: VMEM, out_shape),
+        out_specs=jax.tree.map(lambda _: out_spec, out_shape),
         scratch_shapes=scratch,
         compiler_params=pltpu.CompilerParams(vmem_limit_bytes=48 << 20),
         cost_estimate=pl.CostEstimate(flops=COSTS.get(name, 0), bytes_accessed=0, transcendentals=0),
@@ -64,7 +64,7 @@
         copy.wait()
 
 
-def pack_kernel(both_ref, weight_ref, first_ref, second_ref, near_pack_ref, far_pack_ref):
+def pack_kernel(second_ref, first_ref, weight_ref, near_pack_ref, far_pack_ref):
     rows = first_ref.shape[0]
     even = jnp.full((rows, 128), lax.axis_index("space") % 2, i32) == 0
     first, second = first_ref[...].astype(f32), second_ref[...].astype(f32)
@@ -86,7 +86,6 @@
         owned = spots == 64 * (lanes // 32) + 32 * pair + lanes % 32
         part = jnp.dot(kernel, owned.astype(f32).astype(bf16), preferred_element_type=f32)
         target[:, 256:384] = part.astype(bf16)
-    far_pack_ref[:, 384:896] = both_ref[:, :, 512:1024].reshape(rows, 512)
 
 
 def tap_sums(products, count, bricks):
@@ -253,20 +252,25 @@
                         padded[pl.ds(80 * (10 * x_pairs[0][0] + y_pairs[0][0]) + 8 * z_to + r, 1), :] = piece
 
 
-def inner_kernel(near_ref, weight_ref, *refs):
-    both, both1, feat2, feat3 = refs[:4]
-    packs, (grid_ref, mat_ref, flat, padded, near, sem) = refs[4:8], refs[8:]
+def inner_kernel(near_ref, *refs):
+    (both, both1), feats, cots, (grid_ref, flat, padded, near, sem) = refs[:2], refs[2:4], refs[4:6], refs[6:]
     copy = pltpu.make_async_copy(near_ref, near, sem)
     copy.start()
-    bricks = feat2.shape[0]
-    feats = [both.at[:, :, 0:512], both1.at[:, :, 0:512], feat2, feat3]
-    cots = [both.at[:, :, 512:1024], both1.at[:, :, 512:1024]]
+    bricks = near_ref.shape[0]
+    feats = [both.at[:, :, 0:512], both1.at[:, :, 0:512], *feats]
+    cots = [both.at[:, :, 512:1024], both1.at[:, :, 512:1024], *cots]
     for s in range(bricks):
-        rows = slice(16 * s, 16 * s + 16)
-        views = [view[s] for view in feats + cots] + [pack[rows, 384:896] for pack in packs[2:]]
-        flat[512 * s : 512 * s + 512] = jnp.transpose(jnp.concatenate(views, axis=0).astype(f32))
+        pair = jnp.concatenate([view[s] for view in feats + cots], axis=0)
+        flat[512 * s : 512 * s + 512] = jnp.transpose(pair.astype(f32))
     flat[512 * bricks : 512 * bricks + 512] = jnp.zeros((512, 128), f32)
-
+    copy.wait()
+    pad_bricks(near, padded, flat, 512, [(1, 0, [(x, x) for x in range(8)])])
+    for x in range(8):
+        grid_ref[800 * x : 800 * x + 800] = padded[800 * x : 800 * x + 800].astype(bf16)
+
+
+def matrix_kernel(weight_ref, *refs):
+    packs, mat_ref = refs[:4], refs[4]
     chan = lax.axis_index("chan")
     lanes = iota((48, 128), 1)
     spots = iota((48, 128), 0)
@@ -292,11 +296,6 @@
             total = term if total is None else total + term
         mat_ref[128 * spot + 64 : 128 * spot + 128] = total.astype(bf16)
 
-    copy.wait()
-    pad_bricks(near, padded, flat, 512, [(1, 0, [(x, x) for x in range(8)])])
-    for x in range(8):
-        grid_ref[800 * x : 800 * x + 800] = padded[800 * x : 800 * x + 800].astype(bf16)
-
 
 def conv_layer(views, mat_ref):
     pieces = [view[80 * b : 80 * b + 640, :] for view in views for b in range(3)]
@@ -306,16 +305,13 @@
 
 
 def middle_kernel(grid_ref, mat_ref, done_ref):
-    def layer(x, carry):
-        views = [grid_ref.at[pl.ds(pl.multiple_of(800 * (x + a), 16), 800)] for a in range(3)]
-        done_ref[pl.ds(pl.multiple_of(512 * x, 512), 512), :] = conv_layer(views, mat_ref)
-        return carry
-
-    lax.fori_loop(0, 6, layer, 0)
+    for x in range(6):
+        views = [grid_ref.at[800 * (x + a) : 800 * (x + a) + 800] for a in range(3)]
+        done_ref[512 * x : 512 * x + 512] = conv_layer(views, mat_ref)
 
 
 def outer_kernel(near_ref, grid_ref, mat_ref, middle_ref, *refs):
-    packs, (out_ref, grad_ref, planes, padded, edges, low, high, near, sem) = refs[:4], refs[4:]
+    packs, (out_any, grad_any, out, grad, planes, padded, edges, low, high, near, sem, sems) = refs[:4], refs[4:]
     copy = pltpu.make_async_copy(near_ref, near, sem)
     copy.start()
     bricks = near_ref.shape[0]
@@ -333,8 +329,13 @@
     for r in range(bricks):
         views = [low[pl.ds(r, 64, 8), :], middle_ref[pl.ds(r, 384, 8), :], high[pl.ds(r, 64, 8), :]]
         turned = jnp.transpose(jnp.concatenate(views, axis=0))
-        out_ref[r] = turned[0:16].astype(bf16)
-        grad_ref[r] = turned[16:32].astype(bf16)
+        out[r] = turned[0:16].astype(bf16)
+        grad[r] = turned[16:32].astype(bf16)
+        pltpu.make_async_copy(out.at[r], out_any.at[r], sems.at[0, r]).start()
+        pltpu.make_async_copy(grad.at[r], grad_any.at[r], sems.at[1, r]).start()
+    for r in range(bricks):
+        pltpu.make_async_copy(out.at[r], out_any.at[r], sems.at[0, r]).wait()
+        pltpu.make_async_copy(grad.at[r], grad_any.at[r], sems.at[1, r]).wait()
 
 
 def finish_kernel(one_ref, other_ref, grad_ref):
@@ -378,12 +379,13 @@
         pairs = [(i * wide + c, place(i, c)) for i in range(length) for c in range(wide)]
         return lax.ppermute(value, ("space", "chan"), pairs)
 
+    with jax.named_scope("plane_second"):
+        second = meet(second, 1)
     with jax.named_scope("plane_first"):
         first = meet(first, 0)
-    with jax.named_scope("plane_second"):
-        second = meet(second, 1)
     both1 = across("both_core", both, 1)
     feat2 = across("feat_y", features, 2)
+    cot2 = across("cot_y", cotangent, 2)
     windows, sums = call(
         near_grad_kernel,
         (shape((14, 512, 256), bf16), shape((4, 32, 128), f32)),
@@ -391,15 +393,16 @@
         near, both, both1,
         specs=[VMEM] * 3,
     )
-    first, second, sums = lax.optimization_barrier((first, second, sums))
+    second, first, sums = lax.optimization_barrier((second, first, sums))
     near_pack, far_pack = call(
         pack_kernel,
-        (shape((rows, 384), bf16), shape((rows, 896), bf16)),
+        (shape((rows, 384), bf16), shape((rows, 384), bf16)),
         [],
-        both, own, first, second,
-        specs=[VMEM] * 4,
-    )
-    far_pack2 = across("pack_y", far_pack, 2)
+        second, first, own,
+        specs=[VMEM] * 3,
+    )
+    feat2, windows = lax.optimization_barrier((feat2, windows))
+    feat3 = across("feat_far", feat2, 1)
     edge_windows, sums = call(
         halo_grad_kernel,
         (shape((2, 64, 1152), bf16), shape((4, 32, 128), f32)),
@@ -407,7 +410,6 @@
         near, near_pack, both, both1, sums,
         specs=[VMEM] * 5,
     )
-    feat3 = across("feat_far", feat2, 1)
     part = call(
         functools.partial(far_grad_kernel, float(bricks * length * 512) ** -0.5),
         shape((224, 128), f32),
@@ -421,25 +423,36 @@
         steps.append(step)
         step *= 2
     other = across("sum_first", part, steps[0], "space")
+    cot2, far_pack, part = lax.optimization_barrier((cot2, far_pack, part))
+    cot3 = across("cot_far", cot2, 1)
+    far_pack2 = across("pack_y", far_pack, 2)
     near_pack1 = across("pack_core", near_pack, 1)
     far_pack3 = across("pack_far", far_pack2, 1)
-    grid, matrix = call(
+    grid = call(
         inner_kernel,
-        (shape((6400, 128), bf16), shape((1152, 128), bf16)),
+        shape((6400, 128), bf16),
         [
             pltpu.VMEM(((bricks + 1) * 512, 128), f32),
             pltpu.VMEM((6400, 128), f32),
             pltpu.SMEM(neighbours.shape, i32),
             pltpu.SemaphoreType.DMA,
         ],
-        near, own, both, both1, feat2, feat3, near_pack, near_pack1, far_pack2, far_pack3,
-        specs=[VMEM] * 10,
+        near, both, both1, feat2, feat3, cot2, cot3,
+        specs=[VMEM] * 7,
+    )
+    other, grid = lax.optimization_barrier((other, grid))
+    matrix = call(
+        matrix_kernel,
+        shape((1152, 128), bf16),
+        [],
+        own, near_pack, near_pack1, far_pack2, far_pack3,
+        specs=[VMEM] * 5,
     )
     for step in steps[1:]:
         part = part + other
         if step < steps[-1]:
             other = across("sum_next", part, step, "space")
-            other, grid = lax.optimization_barrier((other, grid))
+            other, matrix = lax.optimization_barrier((other, matrix))
         else:
             other = across("sum_last", part, step, "space")
     middle = call(middle_kernel, shape((3072, 128), f32), [], grid, matrix, specs=[VMEM, VMEM])
@@ -447,6 +460,8 @@
         outer_kernel,
         (shape(features.shape, bf16), shape(features.shape, bf16)),
         [
+            pltpu.VMEM(features.shape, bf16),
+            pltpu.VMEM(features.shape, bf16),
             pltpu.VMEM(((bricks + 1) * 128, 128), f32),
             pltpu.VMEM((1600, 128), f32),
             pltpu.VMEM((1600, 128), bf16),
@@ -454,9 +469,11 @@
             pltpu.VMEM((512, 128), f32),
             pltpu.SMEM(neighbours.shape, i32),
             pltpu.SemaphoreType.DMA,
+            pltpu.SemaphoreType.DMA((2, bricks)),
         ],
         near, grid, matrix, middle, near_pack, near_pack1, far_pack2, far_pack3,
         specs=[VMEM] * 8,
+        out_spec=HBM,
     )
     other, output, grad_input = lax.optimization_barrier((other, output, grad_input))
     grad_weight = call(finish_kernel, shape(weight.shape, f32), [], part, other, specs=[VMEM, VMEM])

time: 35.7 us -> 33 us (0.924)
  waiting for transfers between devices: 7 us -> 3.2 us
  starting transfers between devices: 12 us -> 14.5 us
  Pallas kernels: 15.8 us -> 14.4 us
    ppermute x9 -> x11, waiting for transfers between devices: 6.99 us -> 3.2 us  [across(): lax.ppermute(value, axis, [(i, i ^ apart) for i in range(lax.axis_size(ax...]
    ppermute x9 -> x11, starting transfers between devices: 9.22 us -> 11.4 us  [across(): lax.ppermute(value, axis, [(i, i ^ apart) for i in range(lax.axis_size(ax...]
    pallas_call x9 -> x10, Pallas kernels: 15.8 us -> 14.4 us  [call(): pl.pallas_call(kernel, name=name, out_shape=out_shape, in_specs=specs, ou...]
  transfers between devices with their start and end apart: 11 -> 13, of which waited for: 4 -> 5; matrix products, arithmetic and copies ran while one was open for 0% -> 0% of each run, Pallas kernels for 39% -> 38%
where the time goes in v3:
time: 33 us; the launch traced here: 32.8 us
  starting transfers between devices  14.5 us (44%)
  Pallas kernels  14.4 us (44%)
  waiting for transfers between devices  3.2 us (10%)
  between operations  0.76 us (2%)
    pallas_call x10, Pallas kernels, call(): pl.pallas_call(kernel, name=name, out_shape=out_shape, in_specs=specs, ou...  14.4 us
    ppermute x11, starting transfers between devices, across(): lax.ppermute(value, axis, [(i, i ^ apart) for i in range(lax.axis_size(ax...  11.4 us
    ppermute x11, waiting for transfers between devices, across(): lax.ppermute(value, axis, [(i, i ^ apart) for i in range(lax.axis_size(ax...  3.2 us
    ppermute x2, starting transfers between devices, meet(): return lax.ppermute(value, ('space', 'chan'), pairs)  3.04 us
  transfers between devices with their start and end apart: 13, of which 5 were waited for; matrix products, arithmetic and copies ran while one was open for 0% of the time, Pallas kernels for 38%

profile of v3, /device:TPU:0, one launch (start us, length us, event | category | flops | bytes accessed | tf_op | source)
XLA Modules:
  0.0 32.8 jit_solution(14995442352217666151)
XLA Ops:
  0.6 1.1 %prepare_kernel.1 = (bf16[8,16,1024]{2,1,0:T(8,128)(2,1)S(1)}, bf16[27,16,64]{2,1,0:T(8,128)(2,1)S(1)}, s32[8,27]{1,0:T(8,128)S(1)}, bf16[128,128]{1,0:T(8,128)(2,1)S(1)}, bf16[128,128]{1,0:T(8,128)(2,1)S(1)}) custom-call(bf16[8,16,512]{2,1,0:T(8,128)(2,1)} %feat_any.1, bf16[8,16,512]{2,1,0:T(8,128)(2,1)} %cot_any.1, bf16[27,16,64]{2,1,0:T(8,128)(2,1)} %weight_any.1, ...), custom_call_target="tpu_custom_call" | custom-call | tf_op jit(solution)/shard_map/prepare_kernel/pallas_call | solution.py:24
  1.7 0.5 %collective-permute-start.3 = (bf16[8,16,1024]{2,1,0:T(8,128)(2,1)S(1)}, bf16[8,16,1024]{2,1,0:T(8,128)(2,1)S(1)}, u32[]{:S(2)}, u32[]{:S(2)}) collective-permute-start(bf16[8,16,1024]{2,1,0:T(8,128)(2,1)S(1)} %get-tuple-element.34.both_ref.refs_0_), channel_id=1, source_target_pairs={{0,1},{1,0},{2,3},{3,2},{4,5},{5,4},{6,7},{7,6},{8,9},{9,8},{10,11... | collective-permute-start | bytes 786440 | tf_op jit(solution)/shard_map/both_core/ppermute | solution.py:357
  2.3 2.6 %collective-permute-start.4 = (bf16[8,16,512]{2,1,0:T(8,128)(2,1)}, bf16[8,16,512]{2,1,0:T(8,128)(2,1)S(1)}, u32[]{:S(2)}, u32[]{:S(2)}) collective-permute-start(bf16[8,16,512]{2,1,0:T(8,128)(2,1)} %feat_any.1), channel_id=1, source_target_pairs={{0,2},{1,3},{2,0},{3,1},{4,6},{5,7},{6,4},{7,5},{8,10},{9,11},{10,... | collective-permute-start | bytes 393224 | tf_op jit(solution)/shard_map/feat_y/ppermute | solution.py:357
  4.8 0.2 collective-permute-start.1
  5.0 2.9 %collective-permute-start.2 = (bf16[128,128]{1,0:T(8,128)(2,1)S(1)}, bf16[128,128]{1,0:T(8,128)(2,1)S(1)}, u32[]{:S(2)}, u32[]{:S(2)}) collective-permute-start(bf16[128,128]{1,0:T(8,128)(2,1)S(1)} %get-tuple-element.32), channel_id=1, source_target_pairs={{0,4},{1,5},{2,6},{3,7},{4,0},{5,1},{6,2},{7,3},{8,12},{9,13},{10,... | collective-permute-start | bytes 98312 | tf_op jit(solution)/shard_map/plane_first/ppermute | solution.py:380
  7.9 0.5 %collective-permute-start = (bf16[8,16,512]{2,1,0:T(8,128)(2,1)}, bf16[8,16,512]{2,1,0:T(8,128)(2,1)S(1)}, u32[]{:S(2)}, u32[]{:S(2)}) collective-permute-start(bf16[8,16,512]{2,1,0:T(8,128)(2,1)} %cot_any.1), channel_id=1, source_target_pairs={{0,2},{1,3},{2,0},{3,1},{4,6},{5,7},{6,4},{7,5},{8,10},{9,11},{10,... | collective-permute-start | bytes 393224 | tf_op jit(solution)/shard_map/cot_y/ppermute | solution.py:357
  8.4 1.8 %near_grad_kernel.1 = (bf16[14,512,256]{2,1,0:T(8,128)(2,1)S(1)}, f32[4,32,128]{2,1,0:T(8,128)S(1)}) custom-call(s32[8,27]{1,0:T(8,128)S(1)} %get-tuple-element.33.near_ref, bf16[8,16,1024]{2,1,0:T(8,128)(2,1)S(1)} %get-tuple-element.34.both_ref.refs_0_, bf16[8,16,1024]{2,1,0:T(8,128)(2,1)S(1)} %collective-permute-done.3.both1_ref.refs_1_), custom_call_target="tpu_custom_call" | custom-call | tf_op jit(solution)/shard_map/near_grad_kernel/pallas_call | solution.py:24
  10.2 0.0 collective-permute-done.2.first_ref
  10.2 0.0 collective-permute-done.4.feat2_ref.refs_2_
  10.2 0.1 collective-permute-start.5
  10.3 0.2 pack_kernel.1
  10.6 0.9 %halo_grad_kernel.1 = (bf16[2,64,1152]{2,1,0:T(8,128)(2,1)S(1)}, f32[4,32,128]{2,1,0:T(8,128)S(1)}) custom-call(s32[8,27]{1,0:T(8,128)S(1)} %get-tuple-element.33.near_ref, bf16[128,384]{1,0:T(8,128)(2,1)S(1)} %get-tuple-element.42.packed_ref.refs_0_, bf16[8,16,1024]{2,1,0:T(8,128)(2,1)S(1)} %get-tuple-element.34.both_ref.refs_0_, ...), custom_call_target="tpu_custom_call" | custom-call | tf_op jit(solution)/shard_map/halo_grad_kernel/pallas_call | solution.py:24
  11.5 0.2 collective-permute-done.5.feat3_ref.refs_3_
  11.7 1.6 %far_grad_kernel.1 = f32[224,128]{1,0:T(8,128)S(1)} custom-call(bf16[14,512,256]{2,1,0:T(8,128)(2,1)S(1)} %get-tuple-element.41.windows_ref, bf16[2,64,1152]{2,1,0:T(8,128)(2,1)S(1)} %get-tuple-element.44.edge_windows_ref, bf16[8,16,512]{2,1,0:T(8,128)(2,1)S(1)} %collective-permute-done.4.feat2_ref.refs_2_, ...), custom_call_target="tpu_custom_call" | custom-call | tf_op jit(solution)/shard_map/far_grad_kernel/pallas_call | solution.py:24
  13.3 0.0 collective-permute-done.refs_4_
  13.3 0.4 %collective-permute-start.7 = (bf16[8,16,512]{2,1,0:T(8,128)(2,1)S(1)}, bf16[8,16,512]{2,1,0:T(8,128)(2,1)S(1)}, u32[]{:S(2)}, u32[]{:S(2)}) collective-permute-start(bf16[8,16,512]{2,1,0:T(8,128)(2,1)S(1)} %collective-permute-done.refs_4_), channel_id=1, source_target_pairs={{0,1},{1,0},{2,3},{3,2},{4,5},{5,4},{6,7},{7,6},{8,9},{9,8},{10,11... | collective-permute-start | bytes 393224 | tf_op jit(solution)/shard_map/cot_far/ppermute | solution.py:357
  13.6 1.5 %collective-permute-start.6 = (f32[224,128]{1,0:T(8,128)S(1)}, f32[224,128]{1,0:T(8,128)S(1)}, u32[]{:S(2)}, u32[]{:S(2)}) collective-permute-start(f32[224,128]{1,0:T(8,128)S(1)} %far_grad_kernel.1), channel_id=1, source_target_pairs={{0,4},{4,0},{8,12},{12,8},{16,20},{20,16},{24,28},{28,24},{1,5},{5... | collective-permute-start | bytes 344072 | tf_op jit(solution)/shard_map/sum_first/ppermute | solution.py:357
  15.1 1.1 %collective-permute-start.10 = (bf16[128,384]{1,0:T(8,128)(2,1)S(1)}, bf16[128,384]{1,0:T(8,128)(2,1)S(1)}, u32[]{:S(2)}, u32[]{:S(2)}) collective-permute-start(bf16[128,384]{1,0:T(8,128)(2,1)S(1)} %get-tuple-element.50), channel_id=1, source_target_pairs={{0,2},{1,3},{2,0},{3,1},{4,6},{5,7},{6,4},{7,5},{8,10},{9,11},{10,... | collective-permute-start | bytes 294920 | tf_op jit(solution)/shard_map/pack_y/ppermute | solution.py:357
  16.2 0.0 collective-permute-done.7.refs_5_
  16.2 1.9 %inner_kernel.1.grid_ref = bf16[6400,128]{1,0:T(8,128)(2,1)S(1)} custom-call(s32[8,27]{1,0:T(8,128)S(1)} %get-tuple-element.33.near_ref, bf16[8,16,1024]{2,1,0:T(8,128)(2,1)S(1)} %get-tuple-element.34.both_ref.refs_0_, bf16[8,16,1024]{2,1,0:T(8,128)(2,1)S(1)} %collective-permute-done.3.both1_ref.refs_1_, ...), custom_call_target="tpu_custom_call" | custom-call | tf_op jit(solution)/shard_map/inner_kernel/pallas_call | solution.py:24
  18.2 0.7 %collective-permute-done.6 = f32[224,128]{1,0:T(8,128)S(1)} collective-permute-done((f32[224,128]{1,0:T(8,128)S(1)}, f32[224,128]{1,0:T(8,128)S(1)}, u32[]{:S(2)}, u32[]{:S(2)}) %collective-permute-start.6) | collective-permute-done | bytes 114720 | tf_op jit(solution)/shard_map/sum_first/ppermute | solution.py:357
  18.9 1.6 %collective-permute-start.8 = (f32[224,128]{1,0:T(8,128)S(1)}, f32[224,128]{1,0:T(8,128)S(1)}, u32[]{:S(2)}, u32[]{:S(2)}) collective-permute-start(f32[224,128]{1,0:T(8,128)S(1)} %add.6), channel_id=1, source_target_pairs={{0,8},{4,12},{8,0},{12,4},{16,24},{20,28},{24,16},{28,20},{1,9},{5... | collective-permute-start | bytes 344072 | tf_op jit(solution)/shard_map/sum_next/ppermute | solution.py:357
  20.6 0.0 collective-permute-start.9
  20.6 0.5 %collective-permute-start.11 = (bf16[128,384]{1,0:T(8,128)(2,1)S(1)}, bf16[128,384]{1,0:T(8,128)(2,1)S(1)}, u32[]{:S(2)}, u32[]{:S(2)}) collective-permute-start(bf16[128,384]{1,0:T(8,128)(2,1)S(1)} %collective-permute-done.10.refs_2_), channel_id=1, source_target_pairs={{0,1},{1,0},{2,3},{3,2},{4,5},{5,4},{6,7},{7,6},{8,9},{9,8},{10,11... | collective-permute-start | bytes 294920 | tf_op jit(solution)/shard_map/pack_far/ppermute | solution.py:357
  21.1 0.8 %collective-permute-done.9.refs_1_ = bf16[128,384]{1,0:T(8,128)(2,1)S(1)} collective-permute-done((bf16[128,384]{1,0:T(8,128)(2,1)S(1)}, bf16[128,384]{1,0:T(8,128)(2,1)S(1)}, u32[]{:S(2)}, u32[]{:S(2)}) %collective-permute-start.9) | collective-permute-done | bytes 98336 | tf_op jit(solution)/shard_map/pack_core/ppermute | solution.py:357
  21.9 0.2 collective-permute-done.11.refs_3_
  22.0 0.4 %matrix_kernel.1.mat_ref = bf16[1152,128]{1,0:T(8,128)(2,1)S(1)} custom-call(bf16[27,16,64]{2,1,0:T(8,128)(2,1)S(1)} %get-tuple-element.38.weight_ref, bf16[128,384]{1,0:T(8,128)(2,1)S(1)} %get-tuple-element.42.packed_ref.refs_0_, bf16[128,384]{1,0:T(8,128)(2,1)S(1)} %collective-permute-done.9.refs_1_, bf16[128,384]{1,0:T(8,128)(2,1)S(1)} %collective-permute-done.10.refs_2_, ...), custom_call_target="tpu_custom_call" | custom-call | tf_op jit(solution)/shard_map/matrix_kernel/pallas_call | solution.py:24
  22.5 1.3 %collective-permute-done.8 = f32[224,128]{1,0:T(8,128)S(1)} collective-permute-done((f32[224,128]{1,0:T(8,128)S(1)}, f32[224,128]{1,0:T(8,128)S(1)}, u32[]{:S(2)}, u32[]{:S(2)}) %collective-permute-start.8) | collective-permute-done | bytes 114720 | tf_op jit(solution)/shard_map/sum_next/ppermute | solution.py:357
  23.8 2.7 %collective-permute-start.12 = (f32[224,128]{1,0:T(8,128)S(1)}, f32[224,128]{1,0:T(8,128)S(1)}, u32[]{:S(2)}, u32[]{:S(2)}) collective-permute-start(f32[224,128]{1,0:T(8,128)S(1)} %add.7.one_ref), channel_id=1, source_target_pairs={{0,16},{4,20},{8,24},{12,28},{16,0},{20,4},{24,8},{28,12},{1,17},{... | collective-permute-start | bytes 344072 | tf_op jit(solution)/shard_map/sum_last/ppermute | solution.py:357
  26.4 2.6 %middle_kernel.1.middle_ref = f32[3072,128]{1,0:T(8,128)S(1)} custom-call(bf16[6400,128]{1,0:T(8,128)(2,1)S(1)} %inner_kernel.1.grid_ref, bf16[1152,128]{1,0:T(8,128)(2,1)S(1)} %matrix_kernel.1.mat_ref), custom_call_target="tpu_custom_call" | custom-call | tf_op jit(solution)/shard_map/middle_kernel/pallas_call | solution.py:24
  29.0 3.0 %outer_kernel.1 = (bf16[8,16,512]{2,1,0:T(8,128)(2,1)}, bf16[8,16,512]{2,1,0:T(8,128)(2,1)}) custom-call(s32[8,27]{1,0:T(8,128)S(1)} %get-tuple-element.33.near_ref, bf16[6400,128]{1,0:T(8,128)(2,1)S(1)} %inner_kernel.1.grid_ref, bf16[1152,128]{1,0:T(8,128)(2,1)S(1)} %matrix_kernel.1.mat_ref, f32[3072,128]{1,0:T(8,128)S(1)} %middle_kernel.1.middle_ref, ...), custom_call_target="tpu_custom_call" | custom-call | tf_op jit(solution)/shard_map/outer_kernel/pallas_call | solution.py:24
  32.1 0.8 %finish_kernel.1 = f32[27,16,64]{2,1,0:T(8,128)} custom-call(f32[224,128]{1,0:T(8,128)S(1)} %add.7.one_ref, f32[224,128]{1,0:T(8,128)S(1)} %collective-permute-done.12.other_ref), custom_call_target="tpu_custom_call" | custom-call | tf_op jit(solution)/shard_map/finish_kernel/pallas_call | solution.py:24
  (6 shorter events, 0.0 us)
Async XLA Ops:
  1.7 6.7 %collective-permute-start.3 = (bf16[8,16,1024]{2,1,0:T(8,128)(2,1)S(1)}, bf16[8,16,1024]{2,1,0:T(8,128)(2,1)S(1)}, u32[]{:S(2)}, u32[]{:S(2)}) collective-permute-start(bf16[8,16,1024]{2,1,0:T(8,128)(2,1)S(1)} %get-tuple-element.34.both_ref.refs_0_), channel_id=1, source_target_pairs={{0,1},{1,0},{2,3},{3,2},{4,5},{5,4},{6,7},{7,6},{8,9},{9,8},{10,11... | collective-permute-start | bytes 786440 | tf_op jit(solution)/shard_map/both_core/ppermute | solution.py:357
  2.3 8.0 %collective-permute-start.4 = (bf16[8,16,512]{2,1,0:T(8,128)(2,1)}, bf16[8,16,512]{2,1,0:T(8,128)(2,1)S(1)}, u32[]{:S(2)}, u32[]{:S(2)}) collective-permute-start(bf16[8,16,512]{2,1,0:T(8,128)(2,1)} %feat_any.1), channel_id=1, source_target_pairs={{0,2},{1,3},{2,0},{3,1},{4,6},{5,7},{6,4},{7,5},{8,10},{9,11},{10,... | collective-permute-start | bytes 393224 | tf_op jit(solution)/shard_map/feat_y/ppermute | solution.py:357
  4.8 5.4 %collective-permute-start.1 = (bf16[128,128]{1,0:T(8,128)(2,1)S(1)}, bf16[128,128]{1,0:T(8,128)(2,1)S(1)}, u32[]{:S(2)}, u32[]{:S(2)}) collective-permute-start(bf16[128,128]{1,0:T(8,128)(2,1)S(1)} %get-tuple-element.31), channel_id=1, source_target_pairs={{0,1},{1,0},{2,3},{3,2},{4,8},{5,9},{6,10},{7,11},{8,4},{9,5},{10,... | collective-permute-start | bytes 98312 | tf_op jit(solution)/shard_map/plane_second/ppermute | solution.py:380
  5.0 5.2 %collective-permute-start.2 = (bf16[128,128]{1,0:T(8,128)(2,1)S(1)}, bf16[128,128]{1,0:T(8,128)(2,1)S(1)}, u32[]{:S(2)}, u32[]{:S(2)}) collective-permute-start(bf16[128,128]{1,0:T(8,128)(2,1)S(1)} %get-tuple-element.32), channel_id=1, source_target_pairs={{0,4},{1,5},{2,6},{3,7},{4,0},{5,1},{6,2},{7,3},{8,12},{9,13},{10,... | collective-permute-start | bytes 98312 | tf_op jit(solution)/shard_map/plane_first/ppermute | solution.py:380
  7.9 5.4 %collective-permute-start = (bf16[8,16,512]{2,1,0:T(8,128)(2,1)}, bf16[8,16,512]{2,1,0:T(8,128)(2,1)S(1)}, u32[]{:S(2)}, u32[]{:S(2)}) collective-permute-start(bf16[8,16,512]{2,1,0:T(8,128)(2,1)} %cot_any.1), channel_id=1, source_target_pairs={{0,2},{1,3},{2,0},{3,1},{4,6},{5,7},{6,4},{7,5},{8,10},{9,11},{10,... | collective-permute-start | bytes 393224 | tf_op jit(solution)/shard_map/cot_y/ppermute | solution.py:357
  10.2 1.4 %collective-permute-start.5 = (bf16[8,16,512]{2,1,0:T(8,128)(2,1)S(1)}, bf16[8,16,512]{2,1,0:T(8,128)(2,1)S(1)}, u32[]{:S(2)}, u32[]{:S(2)}) collective-permute-start(bf16[8,16,512]{2,1,0:T(8,128)(2,1)S(1)} %collective-permute-done.4.feat2_ref.refs_2_), channel_id=1, source_target_pairs={{0,1},{1,0},{2,3},{3,2},{4,5},{5,4},{6,7},{7,6},{8,9},{9,8},{10,11... | collective-permute-start | bytes 393224 | tf_op jit(solution)/shard_map/feat_far/ppermute | solution.py:357
  13.3 2.9 %collective-permute-start.7 = (bf16[8,16,512]{2,1,0:T(8,128)(2,1)S(1)}, bf16[8,16,512]{2,1,0:T(8,128)(2,1)S(1)}, u32[]{:S(2)}, u32[]{:S(2)}) collective-permute-start(bf16[8,16,512]{2,1,0:T(8,128)(2,1)S(1)} %collective-permute-done.refs_4_), channel_id=1, source_target_pairs={{0,1},{1,0},{2,3},{3,2},{4,5},{5,4},{6,7},{7,6},{8,9},{9,8},{10,11... | collective-permute-start | bytes 393224 | tf_op jit(solution)/shard_map/cot_far/ppermute | solution.py:357
  13.6 5.3 %collective-permute-start.6 = (f32[224,128]{1,0:T(8,128)S(1)}, f32[224,128]{1,0:T(8,128)S(1)}, u32[]{:S(2)}, u32[]{:S(2)}) collective-permute-start(f32[224,128]{1,0:T(8,128)S(1)} %far_grad_kernel.1), channel_id=1, source_target_pairs={{0,4},{4,0},{8,12},{12,8},{16,20},{20,16},{24,28},{28,24},{1,5},{5... | collective-permute-start | bytes 344072 | tf_op jit(solution)/shard_map/sum_first/ppermute | solution.py:357
  15.1 5.4 %collective-permute-start.10 = (bf16[128,384]{1,0:T(8,128)(2,1)S(1)}, bf16[128,384]{1,0:T(8,128)(2,1)S(1)}, u32[]{:S(2)}, u32[]{:S(2)}) collective-permute-start(bf16[128,384]{1,0:T(8,128)(2,1)S(1)} %get-tuple-element.50), channel_id=1, source_target_pairs={{0,2},{1,3},{2,0},{3,1},{4,6},{5,7},{6,4},{7,5},{8,10},{9,11},{10,... | collective-permute-start | bytes 294920 | tf_op jit(solution)/shard_map/pack_y/ppermute | solution.py:357
  18.9 4.9 %collective-permute-start.8 = (f32[224,128]{1,0:T(8,128)S(1)}, f32[224,128]{1,0:T(8,128)S(1)}, u32[]{:S(2)}, u32[]{:S(2)}) collective-permute-start(f32[224,128]{1,0:T(8,128)S(1)} %add.6), channel_id=1, source_target_pairs={{0,8},{4,12},{8,0},{12,4},{16,24},{20,28},{24,16},{28,20},{1,9},{5... | collective-permute-start | bytes 344072 | tf_op jit(solution)/shard_map/sum_next/ppermute | solution.py:357
  20.6 1.3 %collective-permute-start.9 = (bf16[128,384]{1,0:T(8,128)(2,1)S(1)}, bf16[128,384]{1,0:T(8,128)(2,1)S(1)}, u32[]{:S(2)}, u32[]{:S(2)}) collective-permute-start(bf16[128,384]{1,0:T(8,128)(2,1)S(1)} %get-tuple-element.42.packed_ref.refs_0_), channel_id=1, source_target_pairs={{0,1},{1,0},{2,3},{3,2},{4,5},{5,4},{6,7},{7,6},{8,9},{9,8},{10,11... | collective-permute-start | bytes 294920 | tf_op jit(solution)/shard_map/pack_core/ppermute | solution.py:357
  20.6 1.5 %collective-permute-start.11 = (bf16[128,384]{1,0:T(8,128)(2,1)S(1)}, bf16[128,384]{1,0:T(8,128)(2,1)S(1)}, u32[]{:S(2)}, u32[]{:S(2)}) collective-permute-start(bf16[128,384]{1,0:T(8,128)(2,1)S(1)} %collective-permute-done.10.refs_2_), channel_id=1, source_target_pairs={{0,1},{1,0},{2,3},{3,2},{4,5},{5,4},{6,7},{7,6},{8,9},{9,8},{10,11... | collective-permute-start | bytes 294920 | tf_op jit(solution)/shard_map/pack_far/ppermute | solution.py:357
  23.8 8.3 %collective-permute-start.12 = (f32[224,128]{1,0:T(8,128)S(1)}, f32[224,128]{1,0:T(8,128)S(1)}, u32[]{:S(2)}, u32[]{:S(2)}) collective-permute-start(f32[224,128]{1,0:T(8,128)S(1)} %add.7.one_ref), channel_id=1, source_target_pairs={{0,16},{4,20},{8,24},{12,28},{16,0},{20,4},{24,8},{28,12},{1,17},{... | collective-permute-start | bytes 344072 | tf_op jit(solution)/shard_map/sum_last/ppermute | solution.py:357

commit v4 on v3

--- a/solution.py
+++ b/solution.py
@@ -12,6 +12,7 @@
 HBM = pl.BlockSpec(memory_space=pltpu.HBM)
 
 COSTS = {"pack_kernel": 2_000_000_000}
+EARLY = 1
 GROUPS = ((0, 8), (8, 14), (14, 22), (22, 27))
 
 
@@ -88,7 +89,7 @@
         target[:, 256:384] = part.astype(bf16)
 
 
-def tap_sums(products, count, bricks):
+def tap_sums(products, count, bricks, absent=()):
     lane_group = iota((16, 128), 1) // 16
     sums = []
     for begin, end in GROUPS:
@@ -99,7 +100,8 @@
                 chosen = None
                 for brick in range(bricks):
                     start = (view * bricks + brick) * 16
-                    block = products[min(begin + (brick + shift) % 8, end - 1), start : start + 16, :]
+                    tap = min(begin + (brick + shift) % 8, end - 1)
+                    block = jnp.zeros((16, 128), f32) if tap in absent else products[tap, start : start + 16, :]
                     chosen = block if chosen is None else jnp.where(lane_group == brick, block, chosen)
                 if shift:
                     chosen = pltpu.roll(chosen, 16 * shift, 1)
@@ -194,9 +196,7 @@
         both = jnp.dot(plane_ends([both_ref, both1_ref], side), window, preferred_element_type=f32)
         for place in range(9):
             products[18 * (1 - side) + place] = both[:, 128 * place : 128 * place + 128]
-    for place in range(9, 18):
-        products[place] = jnp.zeros((2 * rows, 128), f32)
-    sums = tap_sums(products, 2, bricks)
+    sums = tap_sums(products, 2, bricks, range(9, 18))
     for group in range(4):
         total_ref[group] = sums_ref[group] + jnp.concatenate(sums[group], axis=0)
 
@@ -205,24 +205,29 @@
     chan = lax.axis_index("chan")
     bricks = feat2_ref.shape[0]
     rows = bricks * 16
-    views = [feat2_ref, feat3_ref]
-    for side in range(2):
-        both = jnp.dot(plane_ends(views, side), edge_windows_ref[side], preferred_element_type=f32)
-        for place in range(9):
-            products[18 * (1 - side) + place] = both[:, 128 * place : 128 * place + 128]
-    far = jnp.concatenate([view[...].reshape(rows, 512) for view in views], axis=0)
+    far = jnp.concatenate([view[...].reshape(rows, 512) for view in (feat2_ref, feat3_ref)], axis=0)
     for pair in range(14):
-        both = jnp.dot(far, windows_ref[pair], preferred_element_type=f32)
-        for tap in range(2 * pair, min(2 * pair + 2, 27)):
-            one = both[:, 128 * (tap % 2) : 128 * (tap % 2) + 128]
-            products[tap] = one if 9 <= tap < 18 else one + products[tap]
+        halves = []
+        for index, tap in enumerate((2 * pair, min(2 * pair + 1, 26))):
+            half = windows_ref[pair, :, 128 * index : 128 * index + 128]
+            edge = slice(128 * (tap % 9), 128 * (tap % 9) + 128)
+            if tap < 9:
+                half = jnp.concatenate([half[0:448], edge_windows_ref[1, :, edge]], axis=0)
+            elif tap >= 18:
+                half = jnp.concatenate([edge_windows_ref[0, :, edge], half[64:512]], axis=0)
+            halves.append(half)
+        both = jnp.dot(far, jnp.concatenate(halves, axis=1), preferred_element_type=f32)
+        products[2 * pair] = both[:, 0:128]
+        products[2 * pair + 1] = both[:, 128:256]
     sums = tap_sums(products, 2, bricks)
     for group in range(4):
         both = sums_ref[group]
         for apart, block in enumerate((both[0:16], both[16:32], *sums[group])):
             ordered[group, pl.ds(pl.multiple_of(16 * (chan ^ apart), 16), 16), :] = block
-    part_ref[0:128] = jnp.transpose(jnp.concatenate([ordered[0], ordered[2]], axis=0)) * scale
-    part_ref[128:224] = jnp.transpose(jnp.concatenate([ordered[1], ordered[3]], axis=0))[0:96] * scale
+    turned = [jnp.transpose(jnp.concatenate([ordered[i], ordered[i + 2]], axis=0)) * scale for i in range(2)]
+    turned = jnp.concatenate([turned[0], turned[1][0:96]], axis=0)
+    upper = jnp.concatenate([pltpu.roll(turned[216:224], 64, 1), turned[0:208]], axis=0)
+    part_ref[...] = jnp.where(iota((216, 128), 1) < 64, turned[0:216], upper)
 
 
 def pad_bricks(near, padded, source, size, xs):
@@ -304,14 +309,22 @@
     return total.reshape(512, 128)
 
 
-def middle_kernel(grid_ref, mat_ref, done_ref):
-    for x in range(6):
-        views = [grid_ref.at[800 * (x + a) : 800 * (x + a) + 800] for a in range(3)]
-        done_ref[512 * x : 512 * x + 512] = conv_layer(views, mat_ref)
-
-
-def outer_kernel(near_ref, grid_ref, mat_ref, middle_ref, *refs):
-    packs, (out_any, grad_any, out, grad, planes, padded, edges, low, high, near, sem, sems) = refs[:4], refs[4:]
+def layers(grid_ref, mat_ref, done_ref, first, last):
+    for x in range(first, last):
+        views = [grid_ref.at[800 * (x + a - 1) : 800 * (x + a - 1) + 800] for a in range(3)]
+        done_ref[512 * (x - first) : 512 * (x - first) + 512] = conv_layer(views, mat_ref)
+
+
+def early_kernel(grid_ref, mat_ref, done_ref):
+    layers(grid_ref, mat_ref, done_ref, 1, 1 + EARLY)
+
+
+def late_kernel(grid_ref, mat_ref, done_ref):
+    layers(grid_ref, mat_ref, done_ref, 1 + EARLY, 7)
+
+
+def outer_kernel(near_ref, grid_ref, mat_ref, early_ref, late_ref, *refs):
+    packs, (out, grad, planes, padded, edges, low, high, near, sem) = refs[:4], refs[4:]
     copy = pltpu.make_async_copy(near_ref, near, sem)
     copy.start()
     bricks = near_ref.shape[0]
@@ -327,23 +340,29 @@
     low[...] = conv_layer(layers[0:3], mat_ref)
     high[...] = conv_layer(layers[3:6], mat_ref)
     for r in range(bricks):
-        views = [low[pl.ds(r, 64, 8), :], middle_ref[pl.ds(r, 384, 8), :], high[pl.ds(r, 64, 8), :]]
+        views = [view[pl.ds(r, view.shape[0] // 8, 8), :] for view in (low, early_ref, late_ref, high)]
         turned = jnp.transpose(jnp.concatenate(views, axis=0))
         out[r] = turned[0:16].astype(bf16)
         grad[r] = turned[16:32].astype(bf16)
-        pltpu.make_async_copy(out.at[r], out_any.at[r], sems.at[0, r]).start()
-        pltpu.make_async_copy(grad.at[r], grad_any.at[r], sems.at[1, r]).start()
-    for r in range(bricks):
-        pltpu.make_async_copy(out.at[r], out_any.at[r], sems.at[0, r]).wait()
-        pltpu.make_async_copy(grad.at[r], grad_any.at[r], sems.at[1, r]).wait()
-
-
-def finish_kernel(one_ref, other_ref, grad_ref):
+
+
+def finish_kernel(out_ref, grad_ref, one_ref, other_ref, out_any, grad_any, kernel_any, kernel_grad, sems):
+    copies = [
+        pltpu.make_async_copy(out_ref, out_any, sems.at[0]),
+        pltpu.make_async_copy(grad_ref, grad_any, sems.at[1]),
+        pltpu.make_async_copy(kernel_grad, kernel_any, sems.at[2]),
+    ]
+    for copy in copies[:2]:
+        copy.start()
     total = one_ref[...] + other_ref[...]
     for tap in range(27):
-        slot = tap % 14
-        block = total[16 * slot : 16 * slot + 16]
-        grad_ref[tap] = block[:, 0:64] if tap < 14 else block[:, 64:128]
+        for begin in (0, 8):
+            row = 16 * tap + begin
+            block = total[row % 216 : row % 216 + 8]
+            kernel_grad[tap, begin : begin + 8] = block[:, 0:64] if row < 216 else block[:, 64:128]
+    copies[2].start()
+    for copy in copies:
+        copy.wait()
 
 
 def body(features, weight, cotangent, neighbours):
@@ -412,8 +431,8 @@
     )
     part = call(
         functools.partial(far_grad_kernel, float(bricks * length * 512) ** -0.5),
-        shape((224, 128), f32),
-        [pltpu.VMEM((27, 2 * rows, 128), f32), pltpu.VMEM((4, 64, 128), f32)],
+        shape((216, 128), f32),
+        [pltpu.VMEM((28, 2 * rows, 128), f32), pltpu.VMEM((4, 64, 128), f32)],
         windows, edge_windows, feat2, feat3, sums,
         specs=[VMEM] * 5,
     )
@@ -448,20 +467,19 @@
         own, near_pack, near_pack1, far_pack2, far_pack3,
         specs=[VMEM] * 5,
     )
+    early = call(early_kernel, shape((512 * EARLY, 128), f32), [], grid, matrix, specs=[VMEM, VMEM])
     for step in steps[1:]:
         part = part + other
         if step < steps[-1]:
             other = across("sum_next", part, step, "space")
-            other, matrix = lax.optimization_barrier((other, matrix))
+            other, early, grid = lax.optimization_barrier((other, early, grid))
         else:
             other = across("sum_last", part, step, "space")
-    middle = call(middle_kernel, shape((3072, 128), f32), [], grid, matrix, specs=[VMEM, VMEM])
+    late = call(late_kernel, shape((512 * (6 - EARLY), 128), f32), [], grid, matrix, specs=[VMEM, VMEM])
     output, grad_input = call(
         outer_kernel,
         (shape(features.shape, bf16), shape(features.shape, bf16)),
         [
-            pltpu.VMEM(features.shape, bf16),
-            pltpu.VMEM(features.shape, bf16),
             pltpu.VMEM(((bricks + 1) * 128, 128), f32),
             pltpu.VMEM((1600, 128), f32),
             pltpu.VMEM((1600, 128), bf16),
@@ -469,15 +487,18 @@
             pltpu.VMEM((512, 128), f32),
             pltpu.SMEM(neighbours.shape, i32),
             pltpu.SemaphoreType.DMA,
-            pltpu.SemaphoreType.DMA((2, bricks)),
         ],
-        near, grid, matrix, middle, near_pack, near_pack1, far_pack2, far_pack3,
-        specs=[VMEM] * 8,
+        near, grid, matrix, early, late, near_pack, near_pack1, far_pack2, far_pack3,
+        specs=[VMEM] * 9,
+    )
+    return call(
+        finish_kernel,
+        (shape(features.shape, bf16), shape(features.shape, bf16), shape(weight.shape, f32)),
+        [pltpu.VMEM(weight.shape, f32), pltpu.SemaphoreType.DMA((3,))],
+        output, grad_input, part, other,
+        specs=[VMEM] * 4,
         out_spec=HBM,
     )
-    other, output, grad_input = lax.optimization_barrier((other, output, grad_input))
-    grad_weight = call(finish_kernel, shape(weight.shape, f32), [], part, other, specs=[VMEM, VMEM])
-    return (output, grad_input, grad_weight)
 
 
 def solution(mesh):

time: 33 us -> 32.4 us (0.982)
  Pallas kernels: 14.4 us -> 13.8 us
    pallas_call x10 -> x11, Pallas kernels: 14.4 us -> 13.8 us  [call(): pl.pallas_call(kernel, name=name, out_shape=out_shape, in_specs=specs, ou...]
  transfers between devices with their start and end apart: 13 -> 13, of which waited for: 5 -> 7; matrix products, arithmetic and copies ran while one was open for 0% -> 0% of each run, Pallas kernels for 38% -> 37%
where the time goes in v4:
time: 32.4 us; the launch traced here: 32.2 us
  starting transfers between devices  14.4 us (44%)
  Pallas kernels  13.8 us (43%)
  waiting for transfers between devices  3.34 us (10%)
  between operations  0.75 us (2%)
    pallas_call x11, Pallas kernels, call(): pl.pallas_call(kernel, name=name, out_shape=out_shape, in_specs=specs, ou...  13.8 us
    ppermute x11, starting transfers between devices, across(): lax.ppermute(value, axis, [(i, i ^ apart) for i in range(lax.axis_size(ax...  11.3 us
    ppermute x11, waiting for transfers between devices, across(): lax.ppermute(value, axis, [(i, i ^ apart) for i in range(lax.axis_size(ax...  3.34 us
    ppermute x2, starting transfers between devices, meet(): return lax.ppermute(value, ('space', 'chan'), pairs)  3.04 us
  transfers between devices with their start and end apart: 13, of which 7 were waited for; matrix products, arithmetic and copies ran while one was open for 0% of the time, Pallas kernels for 37%

profile of v4, /device:TPU:0, one launch (start us, length us, event | category | flops | bytes accessed | tf_op | source)
XLA Modules:
  0.0 32.2 jit_solution(17308253085329126765)
XLA Ops:
  0.6 1.1 %prepare_kernel.1 = (bf16[8,16,1024]{2,1,0:T(8,128)(2,1)S(1)}, bf16[27,16,64]{2,1,0:T(8,128)(2,1)S(1)}, s32[8,27]{1,0:T(8,128)S(1)}, bf16[128,128]{1,0:T(8,128)(2,1)S(1)}, bf16[128,128]{1,0:T(8,128)(2,1)S(1)}) custom-call(bf16[8,16,512]{2,1,0:T(8,128)(2,1)} %feat_any.1, bf16[8,16,512]{2,1,0:T(8,128)(2,1)} %cot_any.1, bf16[27,16,64]{2,1,0:T(8,128)(2,1)} %weight_any.1, ...), custom_call_target="tpu_custom_call" | custom-call | tf_op jit(solution)/shard_map/prepare_kernel/pallas_call | solution.py:25
  1.7 0.5 %collective-permute-start.3 = (bf16[8,16,1024]{2,1,0:T(8,128)(2,1)S(1)}, bf16[8,16,1024]{2,1,0:T(8,128)(2,1)S(1)}, u32[]{:S(2)}, u32[]{:S(2)}) collective-permute-start(bf16[8,16,1024]{2,1,0:T(8,128)(2,1)S(1)} %get-tuple-element.32.both_ref.refs_0_), channel_id=1, source_target_pairs={{0,1},{1,0},{2,3},{3,2},{4,5},{5,4},{6,7},{7,6},{8,9},{9,8},{10,11... | collective-permute-start | bytes 786440 | tf_op jit(solution)/shard_map/both_core/ppermute | solution.py:376
  2.3 2.6 %collective-permute-start.4 = (bf16[8,16,512]{2,1,0:T(8,128)(2,1)}, bf16[8,16,512]{2,1,0:T(8,128)(2,1)S(1)}, u32[]{:S(2)}, u32[]{:S(2)}) collective-permute-start(bf16[8,16,512]{2,1,0:T(8,128)(2,1)} %feat_any.1), channel_id=1, source_target_pairs={{0,2},{1,3},{2,0},{3,1},{4,6},{5,7},{6,4},{7,5},{8,10},{9,11},{10,... | collective-permute-start | bytes 393224 | tf_op jit(solution)/shard_map/feat_y/ppermute | solution.py:376
  4.8 0.2 collective-permute-start.1
  5.0 2.9 %collective-permute-start.2 = (bf16[128,128]{1,0:T(8,128)(2,1)S(1)}, bf16[128,128]{1,0:T(8,128)(2,1)S(1)}, u32[]{:S(2)}, u32[]{:S(2)}) collective-permute-start(bf16[128,128]{1,0:T(8,128)(2,1)S(1)} %get-tuple-element.31), channel_id=1, source_target_pairs={{0,4},{1,5},{2,6},{3,7},{4,0},{5,1},{6,2},{7,3},{8,12},{9,13},{10,... | collective-permute-start | bytes 98312 | tf_op jit(solution)/shard_map/plane_first/ppermute | solution.py:399
  7.9 0.5 %collective-permute-start = (bf16[8,16,512]{2,1,0:T(8,128)(2,1)}, bf16[8,16,512]{2,1,0:T(8,128)(2,1)S(1)}, u32[]{:S(2)}, u32[]{:S(2)}) collective-permute-start(bf16[8,16,512]{2,1,0:T(8,128)(2,1)} %cot_any.1), channel_id=1, source_target_pairs={{0,2},{1,3},{2,0},{3,1},{4,6},{5,7},{6,4},{7,5},{8,10},{9,11},{10,... | collective-permute-start | bytes 393224 | tf_op jit(solution)/shard_map/cot_y/ppermute | solution.py:376
  8.4 1.8 %near_grad_kernel.1 = (bf16[14,512,256]{2,1,0:T(8,128)(2,1)S(1)}, f32[4,32,128]{2,1,0:T(8,128)S(1)}) custom-call(s32[8,27]{1,0:T(8,128)S(1)} %get-tuple-element.29.near_ref, bf16[8,16,1024]{2,1,0:T(8,128)(2,1)S(1)} %get-tuple-element.32.both_ref.refs_0_, bf16[8,16,1024]{2,1,0:T(8,128)(2,1)S(1)} %collective-permute-done.3.both1_ref.refs_1_), custom_call_target="tpu_custom_call" | custom-call | tf_op jit(solution)/shard_map/near_grad_kernel/pallas_call | solution.py:25
  10.2 0.0 collective-permute-done.1.second_ref
  10.2 0.0 collective-permute-done.2.first_ref
  10.2 0.1 collective-permute-start.5
  10.3 0.2 pack_kernel.1
  10.6 0.9 %halo_grad_kernel.1 = (bf16[2,64,1152]{2,1,0:T(8,128)(2,1)S(1)}, f32[4,32,128]{2,1,0:T(8,128)S(1)}) custom-call(s32[8,27]{1,0:T(8,128)S(1)} %get-tuple-element.29.near_ref, bf16[128,384]{1,0:T(8,128)(2,1)S(1)} %get-tuple-element.40.packed_ref.refs_0_, bf16[8,16,1024]{2,1,0:T(8,128)(2,1)S(1)} %get-tuple-element.32.both_ref.refs_0_, ...), custom_call_target="tpu_custom_call" | custom-call | tf_op jit(solution)/shard_map/halo_grad_kernel/pallas_call | solution.py:25
  11.5 0.2 collective-permute-done.5.feat3_ref.refs_3_
  11.7 1.4 %far_grad_kernel.1 = f32[216,128]{1,0:T(8,128)S(1)} custom-call(bf16[14,512,256]{2,1,0:T(8,128)(2,1)S(1)} %get-tuple-element.39.windows_ref, bf16[2,64,1152]{2,1,0:T(8,128)(2,1)S(1)} %get-tuple-element.42.edge_windows_ref, bf16[8,16,512]{2,1,0:T(8,128)(2,1)S(1)} %collective-permute-done.4.feat2_ref.refs_2_, ...), custom_call_target="tpu_custom_call" | custom-call | tf_op jit(solution)/shard_map/far_grad_kernel/pallas_call | solution.py:25
  13.0 0.1 collective-permute-done.refs_4_
  13.1 0.3 collective-permute-start.7
  13.4 1.5 %collective-permute-start.6 = (f32[216,128]{1,0:T(8,128)S(1)}, f32[216,128]{1,0:T(8,128)S(1)}, u32[]{:S(2)}, u32[]{:S(2)}) collective-permute-start(f32[216,128]{1,0:T(8,128)S(1)} %far_grad_kernel.1), channel_id=1, source_target_pairs={{0,4},{4,0},{8,12},{12,8},{16,20},{20,16},{24,28},{28,24},{1,5},{5... | collective-permute-start | bytes 331784 | tf_op jit(solution)/shard_map/sum_first/ppermute | solution.py:376
  14.9 1.1 %collective-permute-start.10 = (bf16[128,384]{1,0:T(8,128)(2,1)S(1)}, bf16[128,384]{1,0:T(8,128)(2,1)S(1)}, u32[]{:S(2)}, u32[]{:S(2)}) collective-permute-start(bf16[128,384]{1,0:T(8,128)(2,1)S(1)} %get-tuple-element.49), channel_id=1, source_target_pairs={{0,2},{1,3},{2,0},{3,1},{4,6},{5,7},{6,4},{7,5},{8,10},{9,11},{10,... | collective-permute-start | bytes 294920 | tf_op jit(solution)/shard_map/pack_y/ppermute | solution.py:376
  15.9 1.9 %inner_kernel.1.grid_ref = bf16[6400,128]{1,0:T(8,128)(2,1)S(1)} custom-call(s32[8,27]{1,0:T(8,128)S(1)} %get-tuple-element.29.near_ref, bf16[8,16,1024]{2,1,0:T(8,128)(2,1)S(1)} %get-tuple-element.32.both_ref.refs_0_, bf16[8,16,1024]{2,1,0:T(8,128)(2,1)S(1)} %collective-permute-done.3.both1_ref.refs_1_, ...), custom_call_target="tpu_custom_call" | custom-call | tf_op jit(solution)/shard_map/inner_kernel/pallas_call | solution.py:25
  17.9 0.7 %collective-permute-done.6 = f32[216,128]{1,0:T(8,128)S(1)} collective-permute-done((f32[216,128]{1,0:T(8,128)S(1)}, f32[216,128]{1,0:T(8,128)S(1)}, u32[]{:S(2)}, u32[]{:S(2)}) %collective-permute-start.6) | collective-permute-done | bytes 110624 | tf_op jit(solution)/shard_map/sum_first/ppermute | solution.py:376
  18.6 1.6 %collective-permute-start.8 = (f32[216,128]{1,0:T(8,128)S(1)}, f32[216,128]{1,0:T(8,128)S(1)}, u32[]{:S(2)}, u32[]{:S(2)}) collective-permute-start(f32[216,128]{1,0:T(8,128)S(1)} %add.6), channel_id=1, source_target_pairs={{0,8},{4,12},{8,0},{12,4},{16,24},{20,28},{24,16},{28,20},{1,9},{5... | collective-permute-start | bytes 331784 | tf_op jit(solution)/shard_map/sum_next/ppermute | solution.py:376
  20.2 0.5 %collective-permute-start.11 = (bf16[128,384]{1,0:T(8,128)(2,1)S(1)}, bf16[128,384]{1,0:T(8,128)(2,1)S(1)}, u32[]{:S(2)}, u32[]{:S(2)}) collective-permute-start(bf16[128,384]{1,0:T(8,128)(2,1)S(1)} %collective-permute-done.10.refs_2_), channel_id=1, source_target_pairs={{0,1},{1,0},{2,3},{3,2},{4,5},{5,4},{6,7},{7,6},{8,9},{9,8},{10,11... | collective-permute-start | bytes 294920 | tf_op jit(solution)/shard_map/pack_far/ppermute | solution.py:376
  20.8 0.8 %collective-permute-done.9.refs_1_ = bf16[128,384]{1,0:T(8,128)(2,1)S(1)} collective-permute-done((bf16[128,384]{1,0:T(8,128)(2,1)S(1)}, bf16[128,384]{1,0:T(8,128)(2,1)S(1)}, u32[]{:S(2)}, u32[]{:S(2)}) %collective-permute-start.9) | collective-permute-done | bytes 98336 | tf_op jit(solution)/shard_map/pack_core/ppermute | solution.py:376
  21.5 0.2 collective-permute-done.11.refs_3_
  21.7 0.4 %matrix_kernel.1.mat_ref = bf16[1152,128]{1,0:T(8,128)(2,1)S(1)} custom-call(bf16[27,16,64]{2,1,0:T(8,128)(2,1)S(1)} %get-tuple-element.36.weight_ref, bf16[128,384]{1,0:T(8,128)(2,1)S(1)} %get-tuple-element.40.packed_ref.refs_0_, bf16[128,384]{1,0:T(8,128)(2,1)S(1)} %collective-permute-done.9.refs_1_, bf16[128,384]{1,0:T(8,128)(2,1)S(1)} %collective-permute-done.10.refs_2_, ...), custom_call_target="tpu_custom_call" | custom-call | tf_op jit(solution)/shard_map/matrix_kernel/pallas_call | solution.py:25
  22.1 0.7 %early_kernel.1.early_ref = f32[512,128]{1,0:T(8,128)S(1)} custom-call(bf16[6400,128]{1,0:T(8,128)(2,1)S(1)} %inner_kernel.1.grid_ref, bf16[1152,128]{1,0:T(8,128)(2,1)S(1)} %matrix_kernel.1.mat_ref), custom_call_target="tpu_custom_call" | custom-call | tf_op jit(solution)/shard_map/early_kernel/pallas_call | solution.py:25
  22.8 0.6 %collective-permute-done.8 = f32[216,128]{1,0:T(8,128)S(1)} collective-permute-done((f32[216,128]{1,0:T(8,128)S(1)}, f32[216,128]{1,0:T(8,128)S(1)}, u32[]{:S(2)}, u32[]{:S(2)}) %collective-permute-start.8) | collective-permute-done | bytes 110624 | tf_op jit(solution)/shard_map/sum_next/ppermute | solution.py:376
  23.4 2.7 %collective-permute-start.12 = (f32[216,128]{1,0:T(8,128)S(1)}, f32[216,128]{1,0:T(8,128)S(1)}, u32[]{:S(2)}, u32[]{:S(2)}) collective-permute-start(f32[216,128]{1,0:T(8,128)S(1)} %add.7.one_ref), channel_id=1, source_target_pairs={{0,16},{4,20},{8,24},{12,28},{16,0},{20,4},{24,8},{28,12},{1,17},{... | collective-permute-start | bytes 331784 | tf_op jit(solution)/shard_map/sum_last/ppermute | solution.py:376
  26.1 2.2 %late_kernel.1.late_ref = f32[2560,128]{1,0:T(8,128)S(1)} custom-call(bf16[6400,128]{1,0:T(8,128)(2,1)S(1)} %inner_kernel.1.grid_ref, bf16[1152,128]{1,0:T(8,128)(2,1)S(1)} %matrix_kernel.1.mat_ref), custom_call_target="tpu_custom_call" | custom-call | tf_op jit(solution)/shard_map/late_kernel/pallas_call | solution.py:25
  28.3 2.3 %outer_kernel.1 = (bf16[8,16,512]{2,1,0:T(8,128)(2,1)S(1)}, bf16[8,16,512]{2,1,0:T(8,128)(2,1)S(1)}) custom-call(s32[8,27]{1,0:T(8,128)S(1)} %get-tuple-element.29.near_ref, bf16[6400,128]{1,0:T(8,128)(2,1)S(1)} %inner_kernel.1.grid_ref, bf16[1152,128]{1,0:T(8,128)(2,1)S(1)} %matrix_kernel.1.mat_ref, f32[512,128]{1,0:T(8,128)S(1)} %early_kernel.1.early_ref, ...), custom_call_target="tpu_custom_call" | custom-call | tf_op jit(solution)/shard_map/outer_kernel/pallas_call | solution.py:25
  30.6 0.9 %collective-permute-done.12.other_ref = f32[216,128]{1,0:T(8,128)S(1)} collective-permute-done((f32[216,128]{1,0:T(8,128)S(1)}, f32[216,128]{1,0:T(8,128)S(1)}, u32[]{:S(2)}, u32[]{:S(2)}) %collective-permute-start.12) | collective-permute-done | bytes 110624 | tf_op jit(solution)/shard_map/sum_last/ppermute | solution.py:376
  31.4 0.8 %finish_kernel.1 = (bf16[8,16,512]{2,1,0:T(8,128)(2,1)}, bf16[8,16,512]{2,1,0:T(8,128)(2,1)}, f32[27,16,64]{2,1,0:T(8,128)}) custom-call(bf16[8,16,512]{2,1,0:T(8,128)(2,1)S(1)} %get-tuple-element.52.out_ref, bf16[8,16,512]{2,1,0:T(8,128)(2,1)S(1)} %get-tuple-element.53.grad_ref, f32[216,128]{1,0:T(8,128)S(1)} %add.7.one_ref, ...), custom_call_target="tpu_custom_call" | custom-call | tf_op jit(solution)/shard_map/finish_kernel/pallas_call | solution.py:25
  (7 shorter events, 0.0 us)
Async XLA Ops:
  1.7 6.7 %collective-permute-start.3 = (bf16[8,16,1024]{2,1,0:T(8,128)(2,1)S(1)}, bf16[8,16,1024]{2,1,0:T(8,128)(2,1)S(1)}, u32[]{:S(2)}, u32[]{:S(2)}) collective-permute-start(bf16[8,16,1024]{2,1,0:T(8,128)(2,1)S(1)} %get-tuple-element.32.both_ref.refs_0_), channel_id=1, source_target_pairs={{0,1},{1,0},{2,3},{3,2},{4,5},{5,4},{6,7},{7,6},{8,9},{9,8},{10,11... | collective-permute-start | bytes 786440 | tf_op jit(solution)/shard_map/both_core/ppermute | solution.py:376
  2.3 8.0 %collective-permute-start.4 = (bf16[8,16,512]{2,1,0:T(8,128)(2,1)}, bf16[8,16,512]{2,1,0:T(8,128)(2,1)S(1)}, u32[]{:S(2)}, u32[]{:S(2)}) collective-permute-start(bf16[8,16,512]{2,1,0:T(8,128)(2,1)} %feat_any.1), channel_id=1, source_target_pairs={{0,2},{1,3},{2,0},{3,1},{4,6},{5,7},{6,4},{7,5},{8,10},{9,11},{10,... | collective-permute-start | bytes 393224 | tf_op jit(solution)/shard_map/feat_y/ppermute | solution.py:376
  4.8 5.4 %collective-permute-start.1 = (bf16[128,128]{1,0:T(8,128)(2,1)S(1)}, bf16[128,128]{1,0:T(8,128)(2,1)S(1)}, u32[]{:S(2)}, u32[]{:S(2)}) collective-permute-start(bf16[128,128]{1,0:T(8,128)(2,1)S(1)} %get-tuple-element.30), channel_id=1, source_target_pairs={{0,1},{1,0},{2,3},{3,2},{4,8},{5,9},{6,10},{7,11},{8,4},{9,5},{10,... | collective-permute-start | bytes 98312 | tf_op jit(solution)/shard_map/plane_second/ppermute | solution.py:399
  5.0 5.2 %collective-permute-start.2 = (bf16[128,128]{1,0:T(8,128)(2,1)S(1)}, bf16[128,128]{1,0:T(8,128)(2,1)S(1)}, u32[]{:S(2)}, u32[]{:S(2)}) collective-permute-start(bf16[128,128]{1,0:T(8,128)(2,1)S(1)} %get-tuple-element.31), channel_id=1, source_target_pairs={{0,4},{1,5},{2,6},{3,7},{4,0},{5,1},{6,2},{7,3},{8,12},{9,13},{10,... | collective-permute-start | bytes 98312 | tf_op jit(solution)/shard_map/plane_first/ppermute | solution.py:399
  7.9 5.2 %collective-permute-start = (bf16[8,16,512]{2,1,0:T(8,128)(2,1)}, bf16[8,16,512]{2,1,0:T(8,128)(2,1)S(1)}, u32[]{:S(2)}, u32[]{:S(2)}) collective-permute-start(bf16[8,16,512]{2,1,0:T(8,128)(2,1)} %cot_any.1), channel_id=1, source_target_pairs={{0,2},{1,3},{2,0},{3,1},{4,6},{5,7},{6,4},{7,5},{8,10},{9,11},{10,... | collective-permute-start | bytes 393224 | tf_op jit(solution)/shard_map/cot_y/ppermute | solution.py:376
  10.2 1.4 %collective-permute-start.5 = (bf16[8,16,512]{2,1,0:T(8,128)(2,1)S(1)}, bf16[8,16,512]{2,1,0:T(8,128)(2,1)S(1)}, u32[]{:S(2)}, u32[]{:S(2)}) collective-permute-start(bf16[8,16,512]{2,1,0:T(8,128)(2,1)S(1)} %collective-permute-done.4.feat2_ref.refs_2_), channel_id=1, source_target_pairs={{0,1},{1,0},{2,3},{3,2},{4,5},{5,4},{6,7},{7,6},{8,9},{9,8},{10,11... | collective-permute-start | bytes 393224 | tf_op jit(solution)/shard_map/feat_far/ppermute | solution.py:376
  13.1 2.8 %collective-permute-start.7 = (bf16[8,16,512]{2,1,0:T(8,128)(2,1)S(1)}, bf16[8,16,512]{2,1,0:T(8,128)(2,1)S(1)}, u32[]{:S(2)}, u32[]{:S(2)}) collective-permute-start(bf16[8,16,512]{2,1,0:T(8,128)(2,1)S(1)} %collective-permute-done.refs_4_), channel_id=1, source_target_pairs={{0,1},{1,0},{2,3},{3,2},{4,5},{5,4},{6,7},{7,6},{8,9},{9,8},{10,11... | collective-permute-start | bytes 393224 | tf_op jit(solution)/shard_map/cot_far/ppermute | solution.py:376
  13.4 5.2 %collective-permute-start.6 = (f32[216,128]{1,0:T(8,128)S(1)}, f32[216,128]{1,0:T(8,128)S(1)}, u32[]{:S(2)}, u32[]{:S(2)}) collective-permute-start(f32[216,128]{1,0:T(8,128)S(1)} %far_grad_kernel.1), channel_id=1, source_target_pairs={{0,4},{4,0},{8,12},{12,8},{16,20},{20,16},{24,28},{28,24},{1,5},{5... | collective-permute-start | bytes 331784 | tf_op jit(solution)/shard_map/sum_first/ppermute | solution.py:376
  14.9 5.4 %collective-permute-start.10 = (bf16[128,384]{1,0:T(8,128)(2,1)S(1)}, bf16[128,384]{1,0:T(8,128)(2,1)S(1)}, u32[]{:S(2)}, u32[]{:S(2)}) collective-permute-start(bf16[128,384]{1,0:T(8,128)(2,1)S(1)} %get-tuple-element.49), channel_id=1, source_target_pairs={{0,2},{1,3},{2,0},{3,1},{4,6},{5,7},{6,4},{7,5},{8,10},{9,11},{10,... | collective-permute-start | bytes 294920 | tf_op jit(solution)/shard_map/pack_y/ppermute | solution.py:376
  18.6 4.8 %collective-permute-start.8 = (f32[216,128]{1,0:T(8,128)S(1)}, f32[216,128]{1,0:T(8,128)S(1)}, u32[]{:S(2)}, u32[]{:S(2)}) collective-permute-start(f32[216,128]{1,0:T(8,128)S(1)} %add.6), channel_id=1, source_target_pairs={{0,8},{4,12},{8,0},{12,4},{16,24},{20,28},{24,16},{28,20},{1,9},{5... | collective-permute-start | bytes 331784 | tf_op jit(solution)/shard_map/sum_next/ppermute | solution.py:376
  20.2 1.3 %collective-permute-start.9 = (bf16[128,384]{1,0:T(8,128)(2,1)S(1)}, bf16[128,384]{1,0:T(8,128)(2,1)S(1)}, u32[]{:S(2)}, u32[]{:S(2)}) collective-permute-start(bf16[128,384]{1,0:T(8,128)(2,1)S(1)} %get-tuple-element.40.packed_ref.refs_0_), channel_id=1, source_target_pairs={{0,1},{1,0},{2,3},{3,2},{4,5},{5,4},{6,7},{7,6},{8,9},{9,8},{10,11... | collective-permute-start | bytes 294920 | tf_op jit(solution)/shard_map/pack_core/ppermute | solution.py:376
  20.2 1.5 %collective-permute-start.11 = (bf16[128,384]{1,0:T(8,128)(2,1)S(1)}, bf16[128,384]{1,0:T(8,128)(2,1)S(1)}, u32[]{:S(2)}, u32[]{:S(2)}) collective-permute-start(bf16[128,384]{1,0:T(8,128)(2,1)S(1)} %collective-permute-done.10.refs_2_), channel_id=1, source_target_pairs={{0,1},{1,0},{2,3},{3,2},{4,5},{5,4},{6,7},{7,6},{8,9},{9,8},{10,11... | collective-permute-start | bytes 294920 | tf_op jit(solution)/shard_map/pack_far/ppermute | solution.py:376
  23.4 8.0 %collective-permute-start.12 = (f32[216,128]{1,0:T(8,128)S(1)}, f32[216,128]{1,0:T(8,128)S(1)}, u32[]{:S(2)}, u32[]{:S(2)}) collective-permute-start(f32[216,128]{1,0:T(8,128)S(1)} %add.7.one_ref), channel_id=1, source_target_pairs={{0,16},{4,20},{8,24},{12,28},{16,0},{20,4},{24,8},{28,12},{1,17},{... | collective-permute-start | bytes 331784 | tf_op jit(solution)/shard_map/sum_last/ppermute | solution.py:376

commit v5 on v4

--- a/solution.py
+++ b/solution.py
@@ -337,10 +337,10 @@
     pad_bricks(near, padded, planes, 128, [(0, 0, [(0, 0)]), (2, 64, [(1, 0)])])
     edges[...] = padded[...].astype(bf16)
     layers = [edges.at[0:800]] + [grid_ref.at[800 * x : 800 * x + 800] for x in (0, 1, 6, 7)] + [edges.at[800:1600]]
-    low[...] = conv_layer(layers[0:3], mat_ref)
-    high[...] = conv_layer(layers[3:6], mat_ref)
+    low[0:512] = conv_layer(layers[0:3], mat_ref)
+    high[0:512] = conv_layer(layers[3:6], mat_ref)
     for r in range(bricks):
-        views = [view[pl.ds(r, view.shape[0] // 8, 8), :] for view in (low, early_ref, late_ref, high)]
+        views = [view[pl.ds(r, view.shape[0] // 8 - 1, 8), :] for view in (low, early_ref, late_ref, high)]
         turned = jnp.transpose(jnp.concatenate(views, axis=0))
         out[r] = turned[0:16].astype(bf16)
         grad[r] = turned[16:32].astype(bf16)
@@ -451,8 +451,8 @@
         inner_kernel,
         shape((6400, 128), bf16),
         [
-            pltpu.VMEM(((bricks + 1) * 512, 128), f32),
-            pltpu.VMEM((6400, 128), f32),
+            pltpu.VMEM(((bricks + 1) * 512 + 64, 128), f32),
+            pltpu.VMEM((7200, 128), f32),
             pltpu.SMEM(neighbours.shape, i32),
             pltpu.SemaphoreType.DMA,
         ],
@@ -467,7 +467,7 @@
         own, near_pack, near_pack1, far_pack2, far_pack3,
         specs=[VMEM] * 5,
     )
-    early = call(early_kernel, shape((512 * EARLY, 128), f32), [], grid, matrix, specs=[VMEM, VMEM])
+    early = call(early_kernel, shape((512 * EARLY + 8, 128), f32), [], grid, matrix, specs=[VMEM, VMEM])
     for step in steps[1:]:
         part = part + other
         if step < steps[-1]:
@@ -475,16 +475,16 @@
             other, early, grid = lax.optimization_barrier((other, early, grid))
         else:
             other = across("sum_last", part, step, "space")
-    late = call(late_kernel, shape((512 * (6 - EARLY), 128), f32), [], grid, matrix, specs=[VMEM, VMEM])
+    late = call(late_kernel, shape((512 * (6 - EARLY) + 8, 128), f32), [], grid, matrix, specs=[VMEM, VMEM])
     output, grad_input = call(
         outer_kernel,
         (shape(features.shape, bf16), shape(features.shape, bf16)),
         [
-            pltpu.VMEM(((bricks + 1) * 128, 128), f32),
+            pltpu.VMEM(((bricks + 1) * 128 + 64, 128), f32),
             pltpu.VMEM((1600, 128), f32),
             pltpu.VMEM((1600, 128), bf16),
-            pltpu.VMEM((512, 128), f32),
-            pltpu.VMEM((512, 128), f32),
+            pltpu.VMEM((520, 128), f32),
+            pltpu.VMEM((520, 128), f32),
             pltpu.SMEM(neighbours.shape, i32),
             pltpu.SemaphoreType.DMA,
         ],

time: 32.4 us -> 32.4 us (level)
  no operation moved by 1% of the time
where the time goes in v5:
time: 32.4 us; the launch traced here: 32.2 us
  starting transfers between devices  14.4 us (44%)
  Pallas kernels  13.7 us (42%)
  waiting for transfers between devices  3.37 us (10%)
  between operations  0.75 us (2%)
    pallas_call x11, Pallas kernels, call(): pl.pallas_call(kernel, name=name, out_shape=out_shape, in_specs=specs, ou...  13.7 us
    ppermute x11, starting transfers between devices, across(): lax.ppermute(value, axis, [(i, i ^ apart) for i in range(lax.axis_size(ax...  11.3 us
    ppermute x11, waiting for transfers between devices, across(): lax.ppermute(value, axis, [(i, i ^ apart) for i in range(lax.axis_size(ax...  3.36 us
    ppermute x2, starting transfers between devices, meet(): return lax.ppermute(value, ('space', 'chan'), pairs)  3.04 us
  transfers between devices with their start and end apart: 13, of which 7 were waited for; matrix products, arithmetic and copies ran while one was open for 0% of the time, Pallas kernels for 37%

profile of v5, /device:TPU:0, one launch (start us, length us, event | category | flops | bytes accessed | tf_op | source)
XLA Modules:
  0.0 32.2 jit_solution(2783649753039007499)
XLA Ops:
  0.6 1.1 %prepare_kernel.1 = (bf16[8,16,1024]{2,1,0:T(8,128)(2,1)S(1)}, bf16[27,16,64]{2,1,0:T(8,128)(2,1)S(1)}, s32[8,27]{1,0:T(8,128)S(1)}, bf16[128,128]{1,0:T(8,128)(2,1)S(1)}, bf16[128,128]{1,0:T(8,128)(2,1)S(1)}) custom-call(bf16[8,16,512]{2,1,0:T(8,128)(2,1)} %feat_any.1, bf16[8,16,512]{2,1,0:T(8,128)(2,1)} %cot_any.1, bf16[27,16,64]{2,1,0:T(8,128)(2,1)} %weight_any.1, ...), custom_call_target="tpu_custom_call" | custom-call | tf_op jit(solution)/shard_map/prepare_kernel/pallas_call | solution.py:25
  1.7 0.5 %collective-permute-start.3 = (bf16[8,16,1024]{2,1,0:T(8,128)(2,1)S(1)}, bf16[8,16,1024]{2,1,0:T(8,128)(2,1)S(1)}, u32[]{:S(2)}, u32[]{:S(2)}) collective-permute-start(bf16[8,16,1024]{2,1,0:T(8,128)(2,1)S(1)} %get-tuple-element.32.both_ref.refs_0_), channel_id=1, source_target_pairs={{0,1},{1,0},{2,3},{3,2},{4,5},{5,4},{6,7},{7,6},{8,9},{9,8},{10,11... | collective-permute-start | bytes 786440 | tf_op jit(solution)/shard_map/both_core/ppermute | solution.py:376
  2.3 2.6 %collective-permute-start.4 = (bf16[8,16,512]{2,1,0:T(8,128)(2,1)}, bf16[8,16,512]{2,1,0:T(8,128)(2,1)S(1)}, u32[]{:S(2)}, u32[]{:S(2)}) collective-permute-start(bf16[8,16,512]{2,1,0:T(8,128)(2,1)} %feat_any.1), channel_id=1, source_target_pairs={{0,2},{1,3},{2,0},{3,1},{4,6},{5,7},{6,4},{7,5},{8,10},{9,11},{10,... | collective-permute-start | bytes 393224 | tf_op jit(solution)/shard_map/feat_y/ppermute | solution.py:376
  4.8 0.2 collective-permute-start.1
  5.0 2.9 %collective-permute-start.2 = (bf16[128,128]{1,0:T(8,128)(2,1)S(1)}, bf16[128,128]{1,0:T(8,128)(2,1)S(1)}, u32[]{:S(2)}, u32[]{:S(2)}) collective-permute-start(bf16[128,128]{1,0:T(8,128)(2,1)S(1)} %get-tuple-element.31), channel_id=1, source_target_pairs={{0,4},{1,5},{2,6},{3,7},{4,0},{5,1},{6,2},{7,3},{8,12},{9,13},{10,... | collective-permute-start | bytes 98312 | tf_op jit(solution)/shard_map/plane_first/ppermute | solution.py:399
  7.9 0.5 %collective-permute-start = (bf16[8,16,512]{2,1,0:T(8,128)(2,1)}, bf16[8,16,512]{2,1,0:T(8,128)(2,1)S(1)}, u32[]{:S(2)}, u32[]{:S(2)}) collective-permute-start(bf16[8,16,512]{2,1,0:T(8,128)(2,1)} %cot_any.1), channel_id=1, source_target_pairs={{0,2},{1,3},{2,0},{3,1},{4,6},{5,7},{6,4},{7,5},{8,10},{9,11},{10,... | collective-permute-start | bytes 393224 | tf_op jit(solution)/shard_map/cot_y/ppermute | solution.py:376
  8.4 1.8 %near_grad_kernel.1 = (bf16[14,512,256]{2,1,0:T(8,128)(2,1)S(1)}, f32[4,32,128]{2,1,0:T(8,128)S(1)}) custom-call(s32[8,27]{1,0:T(8,128)S(1)} %get-tuple-element.29.near_ref, bf16[8,16,1024]{2,1,0:T(8,128)(2,1)S(1)} %get-tuple-element.32.both_ref.refs_0_, bf16[8,16,1024]{2,1,0:T(8,128)(2,1)S(1)} %collective-permute-done.3.both1_ref.refs_1_), custom_call_target="tpu_custom_call" | custom-call | tf_op jit(solution)/shard_map/near_grad_kernel/pallas_call | solution.py:25
  10.2 0.0 collective-permute-done.1.second_ref
  10.2 0.1 collective-permute-start.5
  10.3 0.2 pack_kernel.1
  10.6 0.9 %halo_grad_kernel.1 = (bf16[2,64,1152]{2,1,0:T(8,128)(2,1)S(1)}, f32[4,32,128]{2,1,0:T(8,128)S(1)}) custom-call(s32[8,27]{1,0:T(8,128)S(1)} %get-tuple-element.29.near_ref, bf16[128,384]{1,0:T(8,128)(2,1)S(1)} %get-tuple-element.40.packed_ref.refs_0_, bf16[8,16,1024]{2,1,0:T(8,128)(2,1)S(1)} %get-tuple-element.32.both_ref.refs_0_, ...), custom_call_target="tpu_custom_call" | custom-call | tf_op jit(solution)/shard_map/halo_grad_kernel/pallas_call | solution.py:25
  11.5 0.2 collective-permute-done.5.feat3_ref.refs_3_
  11.7 1.4 %far_grad_kernel.1 = f32[216,128]{1,0:T(8,128)S(1)} custom-call(bf16[14,512,256]{2,1,0:T(8,128)(2,1)S(1)} %get-tuple-element.39.windows_ref, bf16[2,64,1152]{2,1,0:T(8,128)(2,1)S(1)} %get-tuple-element.42.edge_windows_ref, bf16[8,16,512]{2,1,0:T(8,128)(2,1)S(1)} %collective-permute-done.4.feat2_ref.refs_2_, ...), custom_call_target="tpu_custom_call" | custom-call | tf_op jit(solution)/shard_map/far_grad_kernel/pallas_call | solution.py:25
  13.0 0.1 collective-permute-done.refs_4_
  13.1 0.3 collective-permute-start.7
  13.4 1.5 %collective-permute-start.6 = (f32[216,128]{1,0:T(8,128)S(1)}, f32[216,128]{1,0:T(8,128)S(1)}, u32[]{:S(2)}, u32[]{:S(2)}) collective-permute-start(f32[216,128]{1,0:T(8,128)S(1)} %far_grad_kernel.1), channel_id=1, source_target_pairs={{0,4},{4,0},{8,12},{12,8},{16,20},{20,16},{24,28},{28,24},{1,5},{5... | collective-permute-start | bytes 331784 | tf_op jit(solution)/shard_map/sum_first/ppermute | solution.py:376
  14.9 1.1 %collective-permute-start.10 = (bf16[128,384]{1,0:T(8,128)(2,1)S(1)}, bf16[128,384]{1,0:T(8,128)(2,1)S(1)}, u32[]{:S(2)}, u32[]{:S(2)}) collective-permute-start(bf16[128,384]{1,0:T(8,128)(2,1)S(1)} %get-tuple-element.49), channel_id=1, source_target_pairs={{0,2},{1,3},{2,0},{3,1},{4,6},{5,7},{6,4},{7,5},{8,10},{9,11},{10,... | collective-permute-start | bytes 294920 | tf_op jit(solution)/shard_map/pack_y/ppermute | solution.py:376
  15.9 1.9 %inner_kernel.1.grid_ref = bf16[6400,128]{1,0:T(8,128)(2,1)S(1)} custom-call(s32[8,27]{1,0:T(8,128)S(1)} %get-tuple-element.29.near_ref, bf16[8,16,1024]{2,1,0:T(8,128)(2,1)S(1)} %get-tuple-element.32.both_ref.refs_0_, bf16[8,16,1024]{2,1,0:T(8,128)(2,1)S(1)} %collective-permute-done.3.both1_ref.refs_1_, ...), custom_call_target="tpu_custom_call" | custom-call | tf_op jit(solution)/shard_map/inner_kernel/pallas_call | solution.py:25
  17.9 0.7 %collective-permute-done.6 = f32[216,128]{1,0:T(8,128)S(1)} collective-permute-done((f32[216,128]{1,0:T(8,128)S(1)}, f32[216,128]{1,0:T(8,128)S(1)}, u32[]{:S(2)}, u32[]{:S(2)}) %collective-permute-start.6) | collective-permute-done | bytes 110624 | tf_op jit(solution)/shard_map/sum_first/ppermute | solution.py:376
  18.6 1.6 %collective-permute-start.8 = (f32[216,128]{1,0:T(8,128)S(1)}, f32[216,128]{1,0:T(8,128)S(1)}, u32[]{:S(2)}, u32[]{:S(2)}) collective-permute-start(f32[216,128]{1,0:T(8,128)S(1)} %add.6), channel_id=1, source_target_pairs={{0,8},{4,12},{8,0},{12,4},{16,24},{20,28},{24,16},{28,20},{1,9},{5... | collective-permute-start | bytes 331784 | tf_op jit(solution)/shard_map/sum_next/ppermute | solution.py:376
  20.2 0.0 collective-permute-start.9
  20.2 0.5 %collective-permute-start.11 = (bf16[128,384]{1,0:T(8,128)(2,1)S(1)}, bf16[128,384]{1,0:T(8,128)(2,1)S(1)}, u32[]{:S(2)}, u32[]{:S(2)}) collective-permute-start(bf16[128,384]{1,0:T(8,128)(2,1)S(1)} %collective-permute-done.10.refs_2_), channel_id=1, source_target_pairs={{0,1},{1,0},{2,3},{3,2},{4,5},{5,4},{6,7},{7,6},{8,9},{9,8},{10,11... | collective-permute-start | bytes 294920 | tf_op jit(solution)/shard_map/pack_far/ppermute | solution.py:376
  20.8 0.8 %collective-permute-done.9.refs_1_ = bf16[128,384]{1,0:T(8,128)(2,1)S(1)} collective-permute-done((bf16[128,384]{1,0:T(8,128)(2,1)S(1)}, bf16[128,384]{1,0:T(8,128)(2,1)S(1)}, u32[]{:S(2)}, u32[]{:S(2)}) %collective-permute-start.9) | collective-permute-done | bytes 98336 | tf_op jit(solution)/shard_map/pack_core/ppermute | solution.py:376
  21.5 0.2 collective-permute-done.11.refs_3_
  21.7 0.4 %matrix_kernel.1.mat_ref = bf16[1152,128]{1,0:T(8,128)(2,1)S(1)} custom-call(bf16[27,16,64]{2,1,0:T(8,128)(2,1)S(1)} %get-tuple-element.36.weight_ref, bf16[128,384]{1,0:T(8,128)(2,1)S(1)} %get-tuple-element.40.packed_ref.refs_0_, bf16[128,384]{1,0:T(8,128)(2,1)S(1)} %collective-permute-done.9.refs_1_, bf16[128,384]{1,0:T(8,128)(2,1)S(1)} %collective-permute-done.10.refs_2_, ...), custom_call_target="tpu_custom_call" | custom-call | tf_op jit(solution)/shard_map/matrix_kernel/pallas_call | solution.py:25
  22.1 0.7 %early_kernel.1.early_ref = f32[520,128]{1,0:T(8,128)S(1)} custom-call(bf16[6400,128]{1,0:T(8,128)(2,1)S(1)} %inner_kernel.1.grid_ref, bf16[1152,128]{1,0:T(8,128)(2,1)S(1)} %matrix_kernel.1.mat_ref), custom_call_target="tpu_custom_call" | custom-call | tf_op jit(solution)/shard_map/early_kernel/pallas_call | solution.py:25
  22.8 0.6 %collective-permute-done.8 = f32[216,128]{1,0:T(8,128)S(1)} collective-permute-done((f32[216,128]{1,0:T(8,128)S(1)}, f32[216,128]{1,0:T(8,128)S(1)}, u32[]{:S(2)}, u32[]{:S(2)}) %collective-permute-start.8) | collective-permute-done | bytes 110624 | tf_op jit(solution)/shard_map/sum_next/ppermute | solution.py:376
  23.4 2.7 %collective-permute-start.12 = (f32[216,128]{1,0:T(8,128)S(1)}, f32[216,128]{1,0:T(8,128)S(1)}, u32[]{:S(2)}, u32[]{:S(2)}) collective-permute-start(f32[216,128]{1,0:T(8,128)S(1)} %add.7.one_ref), channel_id=1, source_target_pairs={{0,16},{4,20},{8,24},{12,28},{16,0},{20,4},{24,8},{28,12},{1,17},{... | collective-permute-start | bytes 331784 | tf_op jit(solution)/shard_map/sum_last/ppermute | solution.py:376
  26.1 2.2 %late_kernel.1.late_ref = f32[2568,128]{1,0:T(8,128)S(1)} custom-call(bf16[6400,128]{1,0:T(8,128)(2,1)S(1)} %inner_kernel.1.grid_ref, bf16[1152,128]{1,0:T(8,128)(2,1)S(1)} %matrix_kernel.1.mat_ref), custom_call_target="tpu_custom_call" | custom-call | tf_op jit(solution)/shard_map/late_kernel/pallas_call | solution.py:25
  28.3 2.3 %outer_kernel.1 = (bf16[8,16,512]{2,1,0:T(8,128)(2,1)S(1)}, bf16[8,16,512]{2,1,0:T(8,128)(2,1)S(1)}) custom-call(s32[8,27]{1,0:T(8,128)S(1)} %get-tuple-element.29.near_ref, bf16[6400,128]{1,0:T(8,128)(2,1)S(1)} %inner_kernel.1.grid_ref, bf16[1152,128]{1,0:T(8,128)(2,1)S(1)} %matrix_kernel.1.mat_ref, f32[520,128]{1,0:T(8,128)S(1)} %early_kernel.1.early_ref, ...), custom_call_target="tpu_custom_call" | custom-call | tf_op jit(solution)/shard_map/outer_kernel/pallas_call | solution.py:25
  30.5 0.9 %collective-permute-done.12.other_ref = f32[216,128]{1,0:T(8,128)S(1)} collective-permute-done((f32[216,128]{1,0:T(8,128)S(1)}, f32[216,128]{1,0:T(8,128)S(1)}, u32[]{:S(2)}, u32[]{:S(2)}) %collective-permute-start.12) | collective-permute-done | bytes 110624 | tf_op jit(solution)/shard_map/sum_last/ppermute | solution.py:376
  31.4 0.8 %finish_kernel.1 = (bf16[8,16,512]{2,1,0:T(8,128)(2,1)}, bf16[8,16,512]{2,1,0:T(8,128)(2,1)}, f32[27,16,64]{2,1,0:T(8,128)}) custom-call(bf16[8,16,512]{2,1,0:T(8,128)(2,1)S(1)} %get-tuple-element.52.out_ref, bf16[8,16,512]{2,1,0:T(8,128)(2,1)S(1)} %get-tuple-element.53.grad_ref, f32[216,128]{1,0:T(8,128)S(1)} %add.7.one_ref, ...), custom_call_target="tpu_custom_call" | custom-call | tf_op jit(solution)/shard_map/finish_kernel/pallas_call | solution.py:25
  (7 shorter events, 0.0 us)
Async XLA Ops:
  1.7 6.7 %collective-permute-start.3 = (bf16[8,16,1024]{2,1,0:T(8,128)(2,1)S(1)}, bf16[8,16,1024]{2,1,0:T(8,128)(2,1)S(1)}, u32[]{:S(2)}, u32[]{:S(2)}) collective-permute-start(bf16[8,16,1024]{2,1,0:T(8,128)(2,1)S(1)} %get-tuple-element.32.both_ref.refs_0_), channel_id=1, source_target_pairs={{0,1},{1,0},{2,3},{3,2},{4,5},{5,4},{6,7},{7,6},{8,9},{9,8},{10,11... | collective-permute-start | bytes 786440 | tf_op jit(solution)/shard_map/both_core/ppermute | solution.py:376
  2.3 8.0 %collective-permute-start.4 = (bf16[8,16,512]{2,1,0:T(8,128)(2,1)}, bf16[8,16,512]{2,1,0:T(8,128)(2,1)S(1)}, u32[]{:S(2)}, u32[]{:S(2)}) collective-permute-start(bf16[8,16,512]{2,1,0:T(8,128)(2,1)} %feat_any.1), channel_id=1, source_target_pairs={{0,2},{1,3},{2,0},{3,1},{4,6},{5,7},{6,4},{7,5},{8,10},{9,11},{10,... | collective-permute-start | bytes 393224 | tf_op jit(solution)/shard_map/feat_y/ppermute | solution.py:376
  4.8 5.4 %collective-permute-start.1 = (bf16[128,128]{1,0:T(8,128)(2,1)S(1)}, bf16[128,128]{1,0:T(8,128)(2,1)S(1)}, u32[]{:S(2)}, u32[]{:S(2)}) collective-permute-start(bf16[128,128]{1,0:T(8,128)(2,1)S(1)} %get-tuple-element.30), channel_id=1, source_target_pairs={{0,1},{1,0},{2,3},{3,2},{4,8},{5,9},{6,10},{7,11},{8,4},{9,5},{10,... | collective-permute-start | bytes 98312 | tf_op jit(solution)/shard_map/plane_second/ppermute | solution.py:399
  5.0 5.2 %collective-permute-start.2 = (bf16[128,128]{1,0:T(8,128)(2,1)S(1)}, bf16[128,128]{1,0:T(8,128)(2,1)S(1)}, u32[]{:S(2)}, u32[]{:S(2)}) collective-permute-start(bf16[128,128]{1,0:T(8,128)(2,1)S(1)} %get-tuple-element.31), channel_id=1, source_target_pairs={{0,4},{1,5},{2,6},{3,7},{4,0},{5,1},{6,2},{7,3},{8,12},{9,13},{10,... | collective-permute-start | bytes 98312 | tf_op jit(solution)/shard_map/plane_first/ppermute | solution.py:399
  7.9 5.2 %collective-permute-start = (bf16[8,16,512]{2,1,0:T(8,128)(2,1)}, bf16[8,16,512]{2,1,0:T(8,128)(2,1)S(1)}, u32[]{:S(2)}, u32[]{:S(2)}) collective-permute-start(bf16[8,16,512]{2,1,0:T(8,128)(2,1)} %cot_any.1), channel_id=1, source_target_pairs={{0,2},{1,3},{2,0},{3,1},{4,6},{5,7},{6,4},{7,5},{8,10},{9,11},{10,... | collective-permute-start | bytes 393224 | tf_op jit(solution)/shard_map/cot_y/ppermute | solution.py:376
  10.2 1.4 %collective-permute-start.5 = (bf16[8,16,512]{2,1,0:T(8,128)(2,1)S(1)}, bf16[8,16,512]{2,1,0:T(8,128)(2,1)S(1)}, u32[]{:S(2)}, u32[]{:S(2)}) collective-permute-start(bf16[8,16,512]{2,1,0:T(8,128)(2,1)S(1)} %collective-permute-done.4.feat2_ref.refs_2_), channel_id=1, source_target_pairs={{0,1},{1,0},{2,3},{3,2},{4,5},{5,4},{6,7},{7,6},{8,9},{9,8},{10,11... | collective-permute-start | bytes 393224 | tf_op jit(solution)/shard_map/feat_far/ppermute | solution.py:376
  13.1 2.8 %collective-permute-start.7 = (bf16[8,16,512]{2,1,0:T(8,128)(2,1)S(1)}, bf16[8,16,512]{2,1,0:T(8,128)(2,1)S(1)}, u32[]{:S(2)}, u32[]{:S(2)}) collective-permute-start(bf16[8,16,512]{2,1,0:T(8,128)(2,1)S(1)} %collective-permute-done.refs_4_), channel_id=1, source_target_pairs={{0,1},{1,0},{2,3},{3,2},{4,5},{5,4},{6,7},{7,6},{8,9},{9,8},{10,11... | collective-permute-start | bytes 393224 | tf_op jit(solution)/shard_map/cot_far/ppermute | solution.py:376
  13.4 5.2 %collective-permute-start.6 = (f32[216,128]{1,0:T(8,128)S(1)}, f32[216,128]{1,0:T(8,128)S(1)}, u32[]{:S(2)}, u32[]{:S(2)}) collective-permute-start(f32[216,128]{1,0:T(8,128)S(1)} %far_grad_kernel.1), channel_id=1, source_target_pairs={{0,4},{4,0},{8,12},{12,8},{16,20},{20,16},{24,28},{28,24},{1,5},{5... | collective-permute-start | bytes 331784 | tf_op jit(solution)/shard_map/sum_first/ppermute | solution.py:376
  14.9 5.4 %collective-permute-start.10 = (bf16[128,384]{1,0:T(8,128)(2,1)S(1)}, bf16[128,384]{1,0:T(8,128)(2,1)S(1)}, u32[]{:S(2)}, u32[]{:S(2)}) collective-permute-start(bf16[128,384]{1,0:T(8,128)(2,1)S(1)} %get-tuple-element.49), channel_id=1, source_target_pairs={{0,2},{1,3},{2,0},{3,1},{4,6},{5,7},{6,4},{7,5},{8,10},{9,11},{10,... | collective-permute-start | bytes 294920 | tf_op jit(solution)/shard_map/pack_y/ppermute | solution.py:376
  18.6 4.8 %collective-permute-start.8 = (f32[216,128]{1,0:T(8,128)S(1)}, f32[216,128]{1,0:T(8,128)S(1)}, u32[]{:S(2)}, u32[]{:S(2)}) collective-permute-start(f32[216,128]{1,0:T(8,128)S(1)} %add.6), channel_id=1, source_target_pairs={{0,8},{4,12},{8,0},{12,4},{16,24},{20,28},{24,16},{28,20},{1,9},{5... | collective-permute-start | bytes 331784 | tf_op jit(solution)/shard_map/sum_next/ppermute | solution.py:376
  20.2 1.3 %collective-permute-start.9 = (bf16[128,384]{1,0:T(8,128)(2,1)S(1)}, bf16[128,384]{1,0:T(8,128)(2,1)S(1)}, u32[]{:S(2)}, u32[]{:S(2)}) collective-permute-start(bf16[128,384]{1,0:T(8,128)(2,1)S(1)} %get-tuple-element.40.packed_ref.refs_0_), channel_id=1, source_target_pairs={{0,1},{1,0},{2,3},{3,2},{4,5},{5,4},{6,7},{7,6},{8,9},{9,8},{10,11... | collective-permute-start | bytes 294920 | tf_op jit(solution)/shard_map/pack_core/ppermute | solution.py:376
  20.2 1.5 %collective-permute-start.11 = (bf16[128,384]{1,0:T(8,128)(2,1)S(1)}, bf16[128,384]{1,0:T(8,128)(2,1)S(1)}, u32[]{:S(2)}, u32[]{:S(2)}) collective-permute-start(bf16[128,384]{1,0:T(8,128)(2,1)S(1)} %collective-permute-done.10.refs_2_), channel_id=1, source_target_pairs={{0,1},{1,0},{2,3},{3,2},{4,5},{5,4},{6,7},{7,6},{8,9},{9,8},{10,11... | collective-permute-start | bytes 294920 | tf_op jit(solution)/shard_map/pack_far/ppermute | solution.py:376
  23.4 8.0 %collective-permute-start.12 = (f32[216,128]{1,0:T(8,128)S(1)}, f32[216,128]{1,0:T(8,128)S(1)}, u32[]{:S(2)}, u32[]{:S(2)}) collective-permute-start(f32[216,128]{1,0:T(8,128)S(1)} %add.7.one_ref), channel_id=1, source_target_pairs={{0,16},{4,20},{8,24},{12,28},{16,0},{20,4},{24,8},{28,12},{1,17},{... | collective-permute-start | bytes 331784 | tf_op jit(solution)/shard_map/sum_last/ppermute | solution.py:376
